TPU v7x, 1024 devices: a whole 4x8x16 slice. The times are simulated.
1024 devices in a mesh: expert: 16 (over z), dp: 64 (over x, y, core).
Axes of the slice: x: 4, y: 8, z: 16, core: 2. Of those that a mesh axis runs over, the one named last changes fastest.
Arguments:
- tokens: bfloat16 [8192, 3584], P('dp', 'expert'), may hold values from -6 to 6
- cotangent: bfloat16 [8192, 3584], P('dp', 'expert'), may hold values from -6 to 6
- routes: int32 [8192, 8], P('dp'), may hold values from 0 to 255, all different within a row; in each aligned block of 128 rows (0 to 127, 128 to 255, ...) at most 6 rows name the same one
- route_weights: float32 [8192, 8], P('dp'), may hold values from 0.1 to 1
- owner_slots: int32 [64], replicated, may hold values from 1 to 4
- gate_weight: bfloat16 [64, 3584, 1024], P('dp', 'expert'), may hold values from -0.09375 to 0.09375
- up_weight: bfloat16 [64, 3584, 1024], P('dp', 'expert'), may hold values from -0.09375 to 0.09375
- down_weight: bfloat16 [64, 1024, 3584], P('dp', None, 'expert'), may hold values from -0.1875 to 0.1875
Outputs:
- mixed: bfloat16 [8192, 3584], P('dp', 'expert')
- input_gradient: bfloat16 [8192, 3584], P('dp', 'expert')
- route_gradient: float32 [8192, 8], P('dp')
- gate_gradient: bfloat16 [64, 3584, 1024], P('dp', 'expert')
- up_gradient: bfloat16 [64, 3584, 1024], P('dp', 'expert')
- down_gradient: bfloat16 [64, 1024, 3584], P('dp', None, 'expert')
Inputs may be any that keep to these rules, and one draw needn't show every extreme that they name: `routes`: each row names 8 different experts. In the 128 rows of one index of dp no expert is named more than 6 times, and some expert held is named exactly 6 times in some such block.
All inputs are finite; a program needn't handle non-finite values.
Results may differ from a plain program's by a relative error of at most 0.035.
Values may be sent and summed in bfloat16 or wider, within the bound.
No kernel may reach another device: no remote copies, remote signals or barrier semaphores. Data moves between devices by JAX's collectives and lax.ppermute only.
A program may use at most 32 MiB of HBM per device.

v0:
```python
import jax
import jax.numpy as jnp
from jax import lax
from jax.sharding import PartitionSpec as P

CAP = 6
SPARE = 2
OWN_MAX = 4


def passed_along(block, axis, distance):
    devices = range(lax.axis_size(axis))
    route = [((i - distance) % len(devices), i) for i in devices]
    return lax.ppermute(block, axis, route)


def route_slots(block_routes, owner_slots, experts_here, slot_count, spare_count):
    flat_routes = block_routes.reshape(-1)
    route_count = flat_routes.shape[0]
    inside = flat_routes < experts_here
    expert_ids = jnp.arange(experts_here, dtype=jnp.int32)
    onehot = (flat_routes[:, None] == expert_ids[None, :]).astype(jnp.int32)
    before = jnp.cumsum(onehot, axis=0) - onehot
    route_rank = jnp.sum(before * onehot, axis=1)
    owner_share = jnp.sum(onehot * owner_slots[None, :], axis=1)
    to_owner = inside & (route_rank < owner_share)
    to_copy = inside & (route_rank >= owner_share) & (route_rank < owner_share + spare_count)
    served = to_owner | to_copy
    half_way = experts_here // 2
    target_dev = jnp.where(to_owner, flat_routes, (flat_routes + half_way) % experts_here)
    target = jnp.where(served, target_dev, experts_here)
    slot_place = jnp.where(
        to_owner, route_rank, slot_count - spare_count + route_rank - owner_share
    )
    slot_place = jnp.where(served, slot_place, 0)
    route_order = jnp.arange(route_count, dtype=jnp.int32)
    slot_table = (
        jnp.zeros((experts_here + 1, slot_count), jnp.int32).at[target, slot_place].set(route_order)
    )
    filled = jnp.zeros((experts_here + 1, slot_count), jnp.int32).at[target, slot_place].set(1)
    return (slot_table[:experts_here], filled[:experts_here] > 0, target, slot_place, served)


def owner_part(blocks):
    return blocks[:, :OWN_MAX].reshape(-1, blocks.shape[-1])


def spare_part(blocks):
    return blocks[:, OWN_MAX:].reshape(-1, blocks.shape[-1])


def joined(owner_values, spare_values, block_count):
    width = owner_values.shape[-1]
    stacked = jnp.concatenate(
        [
            owner_values.reshape(block_count, OWN_MAX, width),
            spare_values.reshape(block_count, SPARE, width),
        ],
        axis=1,
    )
    return stacked.reshape(block_count * CAP, width)


def per_device(
    tokens, cotangent, routes, route_weights, owner_slots, gate_weight, up_weight, down_weight
):
    experts_here = lax.axis_size("dp")
    half_way = experts_here // 2
    token_count = tokens.shape[0]
    feature_count = tokens.shape[1]
    top_count = routes.shape[1]
    slot_table, filled, target, slot_place, served = route_slots(
        routes, owner_slots, experts_here, CAP, SPARE
    )
    token_of = slot_table // top_count
    live_mask = filled[:, :, None]
    token_send = jnp.where(live_mask, tokens[token_of], jnp.zeros((), jnp.bfloat16))
    route_scale = route_weights.reshape(-1)[slot_table]
    scaled_send = jnp.where(
        live_mask, cotangent[token_of].astype(jnp.float32) * route_scale[:, :, None], 0.0
    ).astype(jnp.bfloat16)
    arrived = lax.all_to_all(
        jnp.stack([token_send, scaled_send]), "dp", split_axis=1, concat_axis=1, tiled=True
    )
    row_count = experts_here * CAP
    token_blocks = arrived[0]
    scaled_blocks = arrived[1]
    gate_matrix = gate_weight[0]
    up_matrix = up_weight[0]
    down_matrix = down_weight[0]
    piece_width = gate_matrix.shape[0]
    hidden_count = gate_matrix.shape[1]
    packed = jnp.stack([gate_matrix, up_matrix, down_matrix.reshape(piece_width, hidden_count)])
    copies = passed_along(packed, "dp", half_way)
    gate_copy = copies[0]
    up_copy = copies[1]
    down_copy = copies[2].reshape(hidden_count, piece_width)
    share_width = hidden_count // lax.axis_size("expert")
    share_start = lax.axis_index("expert") * share_width
    contract_last = (((1,), (1,)), ((), ()))
    contract_first = (((0,), (0,)), ((), ()))
    token_own = owner_part(token_blocks)
    token_spare = spare_part(token_blocks)
    scaled_own = owner_part(scaled_blocks)
    scaled_spare = spare_part(scaled_blocks)
    gate_part = joined(
        jnp.dot(token_own, gate_matrix, preferred_element_type=jnp.float32),
        jnp.dot(token_spare, gate_copy, preferred_element_type=jnp.float32),
        experts_here,
    )
    up_part = joined(
        jnp.dot(token_own, up_matrix, preferred_element_type=jnp.float32),
        jnp.dot(token_spare, up_copy, preferred_element_type=jnp.float32),
        experts_here,
    )
    gate_full, up_full = (
        lax.psum(gate_part.astype(jnp.bfloat16), "expert").astype(jnp.float32),
        lax.psum(up_part.astype(jnp.bfloat16), "expert").astype(jnp.float32),
    )
    hidden = (gate_full * jax.nn.sigmoid(gate_full) * up_full).astype(jnp.bfloat16)
    gate_share = lax.dynamic_slice_in_dim(gate_full, share_start, share_width, 1)
    up_share = lax.dynamic_slice_in_dim(up_full, share_start, share_width, 1)
    hidden_blocks = hidden.reshape(experts_here, CAP, hidden_count)
    hidden_own = owner_part(hidden_blocks)
    hidden_spare = spare_part(hidden_blocks)
    out_rows = joined(
        jnp.dot(hidden_own, down_matrix, preferred_element_type=jnp.float32),
        jnp.dot(hidden_spare, down_copy, preferred_element_type=jnp.float32),
        experts_here,
    ).astype(jnp.bfloat16)
    out_blocks = out_rows.reshape(experts_here, CAP, feature_count)
    out_back = lax.all_to_all(out_blocks, "dp", split_axis=0, concat_axis=0, tiled=True)
    down_own = lax.dot_general(
        hidden_own, scaled_own, contract_first, preferred_element_type=jnp.float32
    )
    down_spare = lax.dot_general(
        hidden_spare, scaled_spare, contract_first, preferred_element_type=jnp.float32
    )
    hidden_part = joined(
        lax.dot_general(scaled_own, down_matrix, contract_last, preferred_element_type=jnp.float32),
        lax.dot_general(scaled_spare, down_copy, contract_last, preferred_element_type=jnp.float32),
        experts_here,
    )
    hidden_grad = lax.psum_scatter(
        hidden_part.astype(jnp.bfloat16), "expert", scatter_dimension=1, tiled=True
    ).astype(jnp.float32)
    sigmoid_gate = jax.nn.sigmoid(gate_share)
    gate_delta_share = (
        hidden_grad * up_share * sigmoid_gate * (1.0 + gate_share * (1.0 - sigmoid_gate))
    ).astype(jnp.bfloat16)
    up_delta_share = (hidden_grad * gate_share * sigmoid_gate).astype(jnp.bfloat16)
    gate_delta, up_delta = (
        lax.all_gather(gate_delta_share, "expert", axis=1, tiled=True),
        lax.all_gather(up_delta_share, "expert", axis=1, tiled=True),
    )
    gate_blocks = gate_delta.reshape(experts_here, CAP, hidden_count)
    up_blocks = up_delta.reshape(experts_here, CAP, hidden_count)
    gate_own = owner_part(gate_blocks)
    gate_spare = spare_part(gate_blocks)
    up_own = owner_part(up_blocks)
    up_spare = spare_part(up_blocks)
    input_own = lax.dot_general(
        gate_own, gate_matrix, contract_last, preferred_element_type=jnp.float32
    ) + lax.dot_general(up_own, up_matrix, contract_last, preferred_element_type=jnp.float32)
    input_spare = lax.dot_general(
        gate_spare, gate_copy, contract_last, preferred_element_type=jnp.float32
    ) + lax.dot_general(up_spare, up_copy, contract_last, preferred_element_type=jnp.float32)
    input_rows = joined(input_own, input_spare, experts_here).astype(jnp.bfloat16)
    gate_grad_own = lax.dot_general(
        token_own, gate_own, contract_first, preferred_element_type=jnp.float32
    )
    up_grad_own = lax.dot_general(
        token_own, up_own, contract_first, preferred_element_type=jnp.float32
    )
    gate_grad_spare = lax.dot_general(
        token_spare, gate_spare, contract_first, preferred_element_type=jnp.float32
    )
    up_grad_spare = lax.dot_general(
        token_spare, up_spare, contract_first, preferred_element_type=jnp.float32
    )
    copy_pack = jnp.stack(
        [gate_grad_spare, up_grad_spare, down_spare.reshape(piece_width, hidden_count)]
    ).astype(jnp.bfloat16)
    copy_back = passed_along(copy_pack, "dp", half_way)
    gate_grad = (gate_grad_own + copy_back[0].astype(jnp.float32)).astype(jnp.bfloat16)
    up_grad = (up_grad_own + copy_back[1].astype(jnp.float32)).astype(jnp.bfloat16)
    down_grad = (
        down_own + copy_back[2].reshape(hidden_count, piece_width).astype(jnp.float32)
    ).astype(jnp.bfloat16)
    input_blocks = input_rows.reshape(experts_here, CAP, feature_count)
    input_back = lax.all_to_all(input_blocks, "dp", split_axis=0, concat_axis=0, tiled=True)
    pick_index = jnp.where(served, target * CAP + slot_place, 0)
    out_route = jnp.where(
        served[:, None],
        out_back.reshape(row_count, feature_count)[pick_index],
        jnp.zeros((), jnp.bfloat16),
    )
    input_route = jnp.where(
        served[:, None],
        input_back.reshape(row_count, feature_count)[pick_index],
        jnp.zeros((), jnp.bfloat16),
    )
    out_route = out_route.reshape(token_count, top_count, feature_count).astype(jnp.float32)
    input_route = input_route.reshape(token_count, top_count, feature_count).astype(jnp.float32)
    mixed = jnp.einsum("tk,tkd->td", route_weights, out_route).astype(jnp.bfloat16)
    input_gradient = jnp.sum(input_route, axis=1).astype(jnp.bfloat16)
    score_part = jnp.einsum("td,tkd->tk", cotangent.astype(jnp.float32), out_route)
    route_gradient = lax.psum(score_part, "expert")
    return (mixed, input_gradient, route_gradient, gate_grad[None], up_grad[None], down_grad[None])


def solution(mesh):
    return jax.shard_map(
        per_device,
        mesh=mesh,
        in_specs=(
            P("dp", "expert"),
            P("dp", "expert"),
            P("dp", None),
            P("dp", None),
            P(),
            P("dp", "expert", None),
            P("dp", "expert", None),
            P("dp", None, "expert"),
        ),
        out_specs=(
            P("dp", "expert"),
            P("dp", "expert"),
            P("dp", None),
            P("dp", "expert", None),
            P("dp", "expert", None),
            P("dp", None, "expert"),
        ),
        check_vma=False,
    )
```

profile of v0, /device:TPU:1, one launch (start us, length us, event | category | flops | bytes accessed | tf_op | source)
XLA Modules:
  0.0 516.9 jit_solution(12303789130537214921)
XLA Ops:
  11.7 18.0 %reduce-window.6 = s32[64,8,128]{2,1,0:T(8,128)S(1)} reduce-window(s32[64,8,128]{2,1,0:T(8,128)S(1)} %fusion.40, s32[]{:T(128)} %constant.25.clone.1), window={size=1x1x128 pad=0_0x0_0x127_0}, to_apply=%region_0.0 | reduce-window | flops 8323072 | bytes 524292 | tf_op jit(solution)/shard_map/reduce-window
  31.2 4.3 scatter_custom_fusion.1
  35.5 4.3 scatter_custom_fusion
  40.4 1.9 gather_fusion.2
  42.7 2.1 gather_fusion.1
  44.8 2.1 gather_fusion
  48.6 18.3 %all-to-all-start = ((bf16[2,64,6,224]{3,0,2,1:T(2,128)(2,1)}), bf16[2,64,6,224]{3,0,2,1:T(2,128)(2,1)S(1)}, u32[]{:S(2)}, u32[]{:S(2)}) async-start(bf16[2,64,6,224]{3,0,2,1:T(2,128)(2,1)} %copy.192), calls=%async_computation | async-start | bytes 786432 | tf_op jit(solution)/shard_map/all_to_all | solution.py:82
  69.6 5.2 %collective-permute-start = (bf16[3,224,1024]{2,1,0:T(8,128)(2,1)}, bf16[3,224,1024]{2,1,0:T(8,128)(2,1)S(1)}, u32[]{:S(2)}, u32[]{:S(2)}) collective-permute-start(bf16[3,224,1024]{2,1,0:T(8,128)(2,1)} %pad_maximum_fusion), channel_id=1, source_target_pairs={{32,0},{33,1},{34,2},{35,3},{36,4},{37,5},{38,6},{39,7},{40,8},{41... | collective-permute-start | bytes 4128776 | tf_op jit(solution)/shard_map/ppermute | solution.py:14
  74.8 6.9 %all-to-all-done = bf16[2,64,6,224]{3,0,2,1:T(2,128)(2,1)S(1)} async-done(((bf16[2,64,6,224]{3,0,2,1:T(2,128)(2,1)}), bf16[2,64,6,224]{3,0,2,1:T(2,128)(2,1)S(1)}, u32[]{:S(2)}, u32[]{:S(2)}) %all-to-all-start) | async-done | bytes 344096 | tf_op jit(solution)/shard_map/all_to_all | solution.py:82
  84.4 23.3 %collective-permute-done = bf16[3,224,1024]{2,1,0:T(8,128)(2,1)S(1)} collective-permute-done((bf16[3,224,1024]{2,1,0:T(8,128)(2,1)}, bf16[3,224,1024]{2,1,0:T(8,128)(2,1)S(1)}, u32[]{:S(2)}, u32[]{:S(2)}) %collective-permute-start) | collective-permute-done | bytes 1376288 | tf_op jit(solution)/shard_map/ppermute | solution.py:14
  109.6 2.3 copy.196
  113.9 2.3 copy.198
  118.6 1.9 reshape_squeeze.4
  124.6 130.1 %all-reduce.3.cloned.1.call-done = (bf16[384,1024]{0,1:T(8,128)(2,1)}, bf16[384,1024]{0,1:T(8,128)(2,1)}) async-done(((bf16[384,1024]{0,1:T(8,128)(2,1)}, bf16[384,1024]{0,1:T(8,128)(2,1)}), (bf16[384,1024]{0,1:T(8,128)(2,1)}, bf16[384,1024]{0,1:T(8,128)(2,1)})) %all-reduce.3.cloned.1.call-update) | async-done | bytes 1572880 | tf_op jit(solution)/shard_map/psum | solution.py:118
  254.7 1.9 multiply_convert_fusion
  260.8 1.9 fusion
  263.0 63.4 %reduce-scatter.4.cloned.1.call-done = bf16[64,384]{1,0:T(8,128)(2,1)} async-done(((bf16[1024,384]{1,0:T(8,128)(2,1)}), bf16[64,384]{1,0:T(8,128)(2,1)}) %reduce-scatter.4.cloned.1.call-update) | async-done | bytes 49168
  327.9 26.3 %all_gather.6 = bf16[384,1024]{0,1:T(8,128)(2,1)S(1)} all-gather(bf16[384,64]{0,1:T(8,128)(2,1)S(1)} %get-tuple-element.31), channel_id=1, replica_groups=mesh['expert'=16,'dp'=64] {'expert'}, dimensions={1}, use_global_device_ids=true | all-gather | bytes 835584 | tf_op jit(solution)/shard_map/all_gather | solution.py:153
  357.2 24.7 %all_gather.7 = bf16[384,1024]{0,1:T(8,128)(2,1)S(1)} all-gather(bf16[384,64]{0,1:T(8,128)(2,1)S(1)} %copy-done.19), channel_id=1, replica_groups=mesh['expert'=16,'dp'=64] {'expert'}, dimensions={1}, use_global_device_ids=true | all-gather | bytes 835584 | tf_op jit(solution)/shard_map/all_gather | solution.py:154
  389.2 34.7 %all-to-all-start.1 = ((bf16[64,6,224]{2,1,0:T(8,128)(2,1)}), bf16[64,6,224]{2,1,0:T(8,128)(2,1)}, u32[]{:S(2)}, u32[]{:S(2)}) async-start(bf16[64,6,224]{2,1,0:T(8,128)(2,1)} %copy.203), calls=%async_computation.1 | async-start | bytes 524288 | tf_op jit(solution)/shard_map/all_to_all | solution.py:132
  424.0 2.1 copy.220
  426.1 2.9 stack_reshape.4
  431.1 1.9 fusion.6
  434.2 2.5 pad_maximum_fusion.1
  436.6 4.9 collective-permute-start.1
  445.9 8.4 %all-to-all-start.2 = ((bf16[64,6,224]{2,1,0:T(8,128)(2,1)}), bf16[64,6,224]{2,1,0:T(8,128)(2,1)S(1)}, u32[]{:S(2)}, u32[]{:S(2)}) async-start(bf16[64,6,224]{2,1,0:T(8,128)(2,1)} %pad_maximum_fusion.6), calls=%async_computation.2 | async-start | bytes 524288 | tf_op jit(solution)/shard_map/all_to_all | solution.py:191
  455.4 3.9 gather_fusion.3
  461.4 14.2 %all-to-all-done.2 = bf16[64,6,224]{2,1,0:T(8,128)(2,1)S(1)} async-done(((bf16[64,6,224]{2,1,0:T(8,128)(2,1)}), bf16[64,6,224]{2,1,0:T(8,128)(2,1)S(1)}, u32[]{:S(2)}, u32[]{:S(2)}) %all-to-all-start.2) | async-done | bytes 172064 | tf_op jit(solution)/shard_map/all_to_all | solution.py:191
  475.7 3.9 gather_fusion.4
  480.8 21.2 %psum.23 = f32[128,8]{0,1:T(8,128)} all-reduce(f32[128,8]{0,1:T(8,128)S(1)} %copy.233), channel_id=1, replica_groups=mesh['expert'=16,'dp'=64] {'expert'}, use_global_device_ids=true, to_apply=%region_10.11 | all-reduce | flops 1024 | bytes 8192 | tf_op jit(solution)/shard_map/psum | solution.py:208
  505.1 2.4 fusion.16
  507.6 2.5 fusion.18
  (176 shorter events, 55.3 us)
Async XLA Ops:
  8.1 22.2 %copy-start.23 = (s32[64]{0:T(128)S(1)}, s32[64]{0:T(128)}, u32[]{:S(2)}) copy-start(s32[64]{0:T(128)} %param.12) | copy-start | bytes 772
  9.7 21.3 %copy-start.25 = (s32[2]{0:T(128)S(1)}, s32[2]{0:T(128)}, u32[]{:S(2)}) copy-start(s32[2]{0:T(128)} %constant.78) | copy-start | bytes 28
  9.8 21.3 %copy-start.24 = (s32[2]{0:T(128)S(1)}, s32[2]{0:T(128)}, u32[]{:S(2)}) copy-start(s32[2]{0:T(128)} %constant.75) | copy-start | bytes 28
  47.3 19.7 %copy-start.12 = (bf16[1,1024,224]{1,2,0:T(8,128)(2,1)S(1)}, bf16[1,1024,224]{1,2,0:T(8,128)(2,1)}, u32[]{:S(2)}) copy-start(bf16[1,1024,224]{1,2,0:T(8,128)(2,1)} %param.15) | copy-start | bytes 1376260
  48.6 19.8 %copy-start = (bf16[1,224,1024]{2,1,0:T(8,128)(2,1)S(1)}, bf16[1,224,1024]{2,1,0:T(8,128)(2,1)}, u32[]{:S(2)}) copy-start(bf16[1,224,1024]{2,1,0:T(8,128)(2,1)} %param.13) | copy-start | bytes 1376260
  48.6 19.8 %copy-start.1 = (bf16[1,224,1024]{2,1,0:T(8,128)(2,1)S(1)}, bf16[1,224,1024]{2,1,0:T(8,128)(2,1)}, u32[]{:S(2)}) copy-start(bf16[1,224,1024]{2,1,0:T(8,128)(2,1)} %param.14) | copy-start | bytes 1376260
  48.6 33.1 %all-to-all-start = ((bf16[2,64,6,224]{3,0,2,1:T(2,128)(2,1)}), bf16[2,64,6,224]{3,0,2,1:T(2,128)(2,1)S(1)}, u32[]{:S(2)}, u32[]{:S(2)}) async-start(bf16[2,64,6,224]{3,0,2,1:T(2,128)(2,1)} %copy.192), calls=%async_computation | async-start | bytes 786432 | tf_op jit(solution)/shard_map/all_to_all | solution.py:82
  67.0 187.7 %all-reduce.3.cloned.1.call-start = ((), (), s32[]{:S(2)}) async-start(), calls=%async_computation.5 | async-start | bytes 3145728 | tf_op jit(solution)/shard_map/psum | solution.py:118
  69.6 38.1 %collective-permute-start = (bf16[3,224,1024]{2,1,0:T(8,128)(2,1)}, bf16[3,224,1024]{2,1,0:T(8,128)(2,1)S(1)}, u32[]{:S(2)}, u32[]{:S(2)}) collective-permute-start(bf16[3,224,1024]{2,1,0:T(8,128)(2,1)} %pad_maximum_fusion), channel_id=1, source_target_pairs={{32,0},{33,1},{34,2},{35,3},{36,4},{37,5},{38,6},{39,7},{40,8},{41... | collective-permute-start | bytes 4128776 | tf_op jit(solution)/shard_map/ppermute | solution.py:14
  107.7 10.1 %copy-start.2 = (bf16[3,224,1024]{2,1,0:T(8,128)(2,1)}, bf16[3,224,1024]{2,1,0:T(8,128)(2,1)S(1)}, u32[]{:S(2)}) copy-start(bf16[3,224,1024]{2,1,0:T(8,128)(2,1)S(1)} %collective-permute-done) | copy-start | bytes 4128772
  109.6 2.6 copy-start.10
  113.9 2.4 copy-start.14
  116.3 210.1 %reduce-scatter.4.cloned.1.call-start = ((), (), s32[]{:S(2)}) async-start(), calls=%async_computation.4 | async-start | bytes 835584
  116.4 4.1 copy-start.7
  121.6 1.2 copy-start.18
  121.6 2.3 copy-start.21
  121.6 2.4 copy-start.22
  257.1 1.3 copy-start.6
  258.4 1.1 copy-start.5
  354.8 2.4 copy-start.19
  389.2 56.6 %all-to-all-start.1 = ((bf16[64,6,224]{2,1,0:T(8,128)(2,1)}), bf16[64,6,224]{2,1,0:T(8,128)(2,1)}, u32[]{:S(2)}, u32[]{:S(2)}) async-start(bf16[64,6,224]{2,1,0:T(8,128)(2,1)} %copy.203), calls=%async_computation.1 | async-start | bytes 524288 | tf_op jit(solution)/shard_map/all_to_all | solution.py:132
  424.0 5.9 %copy-start.3 = (bf16[3,224,1024]{2,1,0:T(8,128)(2,1)S(1)}, bf16[3,224,1024]{2,1,0:T(8,128)(2,1)}, u32[]{:S(2)}) copy-start(bf16[3,224,1024]{2,1,0:T(8,128)(2,1)} %copy-done.2) | copy-start | bytes 4128772
  433.0 1.2 copy-start.13
  434.1 7.4 %copy-start.11 = (bf16[256,1024]{1,0:T(8,128)(2,1)S(1)}, bf16[256,1024]{1,0:T(8,128)(2,1)}, u32[]{:S(2)}) copy-start(bf16[256,1024]{1,0:T(8,128)(2,1)} %reshape.346) | copy-start | bytes 1572868
  436.6 65.4 %collective-permute-start.1 = (bf16[3,224,1024]{2,1,0:T(8,128)(2,1)}, bf16[3,224,1024]{2,1,0:T(8,128)(2,1)}, u32[]{:S(2)}, u32[]{:S(2)}) collective-permute-start(bf16[3,224,1024]{2,1,0:T(8,128)(2,1)} %pad_maximum_fusion.1), channel_id=1, source_target_pairs={{32,0},{33,1},{34,2},{35,3},{36,4},{37,5},{38,6},{39,7},{40,8},{41... | collective-permute-start | bytes 4128776 | tf_op jit(solution)/shard_map/ppermute | solution.py:14
  441.9 1.4 copy-start.8
  441.9 1.4 copy-start.9
  444.5 10.8 %copy-start.20 = (s32[1024]{0:T(1024)S(1)}, s32[1024]{0:T(1024)}, u32[]{:S(2)}) copy-start(s32[1024]{0:T(1024)} %broadcast_clamp_fusion) | copy-start | bytes 12292
  445.9 29.7 %all-to-all-start.2 = ((bf16[64,6,224]{2,1,0:T(8,128)(2,1)}), bf16[64,6,224]{2,1,0:T(8,128)(2,1)S(1)}, u32[]{:S(2)}, u32[]{:S(2)}) async-start(bf16[64,6,224]{2,1,0:T(8,128)(2,1)} %pad_maximum_fusion.6), calls=%async_computation.2 | async-start | bytes 524288 | tf_op jit(solution)/shard_map/all_to_all | solution.py:191
  455.4 4.0 copy-start.17
  455.4 4.5 copy-start.16
  505.1 2.4 copy-start.4
  (1 other events, 0.6 us)
Sparse Core Ops, SparseCore 0:
  116.4 138.2 all-reduce.2
  258.4 67.8 reduce-scatter.3
where the time goes:
time: 524 us; the launch traced here: 517 us
  waiting for transfers between devices  238 us (45%)
  blocking collectives  72.3 us (14%)
  starting transfers between devices  71.6 us (14%)
  local copies, waits for them, and re-layouts  67 us (13%)
  other arithmetic  35 us (7%)
  matrix products  18.2 us (3%)
  between operations  14.9 us (3%)
    psum x1, waiting for transfers between devices, per_device(): lax.psum(up_part.astype(jnp.bfloat16), 'expert').astype(jnp.float32)  130 us
    unnamed x3, waiting for transfers between devices  63.4 us
    all_to_all x1, starting transfers between devices, per_device(): lax.all_to_all(out_blocks, 'dp', split_axis=0, concat_axis=0, tiled=True)  34.7 us
    all_gather x1, blocking collectives, per_device(): lax.all_gather(gate_delta_share, 'expert', axis=1, tiled=True)  26.3 us
    all_gather x1, blocking collectives, per_device(): lax.all_gather(up_delta_share, 'expert', axis=1, tiled=True)  24.7 us
    ppermute x2, waiting for transfers between devices, passed_along(): return lax.ppermute(block, axis, route)  23.3 us
    psum x1, blocking collectives, per_device(): route_gradient = lax.psum(score_part, 'expert')  21.2 us
    all_to_all x1, starting transfers between devices, per_device(): lax.all_to_all(jnp.stack([token_send, scaled_send]), 'dp', split_axis=1,...  18.3 us
  transfers between devices with their start and end apart: 7, of which 5 were waited for; matrix products, arithmetic and copies ran while one was open for 10% of the time, Pallas kernels for 0%

commit v1 on v0

v1 whole, which is shorter than its diff:
```python
import jax
import jax.numpy as jnp
from jax import lax
from jax.experimental import pallas as pl
from jax.experimental.pallas import tpu as pltpu
from jax.sharding import PartitionSpec as P

CAP = 6
SPARE = 2
LANES = 128
TILES = 4
GROUP = CAP * TILES
SOURCES = 16
SCORE_LANE = 96
VMEM_LIMIT = 48 * 1024 * 1024

F32 = jnp.float32
BF16 = jnp.bfloat16
CONTRACT_LAST = (((1,), (1,)), ((), ()))
CONTRACT_FIRST = (((0,), (0,)), ((), ()))


def dot(left, right, dims=(((1,), (0,)), ((), ()))):
    return lax.dot_general(left, right, dims, preferred_element_type=F32)


def one_zero(condition):
    return jnp.where(condition, 1.0, 0.0).astype(BF16)


def three_parts(value):
    high = value.astype(BF16)
    rest = value - high.astype(F32)
    middle = rest.astype(BF16)
    return high, middle, (rest - middle.astype(F32)).astype(BF16)


def iota(shape, axis):
    return lax.broadcasted_iota(jnp.int32, shape, axis)


def expert_of_row(row, expert):
    offset = row - GROUP * expert
    return (offset >= 0) & (offset < GROUP)


def tile_and_slot(row):
    place = row - GROUP * lax.shift_right_logical(row * 2731, 16)
    tile = (
        (place >= CAP).astype(jnp.int32)
        + (place >= 2 * CAP).astype(jnp.int32)
        + (place >= 3 * CAP).astype(jnp.int32)
    )
    return tile, place - CAP * tile


def reorder_matrix(sorted_row, sent_row):
    per_tile = SOURCES * CAP
    tile = (
        (sorted_row >= per_tile).astype(jnp.int32)
        + (sorted_row >= 2 * per_tile).astype(jnp.int32)
        + (sorted_row >= 3 * per_tile).astype(jnp.int32)
    )
    within = sorted_row - per_tile * tile
    source = lax.shift_right_logical(within * 43, 8)
    return one_zero(sent_row == within + (GROUP - CAP) * source + CAP * tile)


def dispatch_kernel(tok_ref, cot_ref, routes_ref, weight_ref, slots_ref, send_ref, rank_ref, scale_ref):
    token_count, top_count = routes_ref.shape
    experts = slots_ref.shape[1]
    rows = experts * GROUP
    expert = iota((token_count, experts), 1)
    named = jnp.zeros((token_count, experts), F32)
    scale = jnp.zeros((token_count, experts), F32)
    for k in range(top_count):
        hit = routes_ref[:, k : k + 1] == expert
        named = named + jnp.where(hit, 1.0, 0.0)
        scale = scale + jnp.where(hit, weight_ref[:, k : k + 1], 0.0)
    earlier = one_zero(iota((token_count, token_count), 0) > iota((token_count, token_count), 1))
    rank = dot(earlier, named.astype(BF16))
    limit = slots_ref[...].astype(F32) + float(SPARE)
    rank = jnp.where((named > 0.0) & (rank < limit), rank, -1.0)
    rank_ref[...] = rank
    scale_ref[...] = scale
    spread = one_zero(expert_of_row(iota((rows, experts), 0), iota((rows, experts), 1)))
    tile, slot = tile_and_slot(iota((rows, token_count), 0))
    taken = dot(spread, rank.astype(BF16), CONTRACT_LAST) == slot.astype(F32)
    row_scale = sum(dot(spread, part, CONTRACT_LAST) for part in three_parts(scale))
    row_scale = jnp.sum(jnp.where(taken, row_scale, 0.0), axis=1, keepdims=True)
    row_scale = jnp.where(tile[:, :1] >= 2, row_scale, 1.0)
    width = tok_ref.shape[1]
    picked = jnp.zeros((rows, LANES), F32)
    for index, ref in ((0, tok_ref), (2, cot_ref)):
        low = ref[:, :LANES]
        high = jnp.concatenate(
            [ref[:, LANES:].astype(F32), jnp.zeros((token_count, 2 * LANES - width), F32)], axis=1
        ).astype(BF16)
        picked = picked + dot(one_zero(taken & (tile == index)), low)
        picked = picked + dot(one_zero(taken & (tile == index + 1)), high)
    send_ref[...] = (picked * row_scale).astype(BF16).reshape(send_ref.shape)


def partial_kernel(recv_ref, gate_ref, up_ref, down_ref, part_ref, tok_ref, scaled_ref):
    experts = recv_ref.shape[0]
    hidden = gate_ref.shape[2]
    width = gate_ref.shape[1]
    block = SOURCES * GROUP
    per_tile = SOURCES * CAP
    reorder = reorder_matrix(iota((block, block), 0), iota((block, block), 1))
    for b in range(experts // SOURCES):
        sent = recv_ref[b * SOURCES : (b + 1) * SOURCES].reshape(block, LANES)
        rows = dot(reorder, sent).astype(BF16)
        place = slice(b * per_tile, (b + 1) * per_tile)
        for ref, index in ((tok_ref, 0), (scaled_ref, 2)):
            ref[place, :LANES] = rows[index * per_tile : (index + 1) * per_tile]
            ref[place, LANES:] = rows[(index + 1) * per_tile : (index + 2) * per_tile, : width - LANES]
    step = 256
    for start in range(0, hidden, step):
        columns = slice(start, start + step)
        part_ref[:, start : start + step] = dot(tok_ref[...], gate_ref[0, :, columns]).astype(BF16)
        part_ref[:, hidden + start : hidden + start + step] = dot(
            tok_ref[...], up_ref[0, :, columns]
        ).astype(BF16)
        part_ref[:, 2 * hidden + start : 2 * hidden + start + step] = dot(
            scaled_ref[...], down_ref[0, columns, :], CONTRACT_LAST
        ).astype(BF16)


def middle_kernel(sum_ref, out_ref):
    hidden = sum_ref.shape[1] // 3
    gate = sum_ref[:, :hidden].astype(F32)
    up = sum_ref[:, hidden : 2 * hidden].astype(F32)
    grad = sum_ref[:, 2 * hidden :].astype(F32)
    sigmoid = jax.nn.sigmoid(gate)
    gated = gate * sigmoid
    hidden_value = (gated * up).astype(BF16)
    out_ref[:, :hidden] = hidden_value
    out_ref[:, hidden : 2 * hidden] = (grad * up * sigmoid * (1.0 + gate * (1.0 - sigmoid))).astype(BF16)
    out_ref[:, 2 * hidden : 3 * hidden] = (grad * gated).astype(BF16)
    score = jnp.sum(hidden_value.astype(F32) * grad, axis=1, keepdims=True)
    lane = iota((gate.shape[0], LANES), 1)
    packed = jnp.zeros(lane.shape, F32)
    for index, part in enumerate(three_parts(score)):
        packed = jnp.where(lane == SCORE_LANE + index, part.astype(F32), packed)
    out_ref[:, 3 * hidden :] = packed.astype(BF16)


def rows_kernel(full_ref, gate_ref, up_ref, down_ref, back_ref, tiles_ref):
    experts = back_ref.shape[0]
    hidden = gate_ref.shape[2]
    width = gate_ref.shape[1]
    block = SOURCES * GROUP
    per_tile = SOURCES * CAP
    out_rows = dot(full_ref[:, :hidden], down_ref[0])
    in_rows = dot(full_ref[:, hidden : 2 * hidden], gate_ref[0], CONTRACT_LAST) + dot(
        full_ref[:, 2 * hidden : 3 * hidden], up_ref[0], CONTRACT_LAST
    )
    tiles_ref[0] = out_rows[:, :LANES]
    tiles_ref[1] = full_ref[:, 3 * hidden :].astype(F32)
    tiles_ref[1, :, : width - LANES] = out_rows[:, LANES:]
    tiles_ref[2] = in_rows[:, :LANES]
    tiles_ref[3] = jnp.zeros(tiles_ref.shape[1:], F32)
    tiles_ref[3, :, : width - LANES] = in_rows[:, LANES:]
    restore = reorder_matrix(iota((block, block), 1), iota((block, block), 0))
    for b in range(experts // SOURCES):
        place = slice(b * per_tile, (b + 1) * per_tile)
        stacked = tiles_ref[:, place].astype(BF16).reshape(block, LANES)
        back_ref[b * SOURCES : (b + 1) * SOURCES] = (
            dot(restore, stacked).astype(BF16).reshape(SOURCES, GROUP, LANES)
        )


def combine_kernel(
    back_ref, rank_ref, scale_ref, routes_ref, weight_ref, mixed_ref, input_ref, score_ref
):
    token_count, experts = rank_ref.shape
    top_count = routes_ref.shape[1]
    width = mixed_ref.shape[1]
    rows = experts * GROUP
    back = back_ref[...].reshape(rows, LANES)
    spread = one_zero(expert_of_row(iota((experts, rows), 1), iota((experts, rows), 0)))
    tile, slot = tile_and_slot(iota((token_count, rows), 1))
    taken = dot(rank_ref[...].astype(BF16), spread) == slot.astype(F32)
    mixed = [jnp.zeros((token_count, LANES), F32) for _ in range(2)]
    for part in three_parts(scale_ref[...]):
        scale = dot(part, spread)
        for index in range(2):
            chosen = jnp.where(taken & (tile == index), scale, 0.0).astype(BF16)
            mixed[index] = mixed[index] + dot(chosen, back)
    mixed_ref[:, :LANES] = mixed[0].astype(BF16)
    mixed_ref[:, LANES:] = mixed[1][:, : width - LANES].astype(BF16)
    input_ref[:, :LANES] = dot(one_zero(taken & (tile == 2)), back).astype(BF16)
    input_ref[:, LANES:] = dot(one_zero(taken & (tile == 3)), back)[:, : width - LANES].astype(BF16)
    lane = iota((8, LANES), 1)
    score_lanes = one_zero((lane >= SCORE_LANE) & (lane < SCORE_LANE + 3))
    row_score = dot(score_lanes, back, CONTRACT_LAST)[:1]
    routed = jnp.where(taken & (tile == 1), row_score, 0.0)
    by_expert = sum(dot(part, spread, CONTRACT_LAST) for part in three_parts(routed))
    expert = iota((token_count, experts), 1)
    for k in range(top_count):
        hit = routes_ref[:, k : k + 1] == expert
        value = jnp.sum(jnp.where(hit, by_expert, 0.0), axis=1, keepdims=True)
        score_ref[:, k : k + 1] = value / weight_ref[:, k : k + 1]


def kernel_call(body, out_shape, flops, moved, scratch=()):
    return pl.pallas_call(
        body,
        out_shape=out_shape,
        scratch_shapes=scratch,
        compiler_params=pltpu.CompilerParams(vmem_limit_bytes=VMEM_LIMIT),
        cost_estimate=pl.CostEstimate(flops=flops, bytes_accessed=moved, transcendentals=0),
    )


def per_device(
    tokens, cotangent, routes, route_weights, owner_slots, gate_weight, up_weight, down_weight
):
    experts = lax.axis_size("dp")
    parts = lax.axis_size("expert")
    token_count, width = tokens.shape
    hidden = gate_weight.shape[2]
    row_count = experts * CAP
    shape = jax.ShapeDtypeStruct
    exchanged = shape((experts, GROUP, LANES), BF16)
    per_expert = shape((token_count, experts), F32)
    send, rank, scale = kernel_call(
        dispatch_kernel, (exchanged, per_expert, per_expert), 300_000_000, 1_000_000
    )(tokens, cotangent, routes, route_weights, owner_slots.reshape(1, experts))
    arrived = lax.all_to_all(send, "dp", split_axis=0, concat_axis=0, tiled=True)
    rows = shape((row_count, width), BF16)
    part, token_rows, scaled_rows = kernel_call(
        partial_kernel, (shape((row_count, 3 * hidden), BF16), rows, rows), 700_000_000, 4_500_000
    )(arrived, gate_weight, up_weight, down_weight)
    summed = lax.psum_scatter(part, "expert", scatter_dimension=0, tiled=True)
    share = kernel_call(
        middle_kernel, shape((row_count // parts, 3 * hidden + LANES), BF16), 1_000_000, 300_000
    )(summed)
    full = lax.all_gather(share, "expert", axis=0, tiled=True)
    back = kernel_call(
        rows_kernel,
        exchanged,
        700_000_000,
        4_500_000,
        scratch=[pltpu.VMEM((TILES, row_count, LANES), F32)],
    )(full, gate_weight, up_weight, down_weight)
    returned = lax.all_to_all(back, "dp", split_axis=0, concat_axis=0, tiled=True)
    gate_grad = dot(token_rows, full[:, hidden : 2 * hidden], CONTRACT_FIRST).astype(BF16)
    up_grad = dot(token_rows, full[:, 2 * hidden : 3 * hidden], CONTRACT_FIRST).astype(BF16)
    down_grad = dot(full[:, :hidden], scaled_rows, CONTRACT_FIRST).astype(BF16)
    token_shape = shape(tokens.shape, BF16)
    mixed, input_gradient, route_gradient = kernel_call(
        combine_kernel,
        (token_shape, token_shape, shape(routes.shape, F32)),
        500_000_000,
        1_000_000,
    )(returned, rank, scale, routes, route_weights)
    return (mixed, input_gradient, route_gradient, gate_grad[None], up_grad[None], down_grad[None])


def solution(mesh):
    return jax.shard_map(
        per_device,
        mesh=mesh,
        in_specs=(
            P("dp", "expert"),
            P("dp", "expert"),
            P("dp", None),
            P("dp", None),
            P(),
            P("dp", "expert", None),
            P("dp", "expert", None),
            P("dp", None, "expert"),
        ),
        out_specs=(
            P("dp", "expert"),
            P("dp", "expert"),
            P("dp", None),
            P("dp", "expert", None),
            P("dp", "expert", None),
            P("dp", None, "expert"),
        ),
        check_vma=False,
    )
```

time: 524 us -> 249 us (0.48); the launches traced: 517 us -> 248 us
  blocking collectives: 72.3 us -> 0 us
  waiting for transfers between devices: 238 us -> 167 us
  local copies, waits for them, and re-layouts: 67 us -> 15.1 us
  other arithmetic: 35 us -> 0 us
  starting transfers between devices: 71.6 us -> 37.4 us
  matrix products: 18.2 us -> 3.61 us
  Pallas kernels: 0 us -> 10.8 us
    psum x1 -> x0, waiting for transfers between devices: 130 us -> none  [per_device(): lax.psum(up_part.astype(jnp.bfloat16), 'expert').astype(jnp.float32)]
    all_gather x0 -> x1, waiting for transfers between devices: none -> 77.9 us  [per_device(): full = lax.all_gather(share, 'expert', axis=0, tiled=True)]
    reduce_scatter x0 -> x1, waiting for transfers between devices: none -> 64.8 us  [per_device(): summed = lax.psum_scatter(part, 'expert', scatter_dimension=0, tiled=True)]
    unnamed x3 -> x2, waiting for transfers between devices: 63.4 us -> 0.03 us
    all_gather x2 -> x0, blocking collectives: 51.1 us -> none  [the longest x1 26.3 us: per_device(): lax.all_gather(gate_delta_share, 'expert', axis=1, tiled=True)]
    all_to_all x3 -> x2, starting transfers between devices: 61.5 us -> 37.3 us  [the longest x1 19.1 us: per_device(): lax.all_to_all(back, 'dp', split_axis=0, concat_axis=0, tiled=True)]
    ppermute x2 -> x0, waiting for transfers between devices: 23.3 us -> none  [passed_along(): return lax.ppermute(block, axis, route)]
    another operation x6 -> x0, other arithmetic: 22 us -> none
  transfers between devices with their start and end apart: 7 -> 4, of which waited for: 5 -> 4; matrix products, arithmetic and copies ran while one was open for 10% -> 2% of each run, Pallas kernels for 0% -> 0%
where the time goes in v1:
time: 249 us; the launch traced here: 248 us
  waiting for transfers between devices  167 us (67%)
  starting transfers between devices  37.4 us (15%)
  local copies, waits for them, and re-layouts  15.1 us (6%)
  between operations  14.1 us (6%)
  Pallas kernels  10.8 us (4%)
  matrix products  3.61 us (1%)
    all_gather x1, waiting for transfers between devices, per_device(): full = lax.all_gather(share, 'expert', axis=0, tiled=True)  77.9 us
    reduce_scatter x1, waiting for transfers between devices, per_device(): summed = lax.psum_scatter(part, 'expert', scatter_dimension=0, tiled=True)  64.8 us
    all_to_all x1, starting transfers between devices, per_device(): lax.all_to_all(back, 'dp', split_axis=0, concat_axis=0, tiled=True)  19.1 us
    all_to_all x1, starting transfers between devices, per_device(): lax.all_to_all(send, 'dp', split_axis=0, concat_axis=0, tiled=True)  18.2 us
    unnamed x32, local copies, waits for them, and re-layouts  15.1 us
    all_to_all x1, waiting for transfers between devices, per_device(): lax.all_to_all(send, 'dp', split_axis=0, concat_axis=0, tiled=True)  13.4 us
    all_to_all x1, waiting for transfers between devices, per_device(): lax.all_to_all(back, 'dp', split_axis=0, concat_axis=0, tiled=True)  11 us
  transfers between devices with their start and end apart: 4, of which 4 were waited for; matrix products, arithmetic and copies ran while one was open for 2% of the time, Pallas kernels for 0%

profile of v1, /device:TPU:1, one launch (start us, length us, event | category | flops | bytes accessed | tf_op | source)
XLA Modules:
  0.0 248.3 jit_solution(6215262927748242119)
XLA Ops:
  7.2 0.9 copy.16.routes_ref
  8.1 0.8 copy.17.weight_ref
  8.8 0.9 copy.14.tok_ref
  9.8 0.9 copy.15.cot_ref
  10.7 0.6 copy-done.7
  11.4 2.5 %shard_map.127 = (bf16[64,24,128]{2,1,0:T(8,128)(2,1)}, f32[128,64]{1,0:T(8,128)S(1)}, f32[128,64]{1,0:T(8,128)S(1)}) custom-call(bf16[128,224]{1,0:T(8,128)(2,1)S(1)} %copy.14.tok_ref, bf16[128,224]{1,0:T(8,128)(2,1)S(1)} %copy.15.cot_ref, s32[128,8]{1,0:T(8,128)S(1)} %copy.16.routes_ref, f32[128,8]{1,0:T(8,128)S(1)} %copy.17.weight_ref, s32[1,64]{1,0:T(1,128)S(1)} %bitcast.10), custom_call_target="tpu_custom_call" | custom-call | flops 300000000 | bytes 1000000 | tf_op jit(solution)/shard_map/pallas_call | solution.py:228
  13.9 0.6 copy-done.8
  14.5 0.6 copy-done.10
  15.1 18.2 %all-to-all-start = ((bf16[64,24,128]{2,1,0:T(8,128)(2,1)}), bf16[64,24,128]{2,1,0:T(8,128)(2,1)S(1)}, u32[]{:S(2)}, u32[]{:S(2)}) async-start(bf16[64,24,128]{2,1,0:T(8,128)(2,1)} %get-tuple-element.15), calls=%async_computation | async-start | bytes 786432 | tf_op jit(solution)/shard_map/all_to_all | solution.py:231
  33.4 1.2 copy.18.down_ref
  34.6 13.4 %all-to-all-done.recv_ref = bf16[64,24,128]{2,1,0:T(8,128)(2,1)S(1)} async-done(((bf16[64,24,128]{2,1,0:T(8,128)(2,1)}), bf16[64,24,128]{2,1,0:T(8,128)(2,1)S(1)}, u32[]{:S(2)}, u32[]{:S(2)}) %all-to-all-start) | async-done | bytes 393248 | tf_op jit(solution)/shard_map/all_to_all | solution.py:231
  48.1 2.6 %shard_map.128 = (bf16[384,3072]{1,0:T(8,128)(2,1)}, bf16[384,224]{1,0:T(8,128)(2,1)S(1)}, bf16[384,224]{1,0:T(8,128)(2,1)S(1)}) custom-call(bf16[64,24,128]{2,1,0:T(8,128)(2,1)S(1)} %all-to-all-done.recv_ref, bf16[1,224,1024]{2,1,0:T(8,128)(2,1)S(1)} %copy-done.2, bf16[1,224,1024]{2,1,0:T(8,128)(2,1)S(1)} %copy-done.4, bf16[1,1024,224]{2,1,0:T(8,128)(2,1)S(1)} %copy.18.down_ref), custom_call_target="tpu_custom_call" | custom-call | flops 700000000 | bytes 4500000 | tf_op jit(solution)/shard_map/pallas_call | solution.py:233
  50.7 0.0 all-gather.2.cloned.1.call-start
  50.7 64.8 %reduce-scatter.2.cloned.1.call-done.sum_ref = bf16[24,3072]{1,0:T(8,128)(2,1)} async-done(((bf16[384,3072]{1,0:T(8,128)(2,1)}), bf16[24,3072]{1,0:T(8,128)(2,1)}) %reduce-scatter.2.cloned.1.call-update) | async-done | bytes 147472 | tf_op jit(solution)/shard_map/reduce_scatter | solution.py:236
  115.5 0.9 copy-done.6
  116.4 0.8 shard_map.129
  117.3 77.9 %all-gather.2.cloned.1.call-done.full_ref = bf16[384,3200]{1,0:T(8,128)(2,1)} async-done(((bf16[24,3200]{1,0:T(8,128)(2,1)}), bf16[384,3200]{1,0:T(8,128)(2,1)}) %all-gather.2.cloned.1.call-update) | async-done | bytes 2457616 | tf_op jit(solution)/shard_map/all_gather | solution.py:240
  195.2 1.7 copy-done
  196.9 1.0 copy-done.3
  197.9 1.0 copy-done.5
  198.9 2.3 shard_map.130
  201.3 19.1 %all-to-all-start.1 = ((bf16[64,24,128]{2,1,0:T(8,128)(2,1)}), bf16[64,24,128]{2,1,0:T(8,128)(2,1)S(1)}, u32[]{:S(2)}, u32[]{:S(2)}) async-start(bf16[64,24,128]{2,1,0:T(8,128)(2,1)} %shard_map.130), calls=%async_computation.2 | async-start | bytes 786432 | tf_op jit(solution)/shard_map/all_to_all | solution.py:248
  220.4 1.2 fusion.1
  221.6 1.2 fusion
  222.8 1.2 fusion.2
  224.0 11.0 %all-to-all-done.1.back_ref = bf16[64,24,128]{2,1,0:T(8,128)(2,1)S(1)} async-done(((bf16[64,24,128]{2,1,0:T(8,128)(2,1)}), bf16[64,24,128]{2,1,0:T(8,128)(2,1)S(1)}, u32[]{:S(2)}, u32[]{:S(2)}) %all-to-all-start.1) | async-done | bytes 393248 | tf_op jit(solution)/shard_map/all_to_all | solution.py:248
  235.0 0.8 copy-done.9
  235.8 0.8 copy-done.11
  236.7 2.6 %shard_map.131 = (bf16[128,224]{1,0:T(8,128)(2,1)S(1)}, bf16[128,224]{1,0:T(8,128)(2,1)S(1)}, f32[128,8]{1,0:T(8,128)S(1)}) custom-call(bf16[64,24,128]{2,1,0:T(8,128)(2,1)S(1)} %all-to-all-done.1.back_ref, f32[128,64]{1,0:T(8,128)S(1)} %copy-done.9, f32[128,64]{1,0:T(8,128)S(1)} %copy-done.11, s32[128,8]{1,0:T(8,128)S(1)} %copy.16.routes_ref, ...), custom_call_target="tpu_custom_call" | custom-call | flops 500000000 | bytes 1000000 | tf_op jit(solution)/shard_map/pallas_call | solution.py:253
  239.3 0.7 copy.22
  240.1 0.7 copy.24
  240.7 0.7 copy.23
  (18 shorter events, 0.1 us)
Async XLA Ops:
  7.2 40.9 %copy-start.4 = (bf16[1,224,1024]{2,1,0:T(8,128)(2,1)S(1)}, bf16[1,224,1024]{2,1,0:T(8,128)(2,1)}, u32[]{:S(2)}) copy-start(bf16[1,224,1024]{2,1,0:T(8,128)(2,1)} %up_ref.3) | copy-start | bytes 1376260
  7.2 40.9 %copy-start.2 = (bf16[1,224,1024]{2,1,0:T(8,128)(2,1)S(1)}, bf16[1,224,1024]{2,1,0:T(8,128)(2,1)}, u32[]{:S(2)}) copy-start(bf16[1,224,1024]{2,1,0:T(8,128)(2,1)} %gate_ref.3) | copy-start | bytes 1376260
  10.7 0.7 copy-start.7
  13.9 0.6 copy-start.8
  14.5 0.6 copy-start.10
  15.1 32.9 %all-to-all-start = ((bf16[64,24,128]{2,1,0:T(8,128)(2,1)}), bf16[64,24,128]{2,1,0:T(8,128)(2,1)S(1)}, u32[]{:S(2)}, u32[]{:S(2)}) async-start(bf16[64,24,128]{2,1,0:T(8,128)(2,1)} %get-tuple-element.15), calls=%async_computation | async-start | bytes 786432 | tf_op jit(solution)/shard_map/all_to_all | solution.py:231
  33.4 82.2 %reduce-scatter.2.cloned.1.call-start = ((), (), s32[]{:S(2)}) async-start(), calls=%async_computation.3 | async-start | bytes 2506752 | tf_op jit(solution)/shard_map/reduce_scatter | solution.py:236
  50.7 144.5 %all-gather.2.cloned.1.call-start = ((), (), s32[]{:S(2)}) async-start(), calls=%async_computation.4 | async-start | bytes 2611200 | tf_op jit(solution)/shard_map/all_gather | solution.py:240
  115.5 0.9 copy-start.6
  195.2 1.7 copy-start
  196.9 1.0 copy-start.3
  197.9 1.0 copy-start.5
  198.9 21.5 %copy-start.1 = (bf16[384,3200]{1,0:T(8,128)(2,1)S(1)}, bf16[384,3200]{1,0:T(8,128)(2,1)}, u32[]{:S(2)}) copy-start(bf16[384,3200]{1,0:T(8,128)(2,1)} %all-gather.2.cloned.1.call-done.full_ref) | copy-start | bytes 7372804
  201.3 33.7 %all-to-all-start.1 = ((bf16[64,24,128]{2,1,0:T(8,128)(2,1)}), bf16[64,24,128]{2,1,0:T(8,128)(2,1)S(1)}, u32[]{:S(2)}, u32[]{:S(2)}) async-start(bf16[64,24,128]{2,1,0:T(8,128)(2,1)} %shard_map.130), calls=%async_computation.2 | async-start | bytes 786432 | tf_op jit(solution)/shard_map/all_to_all | solution.py:248
  235.0 0.8 copy-start.9
  235.8 0.8 copy-start.11
Sparse Core Ops, SparseCore 0:
  50.8 64.6 reduce-scatter.1
  118.8 76.3 all-gather.1

commit v2 on v1

v2 whole, which is shorter than its diff:
```python
import functools

import jax
import jax.numpy as jnp
from jax import lax
from jax.experimental import pallas as pl
from jax.experimental.pallas import tpu as pltpu
from jax.sharding import PartitionSpec as P

CAP = 6
SPARE = 2
LANES = 128
TILES = 4
GROUP = CAP * TILES
SOURCES = 16
RING = 4
SCORE_LANE = 96
VMEM_LIMIT = 24 * 1024 * 1024

F32 = jnp.float32
BF16 = jnp.bfloat16
CONTRACT_LAST = (((1,), (1,)), ((), ()))
CONTRACT_FIRST = (((0,), (0,)), ((), ()))


def dot(left, right, dims=(((1,), (0,)), ((), ()))):
    return lax.dot_general(left, right, dims, preferred_element_type=F32)


def one_zero(condition):
    return jnp.where(condition, 1.0, 0.0).astype(BF16)


def three_parts(value):
    high = value.astype(BF16)
    rest = value - high.astype(F32)
    middle = rest.astype(BF16)
    return high, middle, (rest - middle.astype(F32)).astype(BF16)


def iota(shape, axis):
    return lax.broadcasted_iota(jnp.int32, shape, axis)


def expert_of_row(row, expert):
    offset = row - GROUP * expert
    return (offset >= 0) & (offset < GROUP)


def tile_and_slot(row):
    place = row - GROUP * lax.shift_right_logical(row * 2731, 16)
    tile = (
        (place >= CAP).astype(jnp.int32)
        + (place >= 2 * CAP).astype(jnp.int32)
        + (place >= 3 * CAP).astype(jnp.int32)
    )
    return tile, place - CAP * tile


def reorder_matrix(sorted_row, sent_row):
    per_tile = SOURCES * CAP
    tile = (
        (sorted_row >= per_tile).astype(jnp.int32)
        + (sorted_row >= 2 * per_tile).astype(jnp.int32)
        + (sorted_row >= 3 * per_tile).astype(jnp.int32)
    )
    within = sorted_row - per_tile * tile
    source = lax.shift_right_logical(within * 43, 8)
    return one_zero(sent_row == within + (GROUP - CAP) * source + CAP * tile)


def interleave_matrix(row_count, parts):
    share = row_count // parts
    row = iota((row_count, 1), 0)
    part = sum((row >= share * i).astype(jnp.int32) for i in range(1, parts))
    ring = lax.shift_right_logical(part, 2)
    member = part - RING * ring
    kept = row + share * (member * (parts // RING) + ring - part)
    return one_zero(iota((row_count, row_count), 1) == kept)


def dispatch_kernel(tok_ref, cot_ref, routes_ref, weight_ref, slots_ref, send_ref, plan_ref):
    top_count, token_count = routes_ref.shape
    experts = slots_ref.shape[1]
    rows = experts * GROUP
    expert = iota((experts, token_count), 0)
    named = jnp.zeros((experts, token_count), F32)
    scale = jnp.zeros((experts, token_count), F32)
    for k in range(top_count):
        hit = routes_ref[k : k + 1] == expert
        named = named + jnp.where(hit, 1.0, 0.0)
        scale = scale + jnp.where(hit, weight_ref[k : k + 1], 0.0)
    earlier = one_zero(iota((token_count, token_count), 0) < iota((token_count, token_count), 1))
    rank = dot(named.astype(BF16), earlier)
    diagonal = iota((experts, experts), 0) == iota((experts, experts), 1)
    limit = jnp.sum(jnp.where(diagonal, slots_ref[...].astype(F32), 0.0), axis=1, keepdims=True)
    rank = jnp.where((named > 0.0) & (rank < limit + float(SPARE)), rank, -1.0)
    plan_ref[:experts] = rank
    plan_ref[experts:] = scale
    spread = one_zero(expert_of_row(iota((rows, experts), 0), iota((rows, experts), 1)))
    tile, slot = tile_and_slot(iota((rows, token_count), 0))
    taken = dot(spread, rank.astype(BF16)) == slot.astype(F32)
    row_scale = sum(dot(spread, part) for part in three_parts(scale))
    row_scale = jnp.sum(jnp.where(taken, row_scale, 0.0), axis=1, keepdims=True)
    row_scale = jnp.where(tile[:, :1] >= 2, row_scale, 1.0)
    width = tok_ref.shape[0]
    picked = jnp.zeros((rows, LANES), F32)
    for index, ref in ((0, tok_ref), (2, cot_ref)):
        high = jnp.concatenate(
            [ref[LANES:], jnp.zeros((2 * LANES - width, token_count), BF16)], axis=0
        )
        picked = picked + dot(one_zero(taken & (tile == index)), ref[:LANES], CONTRACT_LAST)
        picked = picked + dot(one_zero(taken & (tile == index + 1)), high, CONTRACT_LAST)
    send_ref[...] = (picked * row_scale).astype(BF16).reshape(send_ref.shape)


def partial_kernel(parts, recv_ref, gate_ref, up_ref, down_ref, part_ref, tok_ref, scaled_ref):
    experts = recv_ref.shape[0]
    width, hidden = gate_ref.shape
    block = SOURCES * GROUP
    per_tile = SOURCES * CAP
    reorder = reorder_matrix(iota((block, block), 0), iota((block, block), 1))
    for b in range(experts // SOURCES):
        sent = recv_ref[b * SOURCES : (b + 1) * SOURCES].reshape(block, LANES)
        rows = dot(reorder, sent).astype(BF16)
        place = slice(b * per_tile, (b + 1) * per_tile)
        for ref, index in ((tok_ref, 0), (scaled_ref, 2)):
            ref[place, :LANES] = rows[index * per_tile : (index + 1) * per_tile]
            ref[place, LANES:] = rows[(index + 1) * per_tile : (index + 2) * per_tile, : width - LANES]
    interleave = interleave_matrix(tok_ref.shape[0], parts)
    token_rows = dot(interleave, tok_ref[...]).astype(BF16)
    scaled_rows = dot(interleave, scaled_ref[...]).astype(BF16)
    step = 256
    for index, (rows, ref) in enumerate(
        ((token_rows, gate_ref), (token_rows, up_ref), (scaled_rows, down_ref))
    ):
        for start in range(0, hidden, step):
            value = dot(rows, ref[:, start : start + step]).astype(BF16)
            part_ref[:, index * hidden + start : index * hidden + start + step] = value


def middle_kernel(sum_ref, out_ref):
    hidden = sum_ref.shape[1] // 3
    gate = sum_ref[:, :hidden].astype(F32)
    up = sum_ref[:, hidden : 2 * hidden].astype(F32)
    grad = sum_ref[:, 2 * hidden :].astype(F32)
    sigmoid = jax.nn.sigmoid(gate)
    gated = gate * sigmoid
    hidden_value = (gated * up).astype(BF16)
    out_ref[:, :hidden] = hidden_value
    out_ref[:, hidden : 2 * hidden] = (grad * up * sigmoid * (1.0 + gate * (1.0 - sigmoid))).astype(BF16)
    out_ref[:, 2 * hidden : 3 * hidden] = (grad * gated).astype(BF16)
    score = jnp.sum(hidden_value.astype(F32) * grad, axis=1, keepdims=True)
    lane = iota((gate.shape[0], LANES), 1)
    packed = jnp.zeros(lane.shape, F32)
    for index, part in enumerate(three_parts(score)):
        packed = jnp.where(lane == SCORE_LANE + index, part.astype(F32), packed)
    out_ref[:, 3 * hidden :] = packed.astype(BF16)


def rows_kernel(
    place_ref,
    own_ref,
    left_ref,
    right_ref,
    far_left_ref,
    far_right_ref,
    gate_ref,
    up_ref,
    down_ref,
    back_ref,
    full_ref,
    tiles_ref,
):
    experts = back_ref.shape[0]
    width, hidden = gate_ref.shape
    block = SOURCES * GROUP
    per_tile = SOURCES * CAP
    held = own_ref.shape[0]
    half = held // 2
    for ref, step, start in (
        (own_ref, 0, 0),
        (right_ref, 1, 0),
        (left_ref, RING - 1, 0),
        (far_left_ref, RING // 2, 0),
        (far_right_ref, RING // 2, half),
    ):
        member = (place_ref[0] + step) & (RING - 1)
        begin = pl.multiple_of(member * held + start, half)
        full_ref[pl.ds(begin, ref.shape[0])] = ref[...]
    out_rows = dot(full_ref[:, :hidden], down_ref[...], CONTRACT_LAST)
    in_rows = dot(full_ref[:, hidden : 2 * hidden], gate_ref[...], CONTRACT_LAST) + dot(
        full_ref[:, 2 * hidden : 3 * hidden], up_ref[...], CONTRACT_LAST
    )
    tiles_ref[0] = out_rows[:, :LANES]
    tiles_ref[1] = full_ref[:, 3 * hidden :].astype(F32)
    tiles_ref[1, :, : width - LANES] = out_rows[:, LANES:]
    tiles_ref[2] = in_rows[:, :LANES]
    tiles_ref[3] = jnp.zeros(tiles_ref.shape[1:], F32)
    tiles_ref[3, :, : width - LANES] = in_rows[:, LANES:]
    restore = reorder_matrix(iota((block, block), 1), iota((block, block), 0))
    for b in range(experts // SOURCES):
        place = slice(b * per_tile, (b + 1) * per_tile)
        stacked = tiles_ref[:, place].astype(BF16).reshape(block, LANES)
        back_ref[b * SOURCES : (b + 1) * SOURCES] = (
            dot(restore, stacked).astype(BF16).reshape(SOURCES, GROUP, LANES)
        )


def combine_kernel(back_ref, plan_ref, routes_ref, weight_ref, mixed_ref, input_ref, score_ref):
    top_count, token_count = routes_ref.shape
    experts = plan_ref.shape[0] // 2
    width = mixed_ref.shape[0]
    rows = experts * GROUP
    back = back_ref[...].reshape(rows, LANES)
    plan = plan_ref[...].T
    rank, scale = plan[:, :experts], plan[:, experts:]
    spread = one_zero(expert_of_row(iota((experts, rows), 1), iota((experts, rows), 0)))
    tile, slot = tile_and_slot(iota((token_count, rows), 1))
    taken = dot(rank.astype(BF16), spread) == slot.astype(F32)
    mixed = [jnp.zeros((token_count, LANES), F32) for _ in range(2)]
    for part in three_parts(scale):
        row_scale = dot(part, spread)
        for index in range(2):
            chosen = jnp.where(taken & (tile == index), row_scale, 0.0).astype(BF16)
            mixed[index] = mixed[index] + dot(chosen, back)
    for ref, low, high in (
        (mixed_ref, mixed[0], mixed[1]),
        (
            input_ref,
            dot(one_zero(taken & (tile == 2)), back),
            dot(one_zero(taken & (tile == 3)), back),
        ),
    ):
        ref[:LANES] = low.T.astype(BF16)
        ref[LANES:] = high.T[: width - LANES].astype(BF16)
    lane = iota((8, LANES), 1)
    score_lanes = one_zero((lane >= SCORE_LANE) & (lane < SCORE_LANE + 3))
    row_score = dot(score_lanes, back, CONTRACT_LAST)[:1]
    routed = jnp.where(taken & (tile == 1), row_score, 0.0)
    by_expert = sum(dot(spread, part, CONTRACT_LAST) for part in three_parts(routed))
    expert = iota((experts, token_count), 0)
    for k in range(top_count):
        hit = routes_ref[k : k + 1] == expert
        value = jnp.sum(jnp.where(hit, by_expert, 0.0), axis=0, keepdims=True)
        score_ref[k : k + 1] = value / weight_ref[k : k + 1]


def kernel_call(body, out_shape, flops, moved, scalars=0, inputs=0, scratch=()):
    places = {}
    if scalars:
        places["in_specs"] = [pl.BlockSpec(memory_space=pltpu.SMEM)] * scalars + [
            pl.BlockSpec(memory_space=pltpu.VMEM)
        ] * inputs
    return pl.pallas_call(
        body,
        out_shape=out_shape,
        scratch_shapes=scratch,
        compiler_params=pltpu.CompilerParams(vmem_limit_bytes=VMEM_LIMIT),
        cost_estimate=pl.CostEstimate(flops=flops, bytes_accessed=moved, transcendentals=0),
        **places,
    )


def shifted(block, distance):
    parts = lax.axis_size("expert")
    return lax.ppermute(block, "expert", [(i, (i + distance) % parts) for i in range(parts)])


def per_device(
    tokens, cotangent, routes, route_weights, owner_slots, gate_weight, up_weight, down_weight
):
    experts = lax.axis_size("dp")
    parts = lax.axis_size("expert")
    token_count, width = tokens.shape
    hidden = gate_weight.shape[2]
    row_count = experts * CAP
    shape = jax.ShapeDtypeStruct
    exchanged = shape((experts, GROUP, LANES), BF16)
    routes_by_rank, weights_by_rank = routes.T, route_weights.T
    gate_matrix, up_matrix, down_matrix = gate_weight[0], up_weight[0], down_weight[0].T
    send, plan = kernel_call(
        dispatch_kernel, (exchanged, shape((2 * experts, token_count), F32)), 300_000_000, 1_000_000
    )(tokens.T, cotangent.T, routes_by_rank, weights_by_rank, owner_slots.reshape(1, experts))
    arrived = lax.all_to_all(send, "dp", split_axis=0, concat_axis=0, tiled=True)
    rows = shape((row_count, width), BF16)
    part, token_rows, scaled_rows = kernel_call(
        functools.partial(partial_kernel, parts),
        (shape((row_count, 3 * hidden), BF16), rows, rows),
        700_000_000,
        4_500_000,
    )(arrived, gate_matrix, up_matrix, down_matrix)
    summed = lax.psum_scatter(part, "expert", scatter_dimension=0, tiled=True)
    share = kernel_call(
        middle_kernel, shape((row_count // parts, 3 * hidden + LANES), BF16), 1_000_000, 300_000
    )(summed)
    own = lax.all_gather(
        share,
        "expert",
        axis=0,
        tiled=True,
        axis_index_groups=[list(range(i, parts, RING)) for i in range(RING)],
    )
    half = own.shape[0] // 2
    left, right = shifted(own, 1), shifted(own, -1)
    far_left, far_right = shifted(left[:half], 1), shifted(right[half:], -1)
    member = (lax.axis_index("expert") % RING).astype(jnp.int32).reshape(1)
    back, full = kernel_call(
        rows_kernel,
        (exchanged, shape((row_count, 3 * hidden + LANES), BF16)),
        700_000_000,
        4_500_000,
        scalars=1,
        inputs=8,
        scratch=[pltpu.VMEM((TILES, row_count, LANES), F32)],
    )(member, own, left, right, far_left, far_right, gate_matrix, up_matrix, down_matrix)
    returned = lax.all_to_all(back, "dp", split_axis=0, concat_axis=0, tiled=True)
    gate_grad = dot(token_rows, full[:, hidden : 2 * hidden], CONTRACT_FIRST).astype(BF16)
    up_grad = dot(token_rows, full[:, 2 * hidden : 3 * hidden], CONTRACT_FIRST).astype(BF16)
    down_grad = dot(scaled_rows, full[:, :hidden], CONTRACT_FIRST).astype(BF16).T
    token_shape = shape((width, token_count), BF16)
    mixed, input_gradient, route_gradient = kernel_call(
        combine_kernel,
        (token_shape, token_shape, shape(routes_by_rank.shape, F32)),
        500_000_000,
        1_000_000,
    )(returned, plan, routes_by_rank, weights_by_rank)
    return (
        mixed.T,
        input_gradient.T,
        route_gradient.T,
        gate_grad[None],
        up_grad[None],
        down_grad[None],
    )


def solution(mesh):
    return jax.shard_map(
        per_device,
        mesh=mesh,
        in_specs=(
            P("dp", "expert"),
            P("dp", "expert"),
            P("dp", None),
            P("dp", None),
            P(),
            P("dp", "expert", None),
            P("dp", "expert", None),
            P("dp", None, "expert"),
        ),
        out_specs=(
            P("dp", "expert"),
            P("dp", "expert"),
            P("dp", None),
            P("dp", "expert", None),
            P("dp", "expert", None),
            P("dp", None, "expert"),
        ),
        check_vma=False,
    )
```

time: 249 us -> 228 us (0.916)
  waiting for transfers between devices: 167 us -> 92.5 us
  blocking collectives: 0 us -> 54.7 us
  matrix products: 3.61 us -> 7.02 us
  local copies, waits for them, and re-layouts: 15.1 us -> 12 us
    all_gather x1 -> x0, waiting for transfers between devices: 77.9 us -> none  [per_device(): full = lax.all_gather(share, 'expert', axis=0, tiled=True)]
    all_to_all x0 -> x1, blocking collectives: none -> 32.1 us  [per_device(): lax.all_to_all(send, 'dp', split_axis=0, concat_axis=0, tiled=True)]
    all_gather x0 -> x1, blocking collectives: none -> 22.6 us  [per_device(): lax.all_gather(share, 'expert', axis=0, tiled=True, axis_index_groups=[li...]
    ppermute x0 -> x4, waiting for transfers between devices: none -> 19.5 us  [shifted(): lax.ppermute(block, 'expert', [(i, (i + distance) % parts) for i in range...]
    all_to_all x1 -> x0, starting transfers between devices: 18.2 us -> none  [per_device(): lax.all_to_all(send, 'dp', split_axis=0, concat_axis=0, tiled=True)]
    ppermute x0 -> x4, starting transfers between devices: none -> 14.3 us  [shifted(): lax.ppermute(block, 'expert', [(i, (i + distance) % parts) for i in range...]
    all_to_all x1 -> x0, waiting for transfers between devices: 13.4 us -> none  [per_device(): lax.all_to_all(send, 'dp', split_axis=0, concat_axis=0, tiled=True)]
    unnamed x32 -> x36, local copies, waits for them, and re-layouts: 15.1 us -> 10.5 us
  transfers between devices with their start and end apart: 4 -> 6, of which waited for: 4 -> 5; matrix products, arithmetic and copies ran while one was open for 2% -> 4% of each run, Pallas kernels for 0% -> 0%
where the time goes in v2:
time: 228 us
  waiting for transfers between devices  92.5 us (41%)
  blocking collectives  54.7 us (24%)
  starting transfers between devices  36.8 us (16%)
  between operations  14.1 us (6%)
  local copies, waits for them, and re-layouts  12 us (5%)
  Pallas kernels  10.3 us (5%)
  matrix products  7.02 us (3%)
    reduce_scatter x1, waiting for transfers between devices, per_device(): summed = lax.psum_scatter(part, 'expert', scatter_dimension=0, tiled=True)  65.4 us
    all_to_all x1, blocking collectives, per_device(): lax.all_to_all(send, 'dp', split_axis=0, concat_axis=0, tiled=True)  32.1 us
    all_gather x1, blocking collectives, per_device(): lax.all_gather(share, 'expert', axis=0, tiled=True, axis_index_groups=[li...  22.6 us
    all_to_all x1, starting transfers between devices, per_device(): lax.all_to_all(back, 'dp', split_axis=0, concat_axis=0, tiled=True)  22.5 us
    ppermute x4, waiting for transfers between devices, shifted(): lax.ppermute(block, 'expert', [(i, (i + distance) % parts) for i in range...  19.5 us
    ppermute x4, starting transfers between devices, shifted(): lax.ppermute(block, 'expert', [(i, (i + distance) % parts) for i in range...  14.3 us
    unnamed x36, local copies, waits for them, and re-layouts  10.5 us
    all_to_all x1, waiting for transfers between devices, per_device(): lax.all_to_all(back, 'dp', split_axis=0, concat_axis=0, tiled=True)  7.59 us
  transfers between devices with their start and end apart: 6, of which 5 were waited for; matrix products, arithmetic and copies ran while one was open for 4% of the time, Pallas kernels for 0%

profile of v2, /device:TPU:1, one launch (start us, length us, event | category | flops | bytes accessed | tf_op | source)
XLA Modules:
  0.0 227.5 jit_solution(6106832537898242014)
XLA Ops:
  7.2 0.8 copy-done.9
  8.0 0.8 copy-done.10
  8.9 0.7 copy-done.11
  9.5 0.7 copy-done.13
  10.9 1.4 shard_map.127
  12.3 32.1 %all_to_all.10.recv_ref = bf16[64,24,128]{2,1,0:T(8,128)(2,1)S(1)} all-to-all(bf16[64,24,128]{2,1,0:T(8,128)(2,1)S(1)} %get-tuple-element.16), channel_id=1, replica_groups=mesh['expert'=16,'dp'=64] {'dp'}, dimensions={0} | all-to-all | bytes 786432 | tf_op jit(solution)/shard_map/all_to_all | solution.py:285
  44.5 1.0 copy-done.1
  45.5 1.0 copy-done.3
  46.5 1.0 copy-done.5
  47.5 2.8 %shard_map.128 = (bf16[384,3072]{1,0:T(8,128)(2,1)}, bf16[384,224]{1,0:T(8,128)(2,1)S(1)}, bf16[384,224]{1,0:T(8,128)(2,1)S(1)}) custom-call(bf16[64,24,128]{2,1,0:T(8,128)(2,1)S(1)} %all_to_all.10.recv_ref, bf16[224,1024]{1,0:T(8,128)(2,1)S(1)} %bitcast.23, bf16[224,1024]{1,0:T(8,128)(2,1)S(1)} %bitcast.25, bf16[224,1024]{1,0:T(8,128)(2,1)S(1)} %bitcast.27), custom_call_target="tpu_custom_call" | custom-call | flops 700000000 | bytes 4500000 | tf_op jit(solution)/shard_map/pallas_call | solution.py:287
  50.3 0.7 copy-done.16
  51.1 65.4 %reduce-scatter.2.cloned.1.call-done.sum_ref = bf16[24,3072]{1,0:T(8,128)(2,1)} async-done(((bf16[384,3072]{1,0:T(8,128)(2,1)}), bf16[24,3072]{1,0:T(8,128)(2,1)}) %reduce-scatter.2.cloned.1.call-update) | async-done | bytes 147472 | tf_op jit(solution)/shard_map/reduce_scatter | solution.py:293
  116.4 0.9 copy-done.8
  117.4 22.6 %all_gather.3.own_ref = bf16[96,3200]{1,0:T(8,128)(2,1)S(1)} all-gather(bf16[24,3200]{1,0:T(8,128)(2,1)S(1)} %shard_map.129), channel_id=1, replica_groups={{0,256,512,768},{64,320,576,832},{128,384,640,896},{192,448,704,960},{1..., dimensions={0}, use_global_device_ids=true | all-gather | bytes 768000 | tf_op jit(solution)/shard_map/all_gather | solution.py:297
  140.0 5.4 %collective-permute-start.1 = (bf16[96,3200]{1,0:T(8,128)(2,1)S(1)}, bf16[96,3200]{1,0:T(8,128)(2,1)S(1)}, u32[]{:S(2)}, u32[]{:S(2)}) collective-permute-start(bf16[96,3200]{1,0:T(8,128)(2,1)S(1)} %all_gather.3.own_ref), channel_id=1, source_target_pairs={{0,960},{64,0},{128,64},{192,128},{256,192},{320,256},{384,320},{4... | collective-permute-start | bytes 1843208 | tf_op jit(solution)/shard_map/ppermute | solution.py:267
  145.5 1.9 collective-permute-start
  147.4 8.8 %collective-permute-done.1.right_ref = bf16[96,3200]{1,0:T(8,128)(2,1)S(1)} collective-permute-done((bf16[96,3200]{1,0:T(8,128)(2,1)S(1)}, bf16[96,3200]{1,0:T(8,128)(2,1)S(1)}, u32[]{:S(2)}, u32[]{:S(2)}) %collective-permute-start.1) | collective-permute-done | bytes 614432 | tf_op jit(solution)/shard_map/ppermute | solution.py:267
  156.2 0.7 slice.21
  156.9 5.0 %collective-permute-start.3 = (bf16[48,3200]{1,0:T(8,128)(2,1)}, bf16[48,3200]{1,0:T(8,128)(2,1)}, u32[]{:S(2)}, u32[]{:S(2)}) collective-permute-start(bf16[48,3200]{1,0:T(8,128)(2,1)} %slice.21), channel_id=1, source_target_pairs={{0,960},{64,0},{128,64},{192,128},{256,192},{320,256},{384,320},{4... | collective-permute-start | bytes 921608 | tf_op jit(solution)/shard_map/ppermute | solution.py:267
  161.9 0.7 slice.20
  162.7 1.9 collective-permute-start.2
  164.6 4.8 %collective-permute-done.3.far_right_ref = bf16[48,3200]{1,0:T(8,128)(2,1)} collective-permute-done((bf16[48,3200]{1,0:T(8,128)(2,1)}, bf16[48,3200]{1,0:T(8,128)(2,1)}, u32[]{:S(2)}, u32[]{:S(2)}) %collective-permute-start.3) | collective-permute-done | bytes 307232 | tf_op jit(solution)/shard_map/ppermute | solution.py:267
  169.4 6.0 %collective-permute-done.2.far_left_ref = bf16[48,3200]{1,0:T(8,128)(2,1)} collective-permute-done((bf16[48,3200]{1,0:T(8,128)(2,1)}, bf16[48,3200]{1,0:T(8,128)(2,1)}, u32[]{:S(2)}, u32[]{:S(2)}) %collective-permute-start.2) | collective-permute-done | bytes 307232 | tf_op jit(solution)/shard_map/ppermute | solution.py:267
  175.3 2.8 %shard_map.130 = (bf16[64,24,128]{2,1,0:T(8,128)(2,1)S(1)}, bf16[384,3200]{1,0:T(8,128)(2,1)S(1)}) custom-call(s32[1]{0:T(128)} %bitcast.place_ref, bf16[96,3200]{1,0:T(8,128)(2,1)S(1)} %all_gather.3.own_ref, bf16[96,3200]{1,0:T(8,128)(2,1)S(1)} %collective-permute-done.left_ref, bf16[96,3200]{1,0:T(8,128)(2,1)S(1)} %collective-permute-done.1.right_ref, ...), custom_call_target="tpu_custom_call" | custom-call | flops 700000000 | bytes 4500000 | tf_op jit(solution)/shard_map/pallas_call | solution.py:308
  178.1 1.4 copy-done
  179.6 0.8 copy-done.7
  180.3 22.5 %all-to-all-start.1 = ((bf16[64,24,128]{2,1,0:T(8,128)(2,1)}), bf16[64,24,128]{2,1,0:T(8,128)(2,1)S(1)}, u32[]{:S(2)}, u32[]{:S(2)}) async-start(bf16[64,24,128]{2,1,0:T(8,128)(2,1)} %copy-done.7), calls=%async_computation.2 | async-start | bytes 786432 | tf_op jit(solution)/shard_map/all_to_all | solution.py:317
  202.9 2.3 %fusion.1 = bf16[1,224,1024]{2,1,0:T(8,128)(2,1)} fusion(bf16[384,224]{1,0:T(8,128)(2,1)S(1)} %get-tuple-element.23, bf16[384,3200]{1,0:T(8,128)(2,1)} %copy-done), kind=kOutput, calls=%fused_computation.4 | convolution fusion | flops 176390144 | bytes 1417216 | tf_op jit(solution)/shard_map/dot_general | solution.py:27
  205.2 2.3 %fusion = bf16[1,224,1024]{2,1,0:T(8,128)(2,1)} fusion(bf16[384,224]{1,0:T(8,128)(2,1)S(1)} %get-tuple-element.23, bf16[384,3200]{1,0:T(8,128)(2,1)} %copy-done), kind=kOutput, calls=%fused_computation.3 | convolution fusion | flops 176390144 | bytes 1417216 | tf_op jit(solution)/shard_map/dot_general | solution.py:27
  207.5 2.4 %fusion.2 = bf16[1,1024,224]{1,2,0:T(8,128)(2,1)} fusion(bf16[384,224]{1,0:T(8,128)(2,1)S(1)} %copy-done.17, bf16[384,3200]{1,0:T(8,128)(2,1)} %copy-done), kind=kOutput, calls=%fused_computation.5 | convolution fusion | flops 176390144 | bytes 1417216 | tf_op jit(solution)/shard_map/dot_general | solution.py:27
  209.9 7.6 %all-to-all-done.1.back_ref = bf16[64,24,128]{2,1,0:T(8,128)(2,1)S(1)} async-done(((bf16[64,24,128]{2,1,0:T(8,128)(2,1)}), bf16[64,24,128]{2,1,0:T(8,128)(2,1)S(1)}, u32[]{:S(2)}, u32[]{:S(2)}) %all-to-all-start.1) | async-done | bytes 393248 | tf_op jit(solution)/shard_map/all_to_all | solution.py:317
  217.5 3.2 %shard_map.131 = (bf16[224,128]{1,0:T(8,128)(2,1)}, bf16[224,128]{1,0:T(8,128)(2,1)}, f32[8,128]{1,0:T(8,128)}) custom-call(bf16[64,24,128]{2,1,0:T(8,128)(2,1)S(1)} %all-to-all-done.1.back_ref, f32[128,128]{1,0:T(8,128)S(1)} %get-tuple-element.19.plan_ref, s32[8,128]{1,0:T(8,128)S(1)} %bitcast.32, f32[8,128]{1,0:T(8,128)S(1)} %bitcast.34), custom_call_target="tpu_custom_call" | custom-call | flops 500000000 | bytes 1000000 | tf_op jit(solution)/shard_map/pallas_call | solution.py:322
  (29 shorter events, 0.9 us)
Async XLA Ops:
  7.2 109.2 %reduce-scatter.2.cloned.1.call-start = ((), (), s32[]{:S(2)}) async-start(), calls=%async_computation.3 | async-start | bytes 2506752 | tf_op jit(solution)/shard_map/reduce_scatter | solution.py:293
  7.2 0.8 copy-start.9
  8.0 0.8 copy-start.10
  8.9 0.7 copy-start.11
  9.5 0.7 copy-start.13
  10.2 0.7 copy-start.15
  44.4 1.0 copy-start.1
  45.5 1.0 copy-start.3
  46.5 1.0 copy-start.5
  50.3 0.7 copy-start.16
  51.0 124.3 %copy-start.2 = (bf16[1,224,1024]{2,1,0:T(8,128)(2,1)S(1)}, bf16[1,224,1024]{2,1,0:T(8,128)(2,1)}, u32[]{:S(2)}) copy-start(bf16[1,224,1024]{2,1,0:T(8,128)(2,1)} %param.13) | copy-start | bytes 1376260
  51.0 124.3 %copy-start.4 = (bf16[1,224,1024]{2,1,0:T(8,128)(2,1)S(1)}, bf16[1,224,1024]{2,1,0:T(8,128)(2,1)}, u32[]{:S(2)}) copy-start(bf16[1,224,1024]{2,1,0:T(8,128)(2,1)} %param.14) | copy-start | bytes 1376260
  51.0 124.3 %copy-start.6 = (bf16[1,1024,224]{1,2,0:T(8,128)(2,1)S(1)}, bf16[1,1024,224]{1,2,0:T(8,128)(2,1)}, u32[]{:S(2)}) copy-start(bf16[1,1024,224]{1,2,0:T(8,128)(2,1)} %param.15) | copy-start | bytes 1376260
  116.4 0.9 copy-start.8
  140.0 16.1 %collective-permute-start.1 = (bf16[96,3200]{1,0:T(8,128)(2,1)S(1)}, bf16[96,3200]{1,0:T(8,128)(2,1)S(1)}, u32[]{:S(2)}, u32[]{:S(2)}) collective-permute-start(bf16[96,3200]{1,0:T(8,128)(2,1)S(1)} %all_gather.3.own_ref), channel_id=1, source_target_pairs={{0,960},{64,0},{128,64},{192,128},{256,192},{320,256},{384,320},{4... | collective-permute-start | bytes 1843208 | tf_op jit(solution)/shard_map/ppermute | solution.py:267
  145.5 16.5 %collective-permute-start = (bf16[96,3200]{1,0:T(8,128)(2,1)S(1)}, bf16[96,3200]{1,0:T(8,128)(2,1)S(1)}, u32[]{:S(2)}, u32[]{:S(2)}) collective-permute-start(bf16[96,3200]{1,0:T(8,128)(2,1)S(1)} %all_gather.3.own_ref), channel_id=1, source_target_pairs={{0,64},{64,128},{128,192},{192,256},{256,320},{320,384},{384,448},... | collective-permute-start | bytes 1843208 | tf_op jit(solution)/shard_map/ppermute | solution.py:267
  156.9 12.5 %collective-permute-start.3 = (bf16[48,3200]{1,0:T(8,128)(2,1)}, bf16[48,3200]{1,0:T(8,128)(2,1)}, u32[]{:S(2)}, u32[]{:S(2)}) collective-permute-start(bf16[48,3200]{1,0:T(8,128)(2,1)} %slice.21), channel_id=1, source_target_pairs={{0,960},{64,0},{128,64},{192,128},{256,192},{320,256},{384,320},{4... | collective-permute-start | bytes 921608 | tf_op jit(solution)/shard_map/ppermute | solution.py:267
  162.7 12.7 %collective-permute-start.2 = (bf16[48,3200]{1,0:T(8,128)(2,1)}, bf16[48,3200]{1,0:T(8,128)(2,1)}, u32[]{:S(2)}, u32[]{:S(2)}) collective-permute-start(bf16[48,3200]{1,0:T(8,128)(2,1)} %slice.20), channel_id=1, source_target_pairs={{0,64},{64,128},{128,192},{192,256},{256,320},{320,384},{384,448},... | collective-permute-start | bytes 921608 | tf_op jit(solution)/shard_map/ppermute | solution.py:267
  178.1 1.5 copy-start
  179.6 0.8 copy-start.7
  180.3 27.2 %copy-start.17 = (bf16[384,224]{1,0:T(8,128)(2,1)S(1)}, bf16[384,224]{1,0:T(8,128)(2,1)}, u32[]{:S(2)}) copy-start(bf16[384,224]{1,0:T(8,128)(2,1)} %copy-done.16) | copy-start | bytes 516100
  180.3 37.2 %copy-start.12 = (s32[128,8]{0,1:T(8,128)S(1)}, s32[128,8]{0,1:T(8,128)}, u32[]{:S(2)}) copy-start(s32[128,8]{0,1:T(8,128)} %param.10) | copy-start | bytes 12292
  180.3 37.2 %copy-start.14 = (f32[128,8]{0,1:T(8,128)S(1)}, f32[128,8]{0,1:T(8,128)}, u32[]{:S(2)}) copy-start(f32[128,8]{0,1:T(8,128)} %param.11) | copy-start | bytes 12292
  180.3 37.1 %all-to-all-start.1 = ((bf16[64,24,128]{2,1,0:T(8,128)(2,1)}), bf16[64,24,128]{2,1,0:T(8,128)(2,1)S(1)}, u32[]{:S(2)}, u32[]{:S(2)}) async-start(bf16[64,24,128]{2,1,0:T(8,128)(2,1)} %copy-done.7), calls=%async_computation.2 | async-start | bytes 786432 | tf_op jit(solution)/shard_map/all_to_all | solution.py:317
Sparse Core Ops, SparseCore 0:
  51.2 65.1 reduce-scatter.1

commit v3 on v2

--- a/solution.py
+++ b/solution.py
@@ -1,5 +1,3 @@
-import functools
-
 import jax
 import jax.numpy as jnp
 from jax import lax
@@ -69,17 +67,35 @@
     return one_zero(sent_row == within + (GROUP - CAP) * source + CAP * tile)
 
 
-def interleave_matrix(row_count, parts):
-    share = row_count // parts
-    row = iota((row_count, 1), 0)
-    part = sum((row >= share * i).astype(jnp.int32) for i in range(1, parts))
-    ring = lax.shift_right_logical(part, 2)
-    member = part - RING * ring
-    kept = row + share * (member * (parts // RING) + ring - part)
-    return one_zero(iota((row_count, row_count), 1) == kept)
-
-
-def dispatch_kernel(tok_ref, cot_ref, routes_ref, weight_ref, slots_ref, send_ref, plan_ref):
+def fetch(sources, targets, sems):
+    copies = [
+        pltpu.make_async_copy(source, target, sems.at[i])
+        for i, (source, target) in enumerate(zip(sources, targets))
+    ]
+    for copy in copies:
+        copy.start()
+    return copies
+
+
+def dispatch_kernel(
+    routes_hbm,
+    weight_hbm,
+    slots_hbm,
+    tok_hbm,
+    cot_hbm,
+    send_ref,
+    plan_ref,
+    routes_ref,
+    weight_ref,
+    slots_ref,
+    tok_ref,
+    cot_ref,
+    sems,
+):
+    arguments = (routes_hbm, weight_hbm, slots_hbm, tok_hbm, cot_hbm)
+    held = (routes_ref, weight_ref, slots_ref, tok_ref, cot_ref)
+    for copy in fetch(arguments, held, sems):
+        copy.wait()
     top_count, token_count = routes_ref.shape
     experts = slots_ref.shape[1]
     rows = experts * GROUP
@@ -114,7 +130,25 @@
     send_ref[...] = (picked * row_scale).astype(BF16).reshape(send_ref.shape)
 
 
-def partial_kernel(parts, recv_ref, gate_ref, up_ref, down_ref, part_ref, tok_ref, scaled_ref):
+def partial_kernel(
+    place_ref,
+    recv_ref,
+    gate_hbm,
+    up_hbm,
+    down_hbm,
+    own_ref,
+    to_right_ref,
+    to_left_ref,
+    next_ref,
+    previous_ref,
+    tok_ref,
+    scaled_ref,
+    gate_ref,
+    up_ref,
+    down_ref,
+    sems,
+):
+    copies = fetch((gate_hbm, up_hbm, down_hbm), (gate_ref, up_ref, down_ref), sems)
     experts = recv_ref.shape[0]
     width, hidden = gate_ref.shape
     block = SOURCES * GROUP
@@ -127,23 +161,52 @@
         for ref, index in ((tok_ref, 0), (scaled_ref, 2)):
             ref[place, :LANES] = rows[index * per_tile : (index + 1) * per_tile]
             ref[place, LANES:] = rows[(index + 1) * per_tile : (index + 2) * per_tile, : width - LANES]
-    interleave = interleave_matrix(tok_ref.shape[0], parts)
-    token_rows = dot(interleave, tok_ref[...]).astype(BF16)
-    scaled_rows = dot(interleave, scaled_ref[...]).astype(BF16)
-    step = 256
-    for index, (rows, ref) in enumerate(
-        ((token_rows, gate_ref), (token_rows, up_ref), (scaled_rows, down_ref))
+    held = tok_ref.shape[0] // RING
+    half = held // 2
+    for copy in copies:
+        copy.wait()
+    for index, (rows_ref, ref) in enumerate(
+        ((tok_ref, gate_ref), (tok_ref, up_ref), (scaled_ref, down_ref))
     ):
-        for start in range(0, hidden, step):
-            value = dot(rows, ref[:, start : start + step]).astype(BF16)
-            part_ref[:, index * hidden + start : index * hidden + start + step] = value
+        columns = slice(index * hidden, (index + 1) * hidden)
+        for step, pieces in (
+            (RING // 2, ((to_right_ref, 0), (to_left_ref, half))),
+            (1, ((next_ref, 0), (to_right_ref, half))),
+            (RING - 1, ((to_left_ref, 0), (previous_ref, 0))),
+            (0, ((own_ref, 0), (own_ref, half))),
+        ):
+            member = (place_ref[0] + step) & (RING - 1)
+            begin = pl.multiple_of(member * held, held)
+            value = dot(rows_ref[pl.ds(begin, held)], ref[...]).astype(BF16)
+            for part, (out_ref, start) in enumerate(pieces):
+                out_ref[start : start + half, columns] = value[part * half : (part + 1) * half]
+
+
+def relay_kernel(next_ref, previous_ref, from_left_ref, from_right_ref, to_right_ref, to_left_ref):
+    half = next_ref.shape[0]
+    to_right_ref[...] = (next_ref[...].astype(F32) + from_left_ref[:half].astype(F32)).astype(BF16)
+    to_left_ref[...] = (previous_ref[...].astype(F32) + from_right_ref[half:].astype(F32)).astype(BF16)
+
+
+def window_kernel(own_ref, from_left_ref, from_right_ref, far_left_ref, far_right_ref, out_ref):
+    half = far_left_ref.shape[0]
+    out_ref[:half] = (
+        own_ref[:half].astype(F32) + from_right_ref[:half].astype(F32) + far_left_ref[...].astype(F32)
+    ).astype(BF16)
+    out_ref[half:] = (
+        own_ref[half:].astype(F32) + from_left_ref[half:].astype(F32) + far_right_ref[...].astype(F32)
+    ).astype(BF16)
 
 
 def middle_kernel(sum_ref, out_ref):
     hidden = sum_ref.shape[1] // 3
-    gate = sum_ref[:, :hidden].astype(F32)
-    up = sum_ref[:, hidden : 2 * hidden].astype(F32)
-    grad = sum_ref[:, 2 * hidden :].astype(F32)
+    share = out_ref.shape[0]
+
+    def summed(index):
+        values = sum_ref[:, index * hidden : (index + 1) * hidden].astype(F32)
+        return sum(values[i * share : (i + 1) * share] for i in range(sum_ref.shape[0] // share))
+
+    gate, up, grad = summed(0), summed(1), summed(2)
     sigmoid = jax.nn.sigmoid(gate)
     gated = gate * sigmoid
     hidden_value = (gated * up).astype(BF16)
@@ -158,24 +221,7 @@
     out_ref[:, 3 * hidden :] = packed.astype(BF16)
 
 
-def rows_kernel(
-    place_ref,
-    own_ref,
-    left_ref,
-    right_ref,
-    far_left_ref,
-    far_right_ref,
-    gate_ref,
-    up_ref,
-    down_ref,
-    back_ref,
-    full_ref,
-    tiles_ref,
-):
-    experts = back_ref.shape[0]
-    width, hidden = gate_ref.shape
-    block = SOURCES * GROUP
-    per_tile = SOURCES * CAP
+def gathered(full_ref, place_ref, own_ref, left_ref, right_ref, far_left_ref, far_right_ref):
     held = own_ref.shape[0]
     half = held // 2
     for ref, step, start in (
@@ -188,6 +234,57 @@
         member = (place_ref[0] + step) & (RING - 1)
         begin = pl.multiple_of(member * held + start, half)
         full_ref[pl.ds(begin, ref.shape[0])] = ref[...]
+
+
+def gradient_kernel(
+    place_ref,
+    own_ref,
+    left_ref,
+    right_ref,
+    far_left_ref,
+    far_right_ref,
+    tok_ref,
+    scaled_ref,
+    gate_ref,
+    up_ref,
+    down_ref,
+    full_ref,
+):
+    hidden = gate_ref.shape[1]
+    gathered(full_ref, place_ref, own_ref, left_ref, right_ref, far_left_ref, far_right_ref)
+    for index, (rows_ref, out_ref) in enumerate(
+        ((scaled_ref, down_ref), (tok_ref, gate_ref), (tok_ref, up_ref))
+    ):
+        columns = slice(index * hidden, (index + 1) * hidden)
+        out_ref[...] = dot(rows_ref[...], full_ref[:, columns], CONTRACT_FIRST).astype(BF16)
+
+
+def rows_kernel(
+    place_ref,
+    own_ref,
+    left_ref,
+    right_ref,
+    far_left_ref,
+    far_right_ref,
+    gate_hbm,
+    up_hbm,
+    down_hbm,
+    back_ref,
+    full_ref,
+    tiles_ref,
+    gate_ref,
+    up_ref,
+    down_ref,
+    sems,
+):
+    copies = fetch((gate_hbm, up_hbm, down_hbm), (gate_ref, up_ref, down_ref), sems)
+    experts = back_ref.shape[0]
+    width, hidden = gate_ref.shape
+    block = SOURCES * GROUP
+    per_tile = SOURCES * CAP
+    gathered(full_ref, place_ref, own_ref, left_ref, right_ref, far_left_ref, far_right_ref)
+    for copy in copies:
+        copy.wait()
     out_rows = dot(full_ref[:, :hidden], down_ref[...], CONTRACT_LAST)
     in_rows = dot(full_ref[:, hidden : 2 * hidden], gate_ref[...], CONTRACT_LAST) + dot(
         full_ref[:, 2 * hidden : 3 * hidden], up_ref[...], CONTRACT_LAST
@@ -246,12 +343,11 @@
         score_ref[k : k + 1] = value / weight_ref[k : k + 1]
 
 
-def kernel_call(body, out_shape, flops, moved, scalars=0, inputs=0, scratch=()):
+def kernel_call(body, out_shape, flops, moved, spaces=None, scratch=()):
     places = {}
-    if scalars:
-        places["in_specs"] = [pl.BlockSpec(memory_space=pltpu.SMEM)] * scalars + [
-            pl.BlockSpec(memory_space=pltpu.VMEM)
-        ] * inputs
+    if spaces is not None:
+        kinds = {"s": pltpu.SMEM, "v": pltpu.VMEM, "a": pl.ANY}
+        places["in_specs"] = [pl.BlockSpec(memory_space=kinds[kind]) for kind in spaces]
     return pl.pallas_call(
         body,
         out_shape=out_shape,
@@ -260,6 +356,12 @@
         cost_estimate=pl.CostEstimate(flops=flops, bytes_accessed=moved, transcendentals=0),
         **places,
     )
+
+
+def held_copies(*arrays):
+    return [pltpu.VMEM(array.shape, array.dtype) for array in arrays] + [
+        pltpu.SemaphoreType.DMA((len(arrays),))
+    ]
 
 
 def shifted(block, distance):
@@ -275,56 +377,77 @@
     token_count, width = tokens.shape
     hidden = gate_weight.shape[2]
     row_count = experts * CAP
+    held = row_count // RING
     shape = jax.ShapeDtypeStruct
     exchanged = shape((experts, GROUP, LANES), BF16)
-    routes_by_rank, weights_by_rank = routes.T, route_weights.T
-    gate_matrix, up_matrix, down_matrix = gate_weight[0], up_weight[0], down_weight[0].T
+    rows = shape((row_count, width), BF16)
+    whole, halved = (shape((size, 3 * hidden), BF16) for size in (held, held // 2))
+    groups = [list(range(i, parts, RING)) for i in range(RING)]
+    member = (lax.axis_index("expert") % RING).astype(jnp.int32).reshape(1)
+    weights = (gate_weight[0], up_weight[0], down_weight[0].T)
+    arguments = (routes.T, route_weights.T, owner_slots.reshape(1, experts), tokens.T, cotangent.T)
     send, plan = kernel_call(
-        dispatch_kernel, (exchanged, shape((2 * experts, token_count), F32)), 300_000_000, 1_000_000
-    )(tokens.T, cotangent.T, routes_by_rank, weights_by_rank, owner_slots.reshape(1, experts))
+        dispatch_kernel,
+        (exchanged, shape((2 * experts, token_count), F32)),
+        300_000_000,
+        1_000_000,
+        spaces="aaaaa",
+        scratch=held_copies(*arguments),
+    )(*arguments)
     arrived = lax.all_to_all(send, "dp", split_axis=0, concat_axis=0, tiled=True)
-    rows = shape((row_count, width), BF16)
-    part, token_rows, scaled_rows = kernel_call(
-        functools.partial(partial_kernel, parts),
-        (shape((row_count, 3 * hidden), BF16), rows, rows),
+    own, to_right, to_left, following, previous, token_rows, scaled_rows = kernel_call(
+        partial_kernel,
+        (whole, whole, whole, halved, halved, rows, rows),
         700_000_000,
         4_500_000,
-    )(arrived, gate_matrix, up_matrix, down_matrix)
-    summed = lax.psum_scatter(part, "expert", scatter_dimension=0, tiled=True)
+        spaces="svaaa",
+        scratch=held_copies(*weights),
+    )(member, arrived, *weights)
+    from_left, from_right = shifted(to_right, 1), shifted(to_left, -1)
+    relay_right, relay_left = kernel_call(relay_kernel, (halved, halved), 300_000, 1_500_000)(
+        following, previous, from_left, from_right
+    )
+    far_left, far_right = shifted(relay_right, 1), shifted(relay_left, -1)
+    window = kernel_call(window_kernel, whole, 600_000, 2_000_000)(
+        own, from_left, from_right, far_left, far_right
+    )
+    summands = lax.all_to_all(
+        window, "expert", split_axis=0, concat_axis=0, tiled=True, axis_index_groups=groups
+    )
     share = kernel_call(
-        middle_kernel, shape((row_count // parts, 3 * hidden + LANES), BF16), 1_000_000, 300_000
-    )(summed)
-    own = lax.all_gather(
-        share,
-        "expert",
-        axis=0,
-        tiled=True,
-        axis_index_groups=[list(range(i, parts, RING)) for i in range(RING)],
-    )
-    half = own.shape[0] // 2
+        middle_kernel, shape((row_count // parts, 3 * hidden + LANES), BF16), 1_000_000, 700_000
+    )(summands)
+    own = lax.all_gather(share, "expert", axis=0, tiled=True, axis_index_groups=groups)
+    half = held // 2
     left, right = shifted(own, 1), shifted(own, -1)
-    far_left, far_right = shifted(left[:half], 1), shifted(right[half:], -1)
-    member = (lax.axis_index("expert") % RING).astype(jnp.int32).reshape(1)
-    back, full = kernel_call(
+    pieces = (own, left, right, shifted(left[:half], 1), shifted(right[half:], -1))
+    full = pltpu.VMEM((row_count, 3 * hidden + LANES), BF16)
+    back = kernel_call(
         rows_kernel,
-        (exchanged, shape((row_count, 3 * hidden + LANES), BF16)),
+        exchanged,
         700_000_000,
         4_500_000,
-        scalars=1,
-        inputs=8,
-        scratch=[pltpu.VMEM((TILES, row_count, LANES), F32)],
-    )(member, own, left, right, far_left, far_right, gate_matrix, up_matrix, down_matrix)
+        spaces="svvvvvaaa",
+        scratch=[full, pltpu.VMEM((TILES, row_count, LANES), F32)] + held_copies(*weights),
+    )(member, *pieces, *weights)
     returned = lax.all_to_all(back, "dp", split_axis=0, concat_axis=0, tiled=True)
-    gate_grad = dot(token_rows, full[:, hidden : 2 * hidden], CONTRACT_FIRST).astype(BF16)
-    up_grad = dot(token_rows, full[:, 2 * hidden : 3 * hidden], CONTRACT_FIRST).astype(BF16)
-    down_grad = dot(scaled_rows, full[:, :hidden], CONTRACT_FIRST).astype(BF16).T
+    matrix = shape((width, hidden), BF16)
+    gate_grad, up_grad, down_grad = kernel_call(
+        gradient_kernel,
+        (matrix, matrix, matrix),
+        700_000_000,
+        4_500_000,
+        spaces="svvvvvvv",
+        scratch=[full],
+    )(member, *pieces, token_rows, scaled_rows)
+    down_grad = down_grad.T
     token_shape = shape((width, token_count), BF16)
     mixed, input_gradient, route_gradient = kernel_call(
         combine_kernel,
-        (token_shape, token_shape, shape(routes_by_rank.shape, F32)),
+        (token_shape, token_shape, shape(arguments[0].shape, F32)),
         500_000_000,
         1_000_000,
-    )(returned, plan, routes_by_rank, weights_by_rank)
+    )(returned, plan, arguments[0], arguments[1])
     return (
         mixed.T,
         input_gradient.T,

time: 228 us -> 201 us (0.88)
  starting transfers between devices: 36.8 us -> 76.5 us
  waiting for transfers between devices: 92.5 us -> 56.8 us
  between operations: 14.1 us -> 0.89 us
  local copies, waits for them, and re-layouts: 12 us -> 2.41 us
  matrix products: 7.02 us -> 0 us
  blocking collectives: 54.7 us -> 50.2 us
  Pallas kernels: 10.3 us -> 13.9 us
    reduce_scatter x1 -> x0, waiting for transfers between devices: 65.4 us -> none  [per_device(): summed = lax.psum_scatter(part, 'expert', scatter_dimension=0, tiled=True)]
    ppermute x4 -> x8, starting transfers between devices: 14.3 us -> 45.4 us  [shifted(): lax.ppermute(block, 'expert', [(i, (i + distance) % parts) for i in range...]
    all_to_all x0 -> x1, starting transfers between devices: none -> 18.4 us  [per_device(): lax.all_to_all(send, 'dp', split_axis=0, concat_axis=0, tiled=True)]
    all_to_all x0 -> x1, waiting for transfers between devices: none -> 14.7 us  [per_device(): lax.all_to_all(send, 'dp', split_axis=0, concat_axis=0, tiled=True)]
    all_to_all x1, blocking collectives: 32.1 us -> 21.3 us  [per_device(): lax.all_to_all(window, 'expert', split_axis=0, concat_axis=0, tiled=True,...]
    ppermute x4 -> x8, waiting for transfers between devices: 19.5 us -> 29.6 us  [shifted(): lax.ppermute(block, 'expert', [(i, (i + distance) % parts) for i in range...]
    all_to_all x1, starting transfers between devices: 22.5 us -> 12.7 us  [per_device(): lax.all_to_all(back, 'dp', split_axis=0, concat_axis=0, tiled=True)]
    unnamed x36 -> x26, local copies, waits for them, and re-layouts: 10.5 us -> 2.36 us
  transfers between devices with their start and end apart: 6 -> 10, of which waited for: 5 -> 9; matrix products, arithmetic and copies ran while one was open for 4% -> 0% of each run, Pallas kernels for 0% -> 1%
where the time goes in v3:
time: 201 us
  starting transfers between devices  76.5 us (38%)
  waiting for transfers between devices  56.8 us (28%)
  blocking collectives  50.2 us (25%)
  Pallas kernels  13.9 us (7%)
  local copies, waits for them, and re-layouts  2.41 us (1%)
    ppermute x8, starting transfers between devices, shifted(): lax.ppermute(block, 'expert', [(i, (i + distance) % parts) for i in range...  45.4 us
    ppermute x8, waiting for transfers between devices, shifted(): lax.ppermute(block, 'expert', [(i, (i + distance) % parts) for i in range...  29.6 us
    all_gather x1, blocking collectives, per_device(): lax.all_gather(share, 'expert', axis=0, tiled=True, axis_index_groups=gro...  29 us
    all_to_all x1, blocking collectives, per_device(): lax.all_to_all(window, 'expert', split_axis=0, concat_axis=0, tiled=True,...  21.3 us
    all_to_all x1, starting transfers between devices, per_device(): lax.all_to_all(send, 'dp', split_axis=0, concat_axis=0, tiled=True)  18.4 us
    all_to_all x1, waiting for transfers between devices, per_device(): lax.all_to_all(send, 'dp', split_axis=0, concat_axis=0, tiled=True)  14.7 us
    all_to_all x1, starting transfers between devices, per_device(): lax.all_to_all(back, 'dp', split_axis=0, concat_axis=0, tiled=True)  12.7 us
    all_to_all x1, waiting for transfers between devices, per_device(): lax.all_to_all(back, 'dp', split_axis=0, concat_axis=0, tiled=True)  12.5 us
  transfers between devices with their start and end apart: 10, of which 9 were waited for; matrix products, arithmetic and copies ran while one was open for 0% of the time, Pallas kernels for 1%

profile of v3, /device:TPU:1, one launch (start us, length us, event | category | flops | bytes accessed | tf_op | source)
XLA Modules:
  0.0 200.7 jit_solution(4769965533751084769)
XLA Ops:
  0.7 0.7 copy-done.11
  1.3 0.8 copy-done.8
  2.2 0.8 copy-done.9
  3.0 2.4 %shard_map.127 = (bf16[64,24,128]{2,1,0:T(8,128)(2,1)}, f32[128,128]{1,0:T(8,128)S(1)}) custom-call(s32[8,128]{1,0:T(8,128)S(1)} %bitcast.31, f32[8,128]{1,0:T(8,128)S(1)} %bitcast.33, s32[1,64]{1,0:T(1,128)S(1)} %bitcast.35, bf16[224,128]{1,0:T(8,128)(2,1)S(1)} %bitcast.29, bf16[224,128]{1,0:T(8,128)(2,1)S(1)} %bitcast.30), custom_call_target="tpu_custom_call" | custom-call | flops 300000000 | bytes 1000000 | tf_op jit(solution)/shard_map/pallas_call | solution.py:389
  5.4 18.4 %all-to-all-start = ((bf16[64,24,128]{2,1,0:T(8,128)(2,1)}), bf16[64,24,128]{2,1,0:T(8,128)(2,1)S(1)}, u32[]{:S(2)}, u32[]{:S(2)}) async-start(bf16[64,24,128]{2,1,0:T(8,128)(2,1)} %get-tuple-element.23), calls=%async_computation | async-start | bytes 786432 | tf_op jit(solution)/shard_map/all_to_all | solution.py:397
  23.8 14.7 %all-to-all-done.recv_ref = bf16[64,24,128]{2,1,0:T(8,128)(2,1)S(1)} async-done(((bf16[64,24,128]{2,1,0:T(8,128)(2,1)}), bf16[64,24,128]{2,1,0:T(8,128)(2,1)S(1)}, u32[]{:S(2)}, u32[]{:S(2)}) %all-to-all-start) | async-done | bytes 393248 | tf_op jit(solution)/shard_map/all_to_all | solution.py:397
  38.5 2.4 %shard_map.128 = (bf16[96,3072]{1,0:T(8,128)(2,1)S(1)}, bf16[96,3072]{1,0:T(8,128)(2,1)S(1)}, bf16[96,3072]{1,0:T(8,128)(2,1)S(1)}, bf16[48,3072]{1,0:T(8,128)(2...) custom-call(s32[1]{0:T(128)} %bitcast.place_ref, ...), custom_call_target="tpu_custom_call" | custom-call | flops 700000000 | bytes 4500000 | tf_op jit(solution)/shard_map/pallas_call | solution.py:398
  40.9 1.9 collective-permute-start
  42.9 11.2 %collective-permute-start.1 = (bf16[96,3072]{1,0:T(8,128)(2,1)S(1)}, bf16[96,3072]{1,0:T(8,128)(2,1)S(1)}, u32[]{:S(2)}, u32[]{:S(2)}) collective-permute-start(bf16[96,3072]{1,0:T(8,128)(2,1)S(1)} %get-tuple-element.26), channel_id=1, source_target_pairs={{0,960},{64,0},{128,64},{192,128},{256,192},{320,256},{384,320},{4... | collective-permute-start | bytes 1769480 | tf_op jit(solution)/shard_map/ppermute | solution.py:369
  54.1 11.4 %collective-permute-done.from_left_ref = bf16[96,3072]{1,0:T(8,128)(2,1)S(1)} collective-permute-done((bf16[96,3072]{1,0:T(8,128)(2,1)S(1)}, bf16[96,3072]{1,0:T(8,128)(2,1)S(1)}, u32[]{:S(2)}, u32[]{:S(2)}) %collective-permute-start) | collective-permute-done | bytes 589856 | tf_op jit(solution)/shard_map/ppermute | solution.py:369
  65.5 0.9 collective-permute-done.1.from_right_ref
  66.4 0.1 shard_map.129
  66.6 1.9 collective-permute-start.2
  68.5 5.3 %collective-permute-start.3 = (bf16[48,3072]{1,0:T(8,128)(2,1)S(1)}, bf16[48,3072]{1,0:T(8,128)(2,1)S(1)}, u32[]{:S(2)}, u32[]{:S(2)}) collective-permute-start(bf16[48,3072]{1,0:T(8,128)(2,1)S(1)} %get-tuple-element.30), channel_id=1, source_target_pairs={{0,960},{64,0},{128,64},{192,128},{256,192},{320,256},{384,320},{4... | collective-permute-start | bytes 884744 | tf_op jit(solution)/shard_map/ppermute | solution.py:369
  73.8 4.2 %collective-permute-done.2.far_left_ref = bf16[48,3072]{1,0:T(8,128)(2,1)S(1)} collective-permute-done((bf16[48,3072]{1,0:T(8,128)(2,1)S(1)}, bf16[48,3072]{1,0:T(8,128)(2,1)S(1)}, u32[]{:S(2)}, u32[]{:S(2)}) %collective-permute-start.2) | collective-permute-done | bytes 294944 | tf_op jit(solution)/shard_map/ppermute | solution.py:369
  78.0 0.9 collective-permute-done.3.far_right_ref
  78.9 0.2 shard_map.130
  79.1 21.3 %all_to_all.21 = bf16[4,24,3072]{2,1,0:T(8,128)(2,1)S(1)} all-to-all(bf16[4,24,3072]{2,1,0:T(8,128)(2,1)S(1)} %bitcast.22), channel_id=1, replica_groups={{0,256,512,768},{64,320,576,832},{128,384,640,896},{192,448,704,960},{1..., dimensions={0} | all-to-all | bytes 1179648 | tf_op jit(solution)/shard_map/all_to_all | solution.py:414
  100.3 0.2 shard_map.131
  100.5 29.0 %all_gather.3.own_ref = bf16[96,3200]{1,0:T(8,128)(2,1)S(1)} all-gather(bf16[24,3200]{1,0:T(8,128)(2,1)S(1)} %shard_map.131), channel_id=1, replica_groups={{0,256,512,768},{64,320,576,832},{128,384,640,896},{192,448,704,960},{1..., dimensions={0}, use_global_device_ids=true | all-gather | bytes 768000 | tf_op jit(solution)/shard_map/all_gather | solution.py:420
  129.5 16.2 %collective-permute-start.4 = (bf16[96,3200]{1,0:T(8,128)(2,1)S(1)}, bf16[96,3200]{1,0:T(8,128)(2,1)S(1)}, u32[]{:S(2)}, u32[]{:S(2)}) collective-permute-start(bf16[96,3200]{1,0:T(8,128)(2,1)S(1)} %all_gather.3.own_ref), channel_id=1, source_target_pairs={{0,64},{64,128},{128,192},{192,256},{256,320},{320,384},{384,448},... | collective-permute-start | bytes 1843208 | tf_op jit(solution)/shard_map/ppermute | solution.py:369
  145.7 2.2 %collective-permute-start.5 = (bf16[96,3200]{1,0:T(8,128)(2,1)S(1)}, bf16[96,3200]{1,0:T(8,128)(2,1)S(1)}, u32[]{:S(2)}, u32[]{:S(2)}) collective-permute-start(bf16[96,3200]{1,0:T(8,128)(2,1)S(1)} %all_gather.3.own_ref), channel_id=1, source_target_pairs={{0,960},{64,0},{128,64},{192,128},{256,192},{320,256},{384,320},{4... | collective-permute-start | bytes 1843208 | tf_op jit(solution)/shard_map/ppermute | solution.py:369
  147.9 7.4 %collective-permute-done.4.left_ref = bf16[96,3200]{1,0:T(8,128)(2,1)S(1)} collective-permute-done((bf16[96,3200]{1,0:T(8,128)(2,1)S(1)}, bf16[96,3200]{1,0:T(8,128)(2,1)S(1)}, u32[]{:S(2)}, u32[]{:S(2)}) %collective-permute-start.4) | collective-permute-done | bytes 614432 | tf_op jit(solution)/shard_map/ppermute | solution.py:369
  155.3 3.9 %collective-permute-start.6 = (bf16[48,3200]{1,0:T(8,128)(2,1)S(1)}, bf16[48,3200]{1,0:T(8,128)(2,1)S(1)}, u32[]{:S(2)}, u32[]{:S(2)}) collective-permute-start(bf16[48,3200]{1,0:T(8,128)(2,1)S(1)} %slice.8), channel_id=1, source_target_pairs={{0,64},{64,128},{128,192},{192,256},{256,320},{320,384},{384,448},... | collective-permute-start | bytes 921608 | tf_op jit(solution)/shard_map/ppermute | solution.py:369
  159.3 2.7 %collective-permute-start.7 = (bf16[48,3200]{1,0:T(8,128)(2,1)S(1)}, bf16[48,3200]{1,0:T(8,128)(2,1)S(1)}, u32[]{:S(2)}, u32[]{:S(2)}) collective-permute-start(bf16[48,3200]{1,0:T(8,128)(2,1)S(1)} %slice.9), channel_id=1, source_target_pairs={{0,960},{64,0},{128,64},{192,128},{256,192},{320,256},{384,320},{4... | collective-permute-start | bytes 921608 | tf_op jit(solution)/shard_map/ppermute | solution.py:369
  162.0 2.3 %collective-permute-done.6.far_left_ref = bf16[48,3200]{1,0:T(8,128)(2,1)S(1)} collective-permute-done((bf16[48,3200]{1,0:T(8,128)(2,1)S(1)}, bf16[48,3200]{1,0:T(8,128)(2,1)S(1)}, u32[]{:S(2)}, u32[]{:S(2)}) %collective-permute-start.6) | collective-permute-done | bytes 307232 | tf_op jit(solution)/shard_map/ppermute | solution.py:369
  164.3 2.6 %collective-permute-done.7.far_right_ref = bf16[48,3200]{1,0:T(8,128)(2,1)S(1)} collective-permute-done((bf16[48,3200]{1,0:T(8,128)(2,1)S(1)}, bf16[48,3200]{1,0:T(8,128)(2,1)S(1)}, u32[]{:S(2)}, u32[]{:S(2)}) %collective-permute-start.7) | collective-permute-done | bytes 307232 | tf_op jit(solution)/shard_map/ppermute | solution.py:369
  166.9 3.3 %shard_map.132 = bf16[64,24,128]{2,1,0:T(8,128)(2,1)} custom-call(s32[1]{0:T(128)} %bitcast.place_ref, bf16[96,3200]{1,0:T(8,128)(2,1)S(1)} %all_gather.3.own_ref, bf16[96,3200]{1,0:T(8,128)(2,1)S(1)} %collective-permute-done.4.left_ref, bf16[96,3200]{1,0:T(8,128)(2,1)S(1)} %collective-permute-done.5.right_ref, ...), custom_call_target="tpu_custom_call" | custom-call | flops 700000000 | bytes 4500000 | tf_op jit(solution)/shard_map/pallas_call | solution.py:425
  170.3 12.7 %all-to-all-start.2 = ((bf16[64,24,128]{2,1,0:T(8,128)(2,1)}), bf16[64,24,128]{2,1,0:T(8,128)(2,1)S(1)}, u32[]{:S(2)}, u32[]{:S(2)}) async-start(bf16[64,24,128]{2,1,0:T(8,128)(2,1)} %shard_map.132), calls=%async_computation.2 | async-start | bytes 786432 | tf_op jit(solution)/shard_map/all_to_all | solution.py:433
  183.0 2.1 %shard_map.134 = (bf16[224,1024]{1,0:T(8,128)(2,1)}, bf16[224,1024]{1,0:T(8,128)(2,1)}, bf16[224,1024]{1,0:T(8,128)(2,1)}) custom-call(s32[1]{0:T(128)} %bitcast.place_ref, bf16[96,3200]{1,0:T(8,128)(2,1)S(1)} %all_gather.3.own_ref, bf16[96,3200]{1,0:T(8,128)(2,1)S(1)} %collective-permute-done.4.left_ref, ...), custom_call_target="tpu_custom_call" | custom-call | flops 700000000 | bytes 4500000 | tf_op jit(solution)/shard_map/pallas_call | solution.py:435
  185.0 12.5 %all-to-all-done.2.back_ref = bf16[64,24,128]{2,1,0:T(8,128)(2,1)S(1)} async-done(((bf16[64,24,128]{2,1,0:T(8,128)(2,1)}), bf16[64,24,128]{2,1,0:T(8,128)(2,1)S(1)}, u32[]{:S(2)}, u32[]{:S(2)}) %all-to-all-start.2) | async-done | bytes 393248 | tf_op jit(solution)/shard_map/all_to_all | solution.py:433
  197.6 3.2 %shard_map.133 = (bf16[224,128]{1,0:T(8,128)(2,1)}, bf16[224,128]{1,0:T(8,128)(2,1)}, f32[8,128]{1,0:T(8,128)}) custom-call(bf16[64,24,128]{2,1,0:T(8,128)(2,1)S(1)} %all-to-all-done.2.back_ref, f32[128,128]{1,0:T(8,128)S(1)} %get-tuple-element.31.plan_ref, s32[8,128]{1,0:T(8,128)S(1)} %bitcast.32, f32[8,128]{1,0:T(8,128)S(1)} %bitcast.34), custom_call_target="tpu_custom_call" | custom-call | flops 500000000 | bytes 1000000 | tf_op jit(solution)/shard_map/pallas_call | solution.py:445
  (26 shorter events, 0.1 us)
Async XLA Ops:
  0.6 0.7 copy-start.11
  0.6 0.7 copy-start.10
  0.7 0.7 copy-start.12
  1.3 0.8 copy-start.8
  2.2 0.8 copy-start.9
  3.0 35.5 %copy-start.1 = (bf16[1,224,1024]{2,1,0:T(8,128)(2,1)S(1)}, bf16[1,224,1024]{2,1,0:T(8,128)(2,1)}, u32[]{:S(2)}) copy-start(bf16[1,224,1024]{2,1,0:T(8,128)(2,1)} %param.14) | copy-start | bytes 1376260
  3.0 35.5 %copy-start.2 = (bf16[1,1024,224]{1,2,0:T(8,128)(2,1)S(1)}, bf16[1,1024,224]{1,2,0:T(8,128)(2,1)}, u32[]{:S(2)}) copy-start(bf16[1,1024,224]{1,2,0:T(8,128)(2,1)} %param.15) | copy-start | bytes 1376260
  5.4 33.1 %copy-start = (bf16[1,224,1024]{2,1,0:T(8,128)(2,1)S(1)}, bf16[1,224,1024]{2,1,0:T(8,128)(2,1)}, u32[]{:S(2)}) copy-start(bf16[1,224,1024]{2,1,0:T(8,128)(2,1)} %param.13) | copy-start | bytes 1376260
  5.4 33.1 %all-to-all-start = ((bf16[64,24,128]{2,1,0:T(8,128)(2,1)}), bf16[64,24,128]{2,1,0:T(8,128)(2,1)S(1)}, u32[]{:S(2)}, u32[]{:S(2)}) async-start(bf16[64,24,128]{2,1,0:T(8,128)(2,1)} %get-tuple-element.23), calls=%async_computation | async-start | bytes 786432 | tf_op jit(solution)/shard_map/all_to_all | solution.py:397
  40.9 25.6 %copy-start.4 = (bf16[384,224]{1,0:T(8,128)(2,1)}, bf16[384,224]{1,0:T(8,128)(2,1)S(1)}, u32[]{:S(2)}) copy-start(bf16[384,224]{1,0:T(8,128)(2,1)S(1)} %get-tuple-element.35.tok_ref) | copy-start | bytes 516100
  40.9 25.6 %copy-start.6 = (bf16[384,224]{1,0:T(8,128)(2,1)}, bf16[384,224]{1,0:T(8,128)(2,1)S(1)}, u32[]{:S(2)}) copy-start(bf16[384,224]{1,0:T(8,128)(2,1)S(1)} %get-tuple-element.36.scaled_ref) | copy-start | bytes 516100
  40.9 24.6 %collective-permute-start = (bf16[96,3072]{1,0:T(8,128)(2,1)S(1)}, bf16[96,3072]{1,0:T(8,128)(2,1)S(1)}, u32[]{:S(2)}, u32[]{:S(2)}) collective-permute-start(bf16[96,3072]{1,0:T(8,128)(2,1)S(1)} %get-tuple-element.25), channel_id=1, source_target_pairs={{0,64},{64,128},{128,192},{192,256},{256,320},{320,384},{384,448},... | collective-permute-start | bytes 1769480 | tf_op jit(solution)/shard_map/ppermute | solution.py:369
  42.9 23.5 %collective-permute-start.1 = (bf16[96,3072]{1,0:T(8,128)(2,1)S(1)}, bf16[96,3072]{1,0:T(8,128)(2,1)S(1)}, u32[]{:S(2)}, u32[]{:S(2)}) collective-permute-start(bf16[96,3072]{1,0:T(8,128)(2,1)S(1)} %get-tuple-element.26), channel_id=1, source_target_pairs={{0,960},{64,0},{128,64},{192,128},{256,192},{320,256},{384,320},{4... | collective-permute-start | bytes 1769480 | tf_op jit(solution)/shard_map/ppermute | solution.py:369
  66.6 11.4 %collective-permute-start.2 = (bf16[48,3072]{1,0:T(8,128)(2,1)S(1)}, bf16[48,3072]{1,0:T(8,128)(2,1)S(1)}, u32[]{:S(2)}, u32[]{:S(2)}) collective-permute-start(bf16[48,3072]{1,0:T(8,128)(2,1)S(1)} %get-tuple-element.29), channel_id=1, source_target_pairs={{0,64},{64,128},{128,192},{192,256},{256,320},{320,384},{384,448},... | collective-permute-start | bytes 884744 | tf_op jit(solution)/shard_map/ppermute | solution.py:369
  68.5 10.4 %collective-permute-start.3 = (bf16[48,3072]{1,0:T(8,128)(2,1)S(1)}, bf16[48,3072]{1,0:T(8,128)(2,1)S(1)}, u32[]{:S(2)}, u32[]{:S(2)}) collective-permute-start(bf16[48,3072]{1,0:T(8,128)(2,1)S(1)} %get-tuple-element.30), channel_id=1, source_target_pairs={{0,960},{64,0},{128,64},{192,128},{256,192},{320,256},{384,320},{4... | collective-permute-start | bytes 884744 | tf_op jit(solution)/shard_map/ppermute | solution.py:369
  129.5 25.8 %collective-permute-start.4 = (bf16[96,3200]{1,0:T(8,128)(2,1)S(1)}, bf16[96,3200]{1,0:T(8,128)(2,1)S(1)}, u32[]{:S(2)}, u32[]{:S(2)}) collective-permute-start(bf16[96,3200]{1,0:T(8,128)(2,1)S(1)} %all_gather.3.own_ref), channel_id=1, source_target_pairs={{0,64},{64,128},{128,192},{192,256},{256,320},{320,384},{384,448},... | collective-permute-start | bytes 1843208 | tf_op jit(solution)/shard_map/ppermute | solution.py:369
  145.7 13.6 %collective-permute-start.5 = (bf16[96,3200]{1,0:T(8,128)(2,1)S(1)}, bf16[96,3200]{1,0:T(8,128)(2,1)S(1)}, u32[]{:S(2)}, u32[]{:S(2)}) collective-permute-start(bf16[96,3200]{1,0:T(8,128)(2,1)S(1)} %all_gather.3.own_ref), channel_id=1, source_target_pairs={{0,960},{64,0},{128,64},{192,128},{256,192},{320,256},{384,320},{4... | collective-permute-start | bytes 1843208 | tf_op jit(solution)/shard_map/ppermute | solution.py:369
  155.3 11.6 %copy-start.3 = (bf16[1,1024,224]{1,2,0:T(8,128)(2,1)S(1)}, bf16[1,1024,224]{1,2,0:T(8,128)(2,1)}, u32[]{:S(2)}) copy-start(bf16[1,1024,224]{1,2,0:T(8,128)(2,1)} %param.15) | copy-start | bytes 1376260
  155.3 8.9 %collective-permute-start.6 = (bf16[48,3200]{1,0:T(8,128)(2,1)S(1)}, bf16[48,3200]{1,0:T(8,128)(2,1)S(1)}, u32[]{:S(2)}, u32[]{:S(2)}) collective-permute-start(bf16[48,3200]{1,0:T(8,128)(2,1)S(1)} %slice.8), channel_id=1, source_target_pairs={{0,64},{64,128},{128,192},{192,256},{256,320},{320,384},{384,448},... | collective-permute-start | bytes 921608 | tf_op jit(solution)/shard_map/ppermute | solution.py:369
  159.3 7.6 %collective-permute-start.7 = (bf16[48,3200]{1,0:T(8,128)(2,1)S(1)}, bf16[48,3200]{1,0:T(8,128)(2,1)S(1)}, u32[]{:S(2)}, u32[]{:S(2)}) collective-permute-start(bf16[48,3200]{1,0:T(8,128)(2,1)S(1)} %slice.9), channel_id=1, source_target_pairs={{0,960},{64,0},{128,64},{192,128},{256,192},{320,256},{384,320},{4... | collective-permute-start | bytes 921608 | tf_op jit(solution)/shard_map/ppermute | solution.py:369
  170.3 12.7 %copy-start.5 = (bf16[384,224]{1,0:T(8,128)(2,1)S(1)}, bf16[384,224]{1,0:T(8,128)(2,1)}, u32[]{:S(2)}) copy-start(bf16[384,224]{1,0:T(8,128)(2,1)} %copy-done.4) | copy-start | bytes 516100
  170.3 12.7 %copy-start.7 = (bf16[384,224]{1,0:T(8,128)(2,1)S(1)}, bf16[384,224]{1,0:T(8,128)(2,1)}, u32[]{:S(2)}) copy-start(bf16[384,224]{1,0:T(8,128)(2,1)} %copy-done.6) | copy-start | bytes 516100
  170.3 27.3 %all-to-all-start.2 = ((bf16[64,24,128]{2,1,0:T(8,128)(2,1)}), bf16[64,24,128]{2,1,0:T(8,128)(2,1)S(1)}, u32[]{:S(2)}, u32[]{:S(2)}) async-start(bf16[64,24,128]{2,1,0:T(8,128)(2,1)} %shard_map.132), calls=%async_computation.2 | async-start | bytes 786432 | tf_op jit(solution)/shard_map/all_to_all | solution.py:433

commit v4 on v3

--- a/solution.py
+++ b/solution.py
@@ -14,6 +14,7 @@
 RING = 4
 SCORE_LANE = 96
 VMEM_LIMIT = 24 * 1024 * 1024
+WHOLE_VMEM = 63 * 1024 * 1024
 
 F32 = jnp.float32
 BF16 = jnp.bfloat16
@@ -188,25 +189,71 @@
     to_left_ref[...] = (previous_ref[...].astype(F32) + from_right_ref[half:].astype(F32)).astype(BF16)
 
 
-def window_kernel(own_ref, from_left_ref, from_right_ref, far_left_ref, far_right_ref, out_ref):
+def window_kernel(
+    place_ref,
+    own_ref,
+    from_left_ref,
+    from_right_ref,
+    far_left_ref,
+    far_right_ref,
+    kept_ref,
+    to_right_ref,
+    to_left_ref,
+    next_ref,
+    previous_ref,
+    window_ref,
+):
     half = far_left_ref.shape[0]
-    out_ref[:half] = (
+    window_ref[:half] = (
         own_ref[:half].astype(F32) + from_right_ref[:half].astype(F32) + far_left_ref[...].astype(F32)
+    )
+    window_ref[half:] = (
+        own_ref[half:].astype(F32) + from_left_ref[half:].astype(F32) + far_right_ref[...].astype(F32)
+    )
+    share, columns = kept_ref.shape
+    split = columns // 2
+
+    def chunk(step, part):
+        member = (lax.shift_right_logical(place_ref[0], 2) + step) & (RING - 1)
+        begin = pl.multiple_of(member * share, share)
+        return window_ref[pl.ds(begin, share), part].astype(BF16)
+
+    low, high = slice(0, split), slice(split, columns)
+    kept_ref[...] = chunk(0, slice(0, columns))
+    to_right_ref[:, low] = chunk(RING // 2, low)
+    to_right_ref[:, high] = chunk(1, high)
+    to_left_ref[:, low] = chunk(RING - 1, low)
+    to_left_ref[:, high] = chunk(RING // 2, high)
+    next_ref[...] = chunk(1, low)
+    previous_ref[...] = chunk(RING - 1, high)
+
+
+def second_relay_kernel(
+    next_ref, previous_ref, from_left_ref, from_right_ref, to_right_ref, to_left_ref
+):
+    split = next_ref.shape[1]
+    to_right_ref[...] = (next_ref[...].astype(F32) + from_left_ref[:, :split].astype(F32)).astype(BF16)
+    to_left_ref[...] = (
+        previous_ref[...].astype(F32) + from_right_ref[:, split:].astype(F32)
     ).astype(BF16)
-    out_ref[half:] = (
-        own_ref[half:].astype(F32) + from_left_ref[half:].astype(F32) + far_right_ref[...].astype(F32)
-    ).astype(BF16)
-
-
-def middle_kernel(sum_ref, out_ref):
-    hidden = sum_ref.shape[1] // 3
-    share = out_ref.shape[0]
-
-    def summed(index):
-        values = sum_ref[:, index * hidden : (index + 1) * hidden].astype(F32)
-        return sum(values[i * share : (i + 1) * share] for i in range(sum_ref.shape[0] // share))
-
-    gate, up, grad = summed(0), summed(1), summed(2)
+
+
+def middle_kernel(
+    kept_ref, from_left_ref, from_right_ref, far_left_ref, far_right_ref, out_ref, sum_ref
+):
+    hidden = kept_ref.shape[1] // 3
+    split = far_left_ref.shape[1]
+    sum_ref[:, :split] = (
+        kept_ref[:, :split].astype(F32)
+        + from_right_ref[:, :split].astype(F32)
+        + far_left_ref[...].astype(F32)
+    )
+    sum_ref[:, split:] = (
+        kept_ref[:, split:].astype(F32)
+        + from_left_ref[:, split:].astype(F32)
+        + far_right_ref[...].astype(F32)
+    )
+    gate, up, grad = (sum_ref[:, i * hidden : (i + 1) * hidden] for i in range(3))
     sigmoid = jax.nn.sigmoid(gate)
     gated = gate * sigmoid
     hidden_value = (gated * up).astype(BF16)
@@ -343,16 +390,16 @@
         score_ref[k : k + 1] = value / weight_ref[k : k + 1]
 
 
-def kernel_call(body, out_shape, flops, moved, spaces=None, scratch=()):
+def kernel_call(body, out_shape, flops, moved, spaces=None, scratch=(), limit=VMEM_LIMIT):
     places = {}
     if spaces is not None:
-        kinds = {"s": pltpu.SMEM, "v": pltpu.VMEM, "a": pl.ANY}
+        kinds = {"s": pltpu.SMEM, "v": pltpu.VMEM, "h": pltpu.HBM}
         places["in_specs"] = [pl.BlockSpec(memory_space=kinds[kind]) for kind in spaces]
     return pl.pallas_call(
         body,
         out_shape=out_shape,
         scratch_shapes=scratch,
-        compiler_params=pltpu.CompilerParams(vmem_limit_bytes=VMEM_LIMIT),
+        compiler_params=pltpu.CompilerParams(vmem_limit_bytes=limit),
         cost_estimate=pl.CostEstimate(flops=flops, bytes_accessed=moved, transcendentals=0),
         **places,
     )
@@ -383,7 +430,7 @@
     rows = shape((row_count, width), BF16)
     whole, halved = (shape((size, 3 * hidden), BF16) for size in (held, held // 2))
     groups = [list(range(i, parts, RING)) for i in range(RING)]
-    member = (lax.axis_index("expert") % RING).astype(jnp.int32).reshape(1)
+    member = lax.axis_index("expert").astype(jnp.int32).reshape(1)
     weights = (gate_weight[0], up_weight[0], down_weight[0].T)
     arguments = (routes.T, route_weights.T, owner_slots.reshape(1, experts), tokens.T, cotangent.T)
     send, plan = kernel_call(
@@ -391,7 +438,8 @@
         (exchanged, shape((2 * experts, token_count), F32)),
         300_000_000,
         1_000_000,
-        spaces="aaaaa",
+        spaces="hhhhh",
+        limit=WHOLE_VMEM,
         scratch=held_copies(*arguments),
     )(*arguments)
     arrived = lax.all_to_all(send, "dp", split_axis=0, concat_axis=0, tiled=True)
@@ -400,7 +448,7 @@
         (whole, whole, whole, halved, halved, rows, rows),
         700_000_000,
         4_500_000,
-        spaces="svaaa",
+        spaces="svhhh",
         scratch=held_copies(*weights),
     )(member, arrived, *weights)
     from_left, from_right = shifted(to_right, 1), shifted(to_left, -1)
@@ -408,15 +456,29 @@
         following, previous, from_left, from_right
     )
     far_left, far_right = shifted(relay_right, 1), shifted(relay_left, -1)
-    window = kernel_call(window_kernel, whole, 600_000, 2_000_000)(
-        own, from_left, from_right, far_left, far_right
-    )
-    summands = lax.all_to_all(
-        window, "expert", split_axis=0, concat_axis=0, tiled=True, axis_index_groups=groups
-    )
+    chunk, chunk_half = (
+        shape((row_count // parts, columns), BF16) for columns in (3 * hidden, 3 * hidden // 2)
+    )
+    kept, to_right, to_left, following, previous = kernel_call(
+        window_kernel,
+        (chunk, chunk, chunk, chunk_half, chunk_half),
+        600_000,
+        2_000_000,
+        spaces="svvvvv",
+        scratch=[pltpu.VMEM(whole.shape, F32)],
+    )(member, own, from_left, from_right, far_left, far_right)
+    from_left, from_right = shifted(to_right, RING), shifted(to_left, -RING)
+    relay_right, relay_left = kernel_call(
+        second_relay_kernel, (chunk_half, chunk_half), 100_000, 400_000
+    )(following, previous, from_left, from_right)
+    far_left, far_right = shifted(relay_right, RING), shifted(relay_left, -RING)
     share = kernel_call(
-        middle_kernel, shape((row_count // parts, 3 * hidden + LANES), BF16), 1_000_000, 700_000
-    )(summands)
+        middle_kernel,
+        shape((row_count // parts, 3 * hidden + LANES), BF16),
+        1_000_000,
+        700_000,
+        scratch=[pltpu.VMEM(chunk.shape, F32)],
+    )(kept, from_left, from_right, far_left, far_right)
     own = lax.all_gather(share, "expert", axis=0, tiled=True, axis_index_groups=groups)
     half = held // 2
     left, right = shifted(own, 1), shifted(own, -1)
@@ -427,7 +489,7 @@
         exchanged,
         700_000_000,
         4_500_000,
-        spaces="svvvvvaaa",
+        spaces="svvvvvhhh",
         scratch=[full, pltpu.VMEM((TILES, row_count, LANES), F32)] + held_copies(*weights),
     )(member, *pieces, *weights)
     returned = lax.all_to_all(back, "dp", split_axis=0, concat_axis=0, tiled=True)

time: 201 us -> 206 us (1.025)
  blocking collectives: 50.2 us -> 26.6 us
  starting transfers between devices: 76.5 us -> 92.3 us
  waiting for transfers between devices: 56.8 us -> 67.8 us
    all_to_all x1 -> x0, blocking collectives: 21.3 us -> none  [per_device(): lax.all_to_all(window, 'expert', split_axis=0, concat_axis=0, tiled=True,...]
    ppermute x8 -> x12, starting transfers between devices: 45.4 us -> 62.8 us  [shifted(): lax.ppermute(block, 'expert', [(i, (i + distance) % parts) for i in range...]
    ppermute x8 -> x12, waiting for transfers between devices: 29.6 us -> 40.6 us  [shifted(): lax.ppermute(block, 'expert', [(i, (i + distance) % parts) for i in range...]
    all_gather x1, blocking collectives: 29 us -> 26.6 us  [per_device(): lax.all_gather(share, 'expert', axis=0, tiled=True, axis_index_groups=gro...]
  transfers between devices with their start and end apart: 10 -> 14, of which waited for: 9 -> 14; matrix products, arithmetic and copies ran while one was open for 0% -> 0% of each run, Pallas kernels for 1% -> 1%
where the time goes in v4:
time: 206 us; the launch traced here: 205 us
  starting transfers between devices  92.3 us (45%)
  waiting for transfers between devices  67.8 us (33%)
  blocking collectives  26.6 us (13%)
  Pallas kernels  14.9 us (7%)
  local copies, waits for them, and re-layouts  2.46 us (1%)
    ppermute x12, starting transfers between devices, shifted(): lax.ppermute(block, 'expert', [(i, (i + distance) % parts) for i in range...  62.8 us
    ppermute x12, waiting for transfers between devices, shifted(): lax.ppermute(block, 'expert', [(i, (i + distance) % parts) for i in range...  40.6 us
    all_gather x1, blocking collectives, per_device(): lax.all_gather(share, 'expert', axis=0, tiled=True, axis_index_groups=gro...  26.6 us
    all_to_all x1, starting transfers between devices, per_device(): lax.all_to_all(send, 'dp', split_axis=0, concat_axis=0, tiled=True)  18.4 us
    all_to_all x1, waiting for transfers between devices, per_device(): lax.all_to_all(send, 'dp', split_axis=0, concat_axis=0, tiled=True)  14.7 us
    all_to_all x1, waiting for transfers between devices, per_device(): lax.all_to_all(back, 'dp', split_axis=0, concat_axis=0, tiled=True)  12.5 us
    all_to_all x1, starting transfers between devices, per_device(): lax.all_to_all(back, 'dp', split_axis=0, concat_axis=0, tiled=True)  11.2 us
  transfers between devices with their start and end apart: 14, of which 14 were waited for; matrix products, arithmetic and copies ran while one was open for 0% of the time, Pallas kernels for 1%

profile of v4, /device:TPU:1, one launch (start us, length us, event | category | flops | bytes accessed | tf_op | source)
XLA Modules:
  0.0 205.0 jit_solution(13654255909662806063)
XLA Ops:
  0.6 3.2 %shard_map.127 = (bf16[64,24,128]{2,1,0:T(8,128)(2,1)}, f32[128,128]{1,0:T(8,128)}) custom-call(s32[8,128]{1,0:T(8,128)} %bitcast.25, f32[8,128]{1,0:T(8,128)} %bitcast.27, s32[1,64]{1,0:T(1,128)} %bitcast.34, bf16[224,128]{1,0:T(8,128)(2,1)} %bitcast.32, bf16[224,128]{1,0:T(8,128)(2,1)} %bitcast.33), custom_call_target="tpu_custom_call" | custom-call | flops 300000000 | bytes 1000000 | tf_op jit(solution)/shard_map/pallas_call | solution.py:436
  3.9 18.4 %all-to-all-start = ((bf16[64,24,128]{2,1,0:T(8,128)(2,1)}), bf16[64,24,128]{2,1,0:T(8,128)(2,1)S(1)}, u32[]{:S(2)}, u32[]{:S(2)}) async-start(bf16[64,24,128]{2,1,0:T(8,128)(2,1)} %get-tuple-element.30), calls=%async_computation | async-start | bytes 786432 | tf_op jit(solution)/shard_map/all_to_all | solution.py:445
  22.2 14.7 %all-to-all-done.recv_ref = bf16[64,24,128]{2,1,0:T(8,128)(2,1)S(1)} async-done(((bf16[64,24,128]{2,1,0:T(8,128)(2,1)}), bf16[64,24,128]{2,1,0:T(8,128)(2,1)S(1)}, u32[]{:S(2)}, u32[]{:S(2)}) %all-to-all-start) | async-done | bytes 393248 | tf_op jit(solution)/shard_map/all_to_all | solution.py:445
  37.0 1.0 copy-done.2
  38.0 2.4 %shard_map.128 = (bf16[96,3072]{1,0:T(8,128)(2,1)S(1)}, bf16[96,3072]{1,0:T(8,128)(2,1)S(1)}, bf16[96,3072]{1,0:T(8,128)(2,1)S(1)}, bf16[48,3072]{1,0:T(8,128)(2...) custom-call(s32[1]{0:T(128)} %bitcast.place_ref, ...), custom_call_target="tpu_custom_call" | custom-call | flops 700000000 | bytes 4500000 | tf_op jit(solution)/shard_map/pallas_call | solution.py:446
  41.7 1.9 collective-permute-start
  43.6 11.2 %collective-permute-start.1 = (bf16[96,3072]{1,0:T(8,128)(2,1)S(1)}, bf16[96,3072]{1,0:T(8,128)(2,1)S(1)}, u32[]{:S(2)}, u32[]{:S(2)}) collective-permute-start(bf16[96,3072]{1,0:T(8,128)(2,1)S(1)} %get-tuple-element.33), channel_id=1, source_target_pairs={{0,960},{64,0},{128,64},{192,128},{256,192},{320,256},{384,320},{4... | collective-permute-start | bytes 1769480 | tf_op jit(solution)/shard_map/ppermute | solution.py:416
  54.9 11.4 %collective-permute-done.from_left_ref = bf16[96,3072]{1,0:T(8,128)(2,1)S(1)} collective-permute-done((bf16[96,3072]{1,0:T(8,128)(2,1)S(1)}, bf16[96,3072]{1,0:T(8,128)(2,1)S(1)}, u32[]{:S(2)}, u32[]{:S(2)}) %collective-permute-start) | collective-permute-done | bytes 589856 | tf_op jit(solution)/shard_map/ppermute | solution.py:416
  67.3 1.9 collective-permute-start.2
  69.2 5.3 %collective-permute-start.3 = (bf16[48,3072]{1,0:T(8,128)(2,1)S(1)}, bf16[48,3072]{1,0:T(8,128)(2,1)S(1)}, u32[]{:S(2)}, u32[]{:S(2)}) collective-permute-start(bf16[48,3072]{1,0:T(8,128)(2,1)S(1)} %get-tuple-element.37), channel_id=1, source_target_pairs={{0,960},{64,0},{128,64},{192,128},{256,192},{320,256},{384,320},{4... | collective-permute-start | bytes 884744 | tf_op jit(solution)/shard_map/ppermute | solution.py:416
  74.6 4.1 %collective-permute-done.2.far_left_ref = bf16[48,3072]{1,0:T(8,128)(2,1)S(1)} collective-permute-done((bf16[48,3072]{1,0:T(8,128)(2,1)S(1)}, bf16[48,3072]{1,0:T(8,128)(2,1)S(1)}, u32[]{:S(2)}, u32[]{:S(2)}) %collective-permute-start.2) | collective-permute-done | bytes 294944 | tf_op jit(solution)/shard_map/ppermute | solution.py:416
  78.7 0.9 collective-permute-done.3.far_right_ref
  80.0 2.2 %collective-permute-start.4 = (bf16[24,3072]{1,0:T(8,128)(2,1)S(1)}, bf16[24,3072]{1,0:T(8,128)(2,1)S(1)}, u32[]{:S(2)}, u32[]{:S(2)}) collective-permute-start(bf16[24,3072]{1,0:T(8,128)(2,1)S(1)} %get-tuple-element.39), channel_id=1, source_target_pairs={{0,256},{64,320},{128,384},{192,448},{256,512},{320,576},{384,640}... | collective-permute-start | bytes 442376 | tf_op jit(solution)/shard_map/ppermute | solution.py:416
  82.3 6.9 %collective-permute-start.5 = (bf16[24,3072]{1,0:T(8,128)(2,1)S(1)}, bf16[24,3072]{1,0:T(8,128)(2,1)S(1)}, u32[]{:S(2)}, u32[]{:S(2)}) collective-permute-start(bf16[24,3072]{1,0:T(8,128)(2,1)S(1)} %get-tuple-element.40), channel_id=1, source_target_pairs={{0,768},{64,832},{128,896},{192,960},{256,0},{320,64},{384,128},{4... | collective-permute-start | bytes 442376 | tf_op jit(solution)/shard_map/ppermute | solution.py:416
  90.1 2.3 %collective-permute-done.5.from_right_ref = bf16[24,3072]{1,0:T(8,128)(2,1)S(1)} collective-permute-done((bf16[24,3072]{1,0:T(8,128)(2,1)S(1)}, bf16[24,3072]{1,0:T(8,128)(2,1)S(1)}, u32[]{:S(2)}, u32[]{:S(2)}) %collective-permute-start.5) | collective-permute-done | bytes 147488 | tf_op jit(solution)/shard_map/ppermute | solution.py:416
  92.4 5.5 %collective-permute-start.6 = (bf16[24,1536]{1,0:T(8,128)(2,1)S(1)}, bf16[24,1536]{1,0:T(8,128)(2,1)S(1)}, u32[]{:S(2)}, u32[]{:S(2)}) collective-permute-start(bf16[24,1536]{1,0:T(8,128)(2,1)S(1)} %get-tuple-element.43), channel_id=1, source_target_pairs={{0,256},{64,320},{128,384},{192,448},{256,512},{320,576},{384,640}... | collective-permute-start | bytes 221192 | tf_op jit(solution)/shard_map/ppermute | solution.py:416
  97.9 3.8 %collective-permute-start.7 = (bf16[24,1536]{1,0:T(8,128)(2,1)S(1)}, bf16[24,1536]{1,0:T(8,128)(2,1)S(1)}, u32[]{:S(2)}, u32[]{:S(2)}) collective-permute-start(bf16[24,1536]{1,0:T(8,128)(2,1)S(1)} %get-tuple-element.44), channel_id=1, source_target_pairs={{0,768},{64,832},{128,896},{192,960},{256,0},{320,64},{384,128},{4... | collective-permute-start | bytes 221192 | tf_op jit(solution)/shard_map/ppermute | solution.py:416
  101.6 2.2 %collective-permute-done.6.far_left_ref = bf16[24,1536]{1,0:T(8,128)(2,1)S(1)} collective-permute-done((bf16[24,1536]{1,0:T(8,128)(2,1)S(1)}, bf16[24,1536]{1,0:T(8,128)(2,1)S(1)}, u32[]{:S(2)}, u32[]{:S(2)}) %collective-permute-start.6) | collective-permute-done | bytes 73760 | tf_op jit(solution)/shard_map/ppermute | solution.py:416
  103.8 3.9 %collective-permute-done.7.far_right_ref = bf16[24,1536]{1,0:T(8,128)(2,1)S(1)} collective-permute-done((bf16[24,1536]{1,0:T(8,128)(2,1)S(1)}, bf16[24,1536]{1,0:T(8,128)(2,1)S(1)}, u32[]{:S(2)}, u32[]{:S(2)}) %collective-permute-start.7) | collective-permute-done | bytes 73760 | tf_op jit(solution)/shard_map/ppermute | solution.py:416
  107.9 26.6 %all_gather.3.own_ref = bf16[96,3200]{1,0:T(8,128)(2,1)S(1)} all-gather(bf16[24,3200]{1,0:T(8,128)(2,1)S(1)} %shard_map.132), channel_id=1, replica_groups={{0,256,512,768},{64,320,576,832},{128,384,640,896},{192,448,704,960},{1..., dimensions={0}, use_global_device_ids=true | all-gather | bytes 768000 | tf_op jit(solution)/shard_map/all_gather | solution.py:482
  134.5 4.9 %collective-permute-start.8 = (bf16[96,3200]{1,0:T(8,128)(2,1)S(1)}, bf16[96,3200]{1,0:T(8,128)(2,1)S(1)}, u32[]{:S(2)}, u32[]{:S(2)}) collective-permute-start(bf16[96,3200]{1,0:T(8,128)(2,1)S(1)} %all_gather.3.own_ref), channel_id=1, source_target_pairs={{0,64},{64,128},{128,192},{192,256},{256,320},{320,384},{384,448},... | collective-permute-start | bytes 1843208 | tf_op jit(solution)/shard_map/ppermute | solution.py:416
  139.5 7.5 %collective-permute-start.9 = (bf16[96,3200]{1,0:T(8,128)(2,1)S(1)}, bf16[96,3200]{1,0:T(8,128)(2,1)S(1)}, u32[]{:S(2)}, u32[]{:S(2)}) collective-permute-start(bf16[96,3200]{1,0:T(8,128)(2,1)S(1)} %all_gather.3.own_ref), channel_id=1, source_target_pairs={{0,960},{64,0},{128,64},{192,128},{256,192},{320,256},{384,320},{4... | collective-permute-start | bytes 1843208 | tf_op jit(solution)/shard_map/ppermute | solution.py:416
  147.0 8.9 %collective-permute-done.8.left_ref = bf16[96,3200]{1,0:T(8,128)(2,1)S(1)} collective-permute-done((bf16[96,3200]{1,0:T(8,128)(2,1)S(1)}, bf16[96,3200]{1,0:T(8,128)(2,1)S(1)}, u32[]{:S(2)}, u32[]{:S(2)}) %collective-permute-start.8) | collective-permute-done | bytes 614432 | tf_op jit(solution)/shard_map/ppermute | solution.py:416
  155.9 2.1 %collective-permute-start.10 = (bf16[48,3200]{1,0:T(8,128)(2,1)S(1)}, bf16[48,3200]{1,0:T(8,128)(2,1)S(1)}, u32[]{:S(2)}, u32[]{:S(2)}) collective-permute-start(bf16[48,3200]{1,0:T(8,128)(2,1)S(1)} %slice.8), channel_id=1, source_target_pairs={{0,64},{64,128},{128,192},{192,256},{256,320},{320,384},{384,448},... | collective-permute-start | bytes 921608 | tf_op jit(solution)/shard_map/ppermute | solution.py:416
  158.2 9.5 %collective-permute-start.11 = (bf16[48,3200]{1,0:T(8,128)(2,1)S(1)}, bf16[48,3200]{1,0:T(8,128)(2,1)S(1)}, u32[]{:S(2)}, u32[]{:S(2)}) collective-permute-start(bf16[48,3200]{1,0:T(8,128)(2,1)S(1)} %slice.9), channel_id=1, source_target_pairs={{0,960},{64,0},{128,64},{192,128},{256,192},{320,256},{384,320},{4... | collective-permute-start | bytes 921608 | tf_op jit(solution)/shard_map/ppermute | solution.py:416
  167.7 4.1 %collective-permute-done.10.far_left_ref = bf16[48,3200]{1,0:T(8,128)(2,1)S(1)} collective-permute-done((bf16[48,3200]{1,0:T(8,128)(2,1)S(1)}, bf16[48,3200]{1,0:T(8,128)(2,1)S(1)}, u32[]{:S(2)}, u32[]{:S(2)}) %collective-permute-start.10) | collective-permute-done | bytes 307232 | tf_op jit(solution)/shard_map/ppermute | solution.py:416
  171.7 0.9 collective-permute-done.11.far_right_ref
  172.7 3.3 %shard_map.133 = bf16[64,24,128]{2,1,0:T(8,128)(2,1)} custom-call(s32[1]{0:T(128)} %bitcast.place_ref, bf16[96,3200]{1,0:T(8,128)(2,1)S(1)} %all_gather.3.own_ref, bf16[96,3200]{1,0:T(8,128)(2,1)S(1)} %collective-permute-done.8.left_ref, bf16[96,3200]{1,0:T(8,128)(2,1)S(1)} %collective-permute-done.9.right_ref, ...), custom_call_target="tpu_custom_call" | custom-call | flops 700000000 | bytes 4500000 | tf_op jit(solution)/shard_map/pallas_call | solution.py:487
  176.0 11.2 %all-to-all-start.1 = ((bf16[64,24,128]{2,1,0:T(8,128)(2,1)}), bf16[64,24,128]{2,1,0:T(8,128)(2,1)S(1)}, u32[]{:S(2)}, u32[]{:S(2)}) async-start(bf16[64,24,128]{2,1,0:T(8,128)(2,1)} %shard_map.133), calls=%async_computation.1 | async-start | bytes 786432 | tf_op jit(solution)/shard_map/all_to_all | solution.py:495
  187.3 2.1 %shard_map.135 = (bf16[224,1024]{1,0:T(8,128)(2,1)}, bf16[224,1024]{1,0:T(8,128)(2,1)}, bf16[224,1024]{1,0:T(8,128)(2,1)}) custom-call(s32[1]{0:T(128)} %bitcast.place_ref, bf16[96,3200]{1,0:T(8,128)(2,1)S(1)} %all_gather.3.own_ref, bf16[96,3200]{1,0:T(8,128)(2,1)S(1)} %collective-permute-done.8.left_ref, ...), custom_call_target="tpu_custom_call" | custom-call | flops 700000000 | bytes 4500000 | tf_op jit(solution)/shard_map/pallas_call | solution.py:497
  189.3 12.5 %all-to-all-done.1.back_ref = bf16[64,24,128]{2,1,0:T(8,128)(2,1)S(1)} async-done(((bf16[64,24,128]{2,1,0:T(8,128)(2,1)}), bf16[64,24,128]{2,1,0:T(8,128)(2,1)S(1)}, u32[]{:S(2)}, u32[]{:S(2)}) %all-to-all-start.1) | async-done | bytes 393248 | tf_op jit(solution)/shard_map/all_to_all | solution.py:495
  201.8 3.2 %shard_map.134 = (bf16[224,128]{1,0:T(8,128)(2,1)}, bf16[224,128]{1,0:T(8,128)(2,1)}, f32[8,128]{1,0:T(8,128)}) custom-call(bf16[64,24,128]{2,1,0:T(8,128)(2,1)S(1)} %all-to-all-done.1.back_ref, f32[128,128]{1,0:T(8,128)S(1)} %copy-done.10, s32[8,128]{1,0:T(8,128)S(1)} %bitcast.26, f32[8,128]{1,0:T(8,128)S(1)} %bitcast.28), custom_call_target="tpu_custom_call" | custom-call | flops 500000000 | bytes 1000000 | tf_op jit(solution)/shard_map/pallas_call | solution.py:507
  (30 shorter events, 4.0 us)
Async XLA Ops:
  0.6 36.3 %copy-start.1 = (bf16[1,224,1024]{2,1,0:T(8,128)(2,1)S(1)}, bf16[1,224,1024]{2,1,0:T(8,128)(2,1)}, u32[]{:S(2)}) copy-start(bf16[1,224,1024]{2,1,0:T(8,128)(2,1)} %param.14) | copy-start | bytes 1376260
  3.8 33.1 %copy-start = (bf16[1,224,1024]{2,1,0:T(8,128)(2,1)S(1)}, bf16[1,224,1024]{2,1,0:T(8,128)(2,1)}, u32[]{:S(2)}) copy-start(bf16[1,224,1024]{2,1,0:T(8,128)(2,1)} %param.13) | copy-start | bytes 1376260
  3.9 33.1 %all-to-all-start = ((bf16[64,24,128]{2,1,0:T(8,128)(2,1)}), bf16[64,24,128]{2,1,0:T(8,128)(2,1)S(1)}, u32[]{:S(2)}, u32[]{:S(2)}) async-start(bf16[64,24,128]{2,1,0:T(8,128)(2,1)} %get-tuple-element.30), calls=%async_computation | async-start | bytes 786432 | tf_op jit(solution)/shard_map/all_to_all | solution.py:445
  36.9 1.0 copy-start.2
  40.4 0.7 copy-start.4
  41.0 0.7 copy-start.6
  41.7 24.6 %collective-permute-start = (bf16[96,3072]{1,0:T(8,128)(2,1)S(1)}, bf16[96,3072]{1,0:T(8,128)(2,1)S(1)}, u32[]{:S(2)}, u32[]{:S(2)}) collective-permute-start(bf16[96,3072]{1,0:T(8,128)(2,1)S(1)} %get-tuple-element.32), channel_id=1, source_target_pairs={{0,64},{64,128},{128,192},{192,256},{256,320},{320,384},{384,448},... | collective-permute-start | bytes 1769480 | tf_op jit(solution)/shard_map/ppermute | solution.py:416
  43.6 23.5 %collective-permute-start.1 = (bf16[96,3072]{1,0:T(8,128)(2,1)S(1)}, bf16[96,3072]{1,0:T(8,128)(2,1)S(1)}, u32[]{:S(2)}, u32[]{:S(2)}) collective-permute-start(bf16[96,3072]{1,0:T(8,128)(2,1)S(1)} %get-tuple-element.33), channel_id=1, source_target_pairs={{0,960},{64,0},{128,64},{192,128},{256,192},{320,256},{384,320},{4... | collective-permute-start | bytes 1769480 | tf_op jit(solution)/shard_map/ppermute | solution.py:416
  67.3 11.4 %collective-permute-start.2 = (bf16[48,3072]{1,0:T(8,128)(2,1)S(1)}, bf16[48,3072]{1,0:T(8,128)(2,1)S(1)}, u32[]{:S(2)}, u32[]{:S(2)}) collective-permute-start(bf16[48,3072]{1,0:T(8,128)(2,1)S(1)} %get-tuple-element.36), channel_id=1, source_target_pairs={{0,64},{64,128},{128,192},{192,256},{256,320},{320,384},{384,448},... | collective-permute-start | bytes 884744 | tf_op jit(solution)/shard_map/ppermute | solution.py:416
  69.2 10.4 %collective-permute-start.3 = (bf16[48,3072]{1,0:T(8,128)(2,1)S(1)}, bf16[48,3072]{1,0:T(8,128)(2,1)S(1)}, u32[]{:S(2)}, u32[]{:S(2)}) collective-permute-start(bf16[48,3072]{1,0:T(8,128)(2,1)S(1)} %get-tuple-element.37), channel_id=1, source_target_pairs={{0,960},{64,0},{128,64},{192,128},{256,192},{320,256},{384,320},{4... | collective-permute-start | bytes 884744 | tf_op jit(solution)/shard_map/ppermute | solution.py:416
  80.0 10.1 %collective-permute-start.4 = (bf16[24,3072]{1,0:T(8,128)(2,1)S(1)}, bf16[24,3072]{1,0:T(8,128)(2,1)S(1)}, u32[]{:S(2)}, u32[]{:S(2)}) collective-permute-start(bf16[24,3072]{1,0:T(8,128)(2,1)S(1)} %get-tuple-element.39), channel_id=1, source_target_pairs={{0,256},{64,320},{128,384},{192,448},{256,512},{320,576},{384,640}... | collective-permute-start | bytes 442376 | tf_op jit(solution)/shard_map/ppermute | solution.py:416
  82.3 10.1 %collective-permute-start.5 = (bf16[24,3072]{1,0:T(8,128)(2,1)S(1)}, bf16[24,3072]{1,0:T(8,128)(2,1)S(1)}, u32[]{:S(2)}, u32[]{:S(2)}) collective-permute-start(bf16[24,3072]{1,0:T(8,128)(2,1)S(1)} %get-tuple-element.40), channel_id=1, source_target_pairs={{0,768},{64,832},{128,896},{192,960},{256,0},{320,64},{384,128},{4... | collective-permute-start | bytes 442376 | tf_op jit(solution)/shard_map/ppermute | solution.py:416
  92.4 11.4 %collective-permute-start.6 = (bf16[24,1536]{1,0:T(8,128)(2,1)S(1)}, bf16[24,1536]{1,0:T(8,128)(2,1)S(1)}, u32[]{:S(2)}, u32[]{:S(2)}) collective-permute-start(bf16[24,1536]{1,0:T(8,128)(2,1)S(1)} %get-tuple-element.43), channel_id=1, source_target_pairs={{0,256},{64,320},{128,384},{192,448},{256,512},{320,576},{384,640}... | collective-permute-start | bytes 221192 | tf_op jit(solution)/shard_map/ppermute | solution.py:416
  97.9 9.9 %collective-permute-start.7 = (bf16[24,1536]{1,0:T(8,128)(2,1)S(1)}, bf16[24,1536]{1,0:T(8,128)(2,1)S(1)}, u32[]{:S(2)}, u32[]{:S(2)}) collective-permute-start(bf16[24,1536]{1,0:T(8,128)(2,1)S(1)} %get-tuple-element.44), channel_id=1, source_target_pairs={{0,768},{64,832},{128,896},{192,960},{256,0},{320,64},{384,128},{4... | collective-permute-start | bytes 221192 | tf_op jit(solution)/shard_map/ppermute | solution.py:416
  134.5 21.4 %collective-permute-start.8 = (bf16[96,3200]{1,0:T(8,128)(2,1)S(1)}, bf16[96,3200]{1,0:T(8,128)(2,1)S(1)}, u32[]{:S(2)}, u32[]{:S(2)}) collective-permute-start(bf16[96,3200]{1,0:T(8,128)(2,1)S(1)} %all_gather.3.own_ref), channel_id=1, source_target_pairs={{0,64},{64,128},{128,192},{192,256},{256,320},{320,384},{384,448},... | collective-permute-start | bytes 1843208 | tf_op jit(solution)/shard_map/ppermute | solution.py:416
  139.5 18.7 %collective-permute-start.9 = (bf16[96,3200]{1,0:T(8,128)(2,1)S(1)}, bf16[96,3200]{1,0:T(8,128)(2,1)S(1)}, u32[]{:S(2)}, u32[]{:S(2)}) collective-permute-start(bf16[96,3200]{1,0:T(8,128)(2,1)S(1)} %all_gather.3.own_ref), channel_id=1, source_target_pairs={{0,960},{64,0},{128,64},{192,128},{256,192},{320,256},{384,320},{4... | collective-permute-start | bytes 1843208 | tf_op jit(solution)/shard_map/ppermute | solution.py:416
  155.9 16.7 %copy-start.3 = (bf16[1,1024,224]{1,2,0:T(8,128)(2,1)S(1)}, bf16[1,1024,224]{1,2,0:T(8,128)(2,1)}, u32[]{:S(2)}) copy-start(bf16[1,1024,224]{1,2,0:T(8,128)(2,1)} %param.15) | copy-start | bytes 1376260
  155.9 15.8 %collective-permute-start.10 = (bf16[48,3200]{1,0:T(8,128)(2,1)S(1)}, bf16[48,3200]{1,0:T(8,128)(2,1)S(1)}, u32[]{:S(2)}, u32[]{:S(2)}) collective-permute-start(bf16[48,3200]{1,0:T(8,128)(2,1)S(1)} %slice.8), channel_id=1, source_target_pairs={{0,64},{64,128},{128,192},{192,256},{256,320},{320,384},{384,448},... | collective-permute-start | bytes 921608 | tf_op jit(solution)/shard_map/ppermute | solution.py:416
  158.2 14.5 %collective-permute-start.11 = (bf16[48,3200]{1,0:T(8,128)(2,1)S(1)}, bf16[48,3200]{1,0:T(8,128)(2,1)S(1)}, u32[]{:S(2)}, u32[]{:S(2)}) collective-permute-start(bf16[48,3200]{1,0:T(8,128)(2,1)S(1)} %slice.9), channel_id=1, source_target_pairs={{0,960},{64,0},{128,64},{192,128},{256,192},{320,256},{384,320},{4... | collective-permute-start | bytes 921608 | tf_op jit(solution)/shard_map/ppermute | solution.py:416
  176.0 11.2 %copy-start.5 = (bf16[384,224]{1,0:T(8,128)(2,1)S(1)}, bf16[384,224]{1,0:T(8,128)(2,1)}, u32[]{:S(2)}) copy-start(bf16[384,224]{1,0:T(8,128)(2,1)} %copy-done.4) | copy-start | bytes 516100
  176.0 11.2 %copy-start.7 = (bf16[384,224]{1,0:T(8,128)(2,1)S(1)}, bf16[384,224]{1,0:T(8,128)(2,1)}, u32[]{:S(2)}) copy-start(bf16[384,224]{1,0:T(8,128)(2,1)} %copy-done.6) | copy-start | bytes 516100
  176.0 25.8 %all-to-all-start.1 = ((bf16[64,24,128]{2,1,0:T(8,128)(2,1)}), bf16[64,24,128]{2,1,0:T(8,128)(2,1)S(1)}, u32[]{:S(2)}, u32[]{:S(2)}) async-start(bf16[64,24,128]{2,1,0:T(8,128)(2,1)} %shard_map.133), calls=%async_computation.1 | async-start | bytes 786432 | tf_op jit(solution)/shard_map/all_to_all | solution.py:495
  187.2 14.6 %copy-start.8 = (s32[128,8]{0,1:T(8,128)S(1)}, s32[128,8]{0,1:T(8,128)}, u32[]{:S(2)}) copy-start(s32[128,8]{0,1:T(8,128)} %param.10) | copy-start | bytes 12292
  187.2 14.6 %copy-start.9 = (f32[128,8]{0,1:T(8,128)S(1)}, f32[128,8]{0,1:T(8,128)}, u32[]{:S(2)}) copy-start(f32[128,8]{0,1:T(8,128)} %param.11) | copy-start | bytes 12292
  187.2 14.6 %copy-start.10 = (f32[128,128]{1,0:T(8,128)S(1)}, f32[128,128]{1,0:T(8,128)}, u32[]{:S(2)}) copy-start(f32[128,128]{1,0:T(8,128)} %get-tuple-element.45.plan_ref) | copy-start | bytes 196612

commit v5 on v3

--- a/solution.py
+++ b/solution.py
@@ -13,6 +13,7 @@
 SOURCES = 16
 RING = 4
 SCORE_LANE = 96
+WEIGHT_PARTS = 2
 VMEM_LIMIT = 24 * 1024 * 1024
 
 F32 = jnp.float32
@@ -188,23 +189,40 @@
     to_left_ref[...] = (previous_ref[...].astype(F32) + from_right_ref[half:].astype(F32)).astype(BF16)
 
 
-def window_kernel(own_ref, from_left_ref, from_right_ref, far_left_ref, far_right_ref, out_ref):
+def window_kernel(
+    place_ref,
+    own_ref,
+    from_left_ref,
+    from_right_ref,
+    far_left_ref,
+    far_right_ref,
+    kept_ref,
+    to_right_ref,
+    to_left_ref,
+    across_ref,
+    window_ref,
+):
     half = far_left_ref.shape[0]
-    out_ref[:half] = (
+    window_ref[:half] = (
         own_ref[:half].astype(F32) + from_right_ref[:half].astype(F32) + far_left_ref[...].astype(F32)
-    ).astype(BF16)
-    out_ref[half:] = (
+    )
+    window_ref[half:] = (
         own_ref[half:].astype(F32) + from_left_ref[half:].astype(F32) + far_right_ref[...].astype(F32)
-    ).astype(BF16)
-
-
-def middle_kernel(sum_ref, out_ref):
-    hidden = sum_ref.shape[1] // 3
-    share = out_ref.shape[0]
+    )
+    share = kept_ref.shape[0]
+    for step, ref in ((1, to_right_ref), (RING - 1, to_left_ref), (RING // 2, across_ref), (0, kept_ref)):
+        member = (lax.shift_right_logical(place_ref[0], 2) + step) & (RING - 1)
+        begin = pl.multiple_of(member * share, share)
+        ref[...] = window_ref[pl.ds(begin, share)].astype(BF16)
+
+
+def middle_kernel(kept_ref, from_left_ref, from_right_ref, across_ref, out_ref):
+    hidden = kept_ref.shape[1] // 3
 
     def summed(index):
-        values = sum_ref[:, index * hidden : (index + 1) * hidden].astype(F32)
-        return sum(values[i * share : (i + 1) * share] for i in range(sum_ref.shape[0] // share))
+        columns = slice(index * hidden, (index + 1) * hidden)
+        refs = (kept_ref, from_left_ref, from_right_ref, across_ref)
+        return sum(ref[:, columns].astype(F32) for ref in refs)
 
     gate, up, grad = summed(0), summed(1), summed(2)
     sigmoid = jax.nn.sigmoid(gate)
@@ -304,38 +322,52 @@
         )
 
 
-def combine_kernel(back_ref, plan_ref, routes_ref, weight_ref, mixed_ref, input_ref, score_ref):
+def choose_kernel(plan_ref, chosen_ref, scored_ref):
+    experts = plan_ref.shape[0] // 2
+    token_count = plan_ref.shape[1]
+    rows = experts * GROUP
+    plan = plan_ref[...].T
+    rank, scale = plan[:, :experts], plan[:, experts:]
+    spread = one_zero(expert_of_row(iota((experts, rows), 1), iota((experts, rows), 0)))
+    tile, slot = tile_and_slot(iota((1, rows), 1))
+    taken = dot(rank.astype(BF16), spread) == slot.astype(F32)
+    for order, part in enumerate(three_parts(scale)[:WEIGHT_PARTS]):
+        row_scale = jnp.where(taken, dot(part, spread), 0.0)
+        for index in range(2):
+            place = (index * WEIGHT_PARTS + order) * token_count
+            chosen_ref[place : place + token_count] = jnp.where(tile == index, row_scale, 0.0).astype(BF16)
+    taken = jnp.where(taken, 1.0, 0.0)
+    for index in range(2):
+        place = (2 * WEIGHT_PARTS + index) * token_count
+        chosen_ref[place : place + token_count] = jnp.where(tile == 2 + index, taken, 0.0).astype(BF16)
+    scored_ref[...] = jnp.where(tile == 1, taken, 0.0).astype(BF16)
+
+
+def combine_kernel(
+    back_ref, chosen_ref, scored_ref, routes_ref, weight_ref, mixed_ref, input_ref, score_ref
+):
     top_count, token_count = routes_ref.shape
-    experts = plan_ref.shape[0] // 2
+    experts = back_ref.shape[0]
     width = mixed_ref.shape[0]
     rows = experts * GROUP
     back = back_ref[...].reshape(rows, LANES)
-    plan = plan_ref[...].T
-    rank, scale = plan[:, :experts], plan[:, experts:]
-    spread = one_zero(expert_of_row(iota((experts, rows), 1), iota((experts, rows), 0)))
-    tile, slot = tile_and_slot(iota((token_count, rows), 1))
-    taken = dot(rank.astype(BF16), spread) == slot.astype(F32)
-    mixed = [jnp.zeros((token_count, LANES), F32) for _ in range(2)]
-    for part in three_parts(scale):
-        row_scale = dot(part, spread)
-        for index in range(2):
-            chosen = jnp.where(taken & (tile == index), row_scale, 0.0).astype(BF16)
-            mixed[index] = mixed[index] + dot(chosen, back)
+    values = dot(chosen_ref[...], back)
+    blocks = [values[i * token_count : (i + 1) * token_count] for i in range(2 * WEIGHT_PARTS + 2)]
+    low, high = sum(blocks[:WEIGHT_PARTS]), sum(blocks[WEIGHT_PARTS : 2 * WEIGHT_PARTS])
     for ref, low, high in (
-        (mixed_ref, mixed[0], mixed[1]),
-        (
-            input_ref,
-            dot(one_zero(taken & (tile == 2)), back),
-            dot(one_zero(taken & (tile == 3)), back),
-        ),
+        (mixed_ref, low, high),
+        (input_ref, blocks[2 * WEIGHT_PARTS], blocks[2 * WEIGHT_PARTS + 1]),
     ):
         ref[:LANES] = low.T.astype(BF16)
         ref[LANES:] = high.T[: width - LANES].astype(BF16)
-    lane = iota((8, LANES), 1)
-    score_lanes = one_zero((lane >= SCORE_LANE) & (lane < SCORE_LANE + 3))
-    row_score = dot(score_lanes, back, CONTRACT_LAST)[:1]
-    routed = jnp.where(taken & (tile == 1), row_score, 0.0)
-    by_expert = sum(dot(spread, part, CONTRACT_LAST) for part in three_parts(routed))
+    lane_of_part = iota((8, LANES), 1) - SCORE_LANE == iota((8, LANES), 0)
+    row_score = dot(one_zero(lane_of_part & (iota((8, LANES), 0) < 3)), back, CONTRACT_LAST)
+    here = expert_of_row(iota((experts, rows), 1), iota((experts, rows), 0))
+    spread = jnp.concatenate(
+        [jnp.where(here, row_score[i : i + 1], 0.0).astype(BF16) for i in range(3)], axis=0
+    )
+    by_expert = dot(spread, scored_ref[...], CONTRACT_LAST)
+    by_expert = sum(by_expert[i * experts : (i + 1) * experts] for i in range(3))
     expert = iota((experts, token_count), 0)
     for k in range(top_count):
         hit = routes_ref[k : k + 1] == expert
@@ -383,7 +415,7 @@
     rows = shape((row_count, width), BF16)
     whole, halved = (shape((size, 3 * hidden), BF16) for size in (held, held // 2))
     groups = [list(range(i, parts, RING)) for i in range(RING)]
-    member = (lax.axis_index("expert") % RING).astype(jnp.int32).reshape(1)
+    member = lax.axis_index("expert").astype(jnp.int32).reshape(1)
     weights = (gate_weight[0], up_weight[0], down_weight[0].T)
     arguments = (routes.T, route_weights.T, owner_slots.reshape(1, experts), tokens.T, cotangent.T)
     send, plan = kernel_call(
@@ -408,15 +440,23 @@
         following, previous, from_left, from_right
     )
     far_left, far_right = shifted(relay_right, 1), shifted(relay_left, -1)
-    window = kernel_call(window_kernel, whole, 600_000, 2_000_000)(
-        own, from_left, from_right, far_left, far_right
-    )
-    summands = lax.all_to_all(
-        window, "expert", split_axis=0, concat_axis=0, tiled=True, axis_index_groups=groups
-    )
+    chunk = shape((row_count // parts, 3 * hidden), BF16)
+    kept, to_right, to_left, across = kernel_call(
+        window_kernel,
+        (chunk, chunk, chunk, chunk),
+        600_000,
+        2_000_000,
+        spaces="svvvvv",
+        scratch=[pltpu.VMEM(whole.shape, F32)],
+    )(member, own, from_left, from_right, far_left, far_right)
     share = kernel_call(
         middle_kernel, shape((row_count // parts, 3 * hidden + LANES), BF16), 1_000_000, 700_000
-    )(summands)
+    )(
+        kept,
+        shifted(to_right, RING),
+        shifted(to_left, -RING),
+        shifted(across, parts // 2),
+    )
     own = lax.all_gather(share, "expert", axis=0, tiled=True, axis_index_groups=groups)
     half = held // 2
     left, right = shifted(own, 1), shifted(own, -1)
@@ -442,12 +482,22 @@
     )(member, *pieces, token_rows, scaled_rows)
     down_grad = down_grad.T
     token_shape = shape((width, token_count), BF16)
+    slots = experts * GROUP
+    chosen, scored = kernel_call(
+        choose_kernel,
+        (
+            shape(((2 * WEIGHT_PARTS + 2) * token_count, slots), BF16),
+            shape((token_count, slots), BF16),
+        ),
+        200_000_000,
+        3_000_000,
+    )(plan)
     mixed, input_gradient, route_gradient = kernel_call(
         combine_kernel,
         (token_shape, token_shape, shape(arguments[0].shape, F32)),
         500_000_000,
         1_000_000,
-    )(returned, plan, arguments[0], arguments[1])
+    )(returned, chosen, scored, arguments[0], arguments[1])
     return (
         mixed.T,
         input_gradient.T,

time: 201 us -> 211 us (1.050)
  blocking collectives: 50.2 us -> 25.7 us
  waiting for transfers between devices: 56.8 us -> 72.7 us
  starting transfers between devices: 76.5 us -> 85.7 us
  local copies, waits for them, and re-layouts: 2.41 us -> 11.5 us
    all_to_all x1 -> x0, blocking collectives: 21.3 us -> none  [per_device(): lax.all_to_all(window, 'expert', split_axis=0, concat_axis=0, tiled=True,...]
    ppermute x8 -> x11, waiting for transfers between devices: 29.6 us -> 48.5 us  [shifted(): lax.ppermute(block, 'expert', [(i, (i + distance) % parts) for i in range...]
    ppermute x8 -> x11, starting transfers between devices: 45.4 us -> 58.3 us  [shifted(): lax.ppermute(block, 'expert', [(i, (i + distance) % parts) for i in range...]
    unnamed x26 -> x34, local copies, waits for them, and re-layouts: 2.36 us -> 11.4 us
    all_to_all x1, starting transfers between devices: 12.7 us -> 9.24 us  [per_device(): lax.all_to_all(back, 'dp', split_axis=0, concat_axis=0, tiled=True)]
    all_gather x1, blocking collectives: 29 us -> 25.7 us  [per_device(): lax.all_gather(share, 'expert', axis=0, tiled=True, axis_index_groups=gro...]
    all_to_all x1, waiting for transfers between devices: 12.5 us -> 9.41 us  [per_device(): lax.all_to_all(back, 'dp', split_axis=0, concat_axis=0, tiled=True)]
  transfers between devices with their start and end apart: 10 -> 13, of which waited for: 9 -> 10; matrix products, arithmetic and copies ran while one was open for 0% -> 0% of each run, Pallas kernels for 1% -> 1%
where the time goes in v5:
time: 211 us; the launch traced here: 210 us
  starting transfers between devices  85.7 us (41%)
  waiting for transfers between devices  72.7 us (34%)
  blocking collectives  25.7 us (12%)
  Pallas kernels  13.4 us (6%)
  local copies, waits for them, and re-layouts  11.5 us (5%)
    ppermute x11, starting transfers between devices, shifted(): lax.ppermute(block, 'expert', [(i, (i + distance) % parts) for i in range...  58.3 us
    ppermute x11, waiting for transfers between devices, shifted(): lax.ppermute(block, 'expert', [(i, (i + distance) % parts) for i in range...  48.5 us
    all_gather x1, blocking collectives, per_device(): lax.all_gather(share, 'expert', axis=0, tiled=True, axis_index_groups=gro...  25.7 us
    all_to_all x1, starting transfers between devices, per_device(): lax.all_to_all(send, 'dp', split_axis=0, concat_axis=0, tiled=True)  18.2 us
    all_to_all x1, waiting for transfers between devices, per_device(): lax.all_to_all(send, 'dp', split_axis=0, concat_axis=0, tiled=True)  14.7 us
    unnamed x34, local copies, waits for them, and re-layouts  11.4 us
    all_to_all x1, waiting for transfers between devices, per_device(): lax.all_to_all(back, 'dp', split_axis=0, concat_axis=0, tiled=True)  9.41 us
    all_to_all x1, starting transfers between devices, per_device(): lax.all_to_all(back, 'dp', split_axis=0, concat_axis=0, tiled=True)  9.24 us
  transfers between devices with their start and end apart: 13, of which 10 were waited for; matrix products, arithmetic and copies ran while one was open for 0% of the time, Pallas kernels for 1%

profile of v5, /device:TPU:1, one launch (start us, length us, event | category | flops | bytes accessed | tf_op | source)
XLA Modules:
  0.0 209.8 jit_solution(6189568059547496157)
XLA Ops:
  4.3 2.4 %shard_map.127 = (bf16[64,24,128]{2,1,0:T(8,128)(2,1)}, f32[128,128]{1,0:T(8,128)S(1)}) custom-call(s32[8,128]{1,0:T(8,128)S(1)} %bitcast.25, f32[8,128]{1,0:T(8,128)S(1)} %bitcast.27, s32[1,64]{1,0:T(1,128)S(1)} %bitcast.31, bf16[224,128]{1,0:T(8,128)(2,1)S(1)} %bitcast.29, bf16[224,128]{1,0:T(8,128)(2,1)S(1)} %bitcast.30), custom_call_target="tpu_custom_call" | custom-call | flops 300000000 | bytes 1000000 | tf_op jit(solution)/shard_map/pallas_call | solution.py:421
  6.7 18.2 %all-to-all-start = ((bf16[64,24,128]{2,1,0:T(8,128)(2,1)}), bf16[64,24,128]{2,1,0:T(8,128)(2,1)S(1)}, u32[]{:S(2)}, u32[]{:S(2)}) async-start(bf16[64,24,128]{2,1,0:T(8,128)(2,1)} %get-tuple-element.29), calls=%async_computation | async-start | bytes 786432 | tf_op jit(solution)/shard_map/all_to_all | solution.py:429
  24.9 14.7 %all-to-all-done.recv_ref = bf16[64,24,128]{2,1,0:T(8,128)(2,1)S(1)} async-done(((bf16[64,24,128]{2,1,0:T(8,128)(2,1)}), bf16[64,24,128]{2,1,0:T(8,128)(2,1)S(1)}, u32[]{:S(2)}, u32[]{:S(2)}) %all-to-all-start) | async-done | bytes 393248 | tf_op jit(solution)/shard_map/all_to_all | solution.py:429
  39.7 1.0 copy-done.2
  40.7 1.0 copy-done.4
  41.7 1.0 copy-done.6
  42.7 2.4 %shard_map.128 = (bf16[96,3072]{1,0:T(8,128)(2,1)S(1)}, bf16[96,3072]{1,0:T(8,128)(2,1)S(1)}, bf16[96,3072]{1,0:T(8,128)(2,1)S(1)}, bf16[48,3072]{1,0:T(8,128)(2...) custom-call(s32[1]{0:T(128)} %bitcast.place_ref, ...), custom_call_target="tpu_custom_call" | custom-call | flops 700000000 | bytes 4500000 | tf_op jit(solution)/shard_map/pallas_call | solution.py:430
  45.8 1.9 collective-permute-start
  47.7 11.2 %collective-permute-start.1 = (bf16[96,3072]{1,0:T(8,128)(2,1)S(1)}, bf16[96,3072]{1,0:T(8,128)(2,1)S(1)}, u32[]{:S(2)}, u32[]{:S(2)}) collective-permute-start(bf16[96,3072]{1,0:T(8,128)(2,1)S(1)} %get-tuple-element.32), channel_id=1, source_target_pairs={{0,960},{64,0},{128,64},{192,128},{256,192},{320,256},{384,320},{4... | collective-permute-start | bytes 1769480 | tf_op jit(solution)/shard_map/ppermute | solution.py:401
  58.9 11.4 %collective-permute-done.from_left_ref = bf16[96,3072]{1,0:T(8,128)(2,1)S(1)} collective-permute-done((bf16[96,3072]{1,0:T(8,128)(2,1)S(1)}, bf16[96,3072]{1,0:T(8,128)(2,1)S(1)}, u32[]{:S(2)}, u32[]{:S(2)}) %collective-permute-start) | collective-permute-done | bytes 589856 | tf_op jit(solution)/shard_map/ppermute | solution.py:401
  71.4 1.9 collective-permute-start.2
  73.3 5.3 %collective-permute-start.3 = (bf16[48,3072]{1,0:T(8,128)(2,1)S(1)}, bf16[48,3072]{1,0:T(8,128)(2,1)S(1)}, u32[]{:S(2)}, u32[]{:S(2)}) collective-permute-start(bf16[48,3072]{1,0:T(8,128)(2,1)S(1)} %get-tuple-element.36), channel_id=1, source_target_pairs={{0,960},{64,0},{128,64},{192,128},{256,192},{320,256},{384,320},{4... | collective-permute-start | bytes 884744 | tf_op jit(solution)/shard_map/ppermute | solution.py:401
  78.6 4.2 %collective-permute-done.2.far_left_ref = bf16[48,3072]{1,0:T(8,128)(2,1)S(1)} collective-permute-done((bf16[48,3072]{1,0:T(8,128)(2,1)S(1)}, bf16[48,3072]{1,0:T(8,128)(2,1)S(1)}, u32[]{:S(2)}, u32[]{:S(2)}) %collective-permute-start.2) | collective-permute-done | bytes 294944 | tf_op jit(solution)/shard_map/ppermute | solution.py:401
  84.1 2.2 %collective-permute-start.4 = (bf16[24,3072]{1,0:T(8,128)(2,1)S(1)}, bf16[24,3072]{1,0:T(8,128)(2,1)S(1)}, u32[]{:S(2)}, u32[]{:S(2)}) collective-permute-start(bf16[24,3072]{1,0:T(8,128)(2,1)S(1)} %get-tuple-element.38), channel_id=1, source_target_pairs={{0,256},{64,320},{128,384},{192,448},{256,512},{320,576},{384,640}... | collective-permute-start | bytes 442376 | tf_op jit(solution)/shard_map/ppermute | solution.py:401
  86.3 6.9 %collective-permute-start.5 = (bf16[24,3072]{1,0:T(8,128)(2,1)S(1)}, bf16[24,3072]{1,0:T(8,128)(2,1)S(1)}, u32[]{:S(2)}, u32[]{:S(2)}) collective-permute-start(bf16[24,3072]{1,0:T(8,128)(2,1)S(1)} %get-tuple-element.39), channel_id=1, source_target_pairs={{0,768},{64,832},{128,896},{192,960},{256,0},{320,64},{384,128},{4... | collective-permute-start | bytes 442376 | tf_op jit(solution)/shard_map/ppermute | solution.py:401
  93.3 5.5 %collective-permute-start.6 = (bf16[24,3072]{1,0:T(8,128)(2,1)S(1)}, bf16[24,3072]{1,0:T(8,128)(2,1)S(1)}, u32[]{:S(2)}, u32[]{:S(2)}) collective-permute-start(bf16[24,3072]{1,0:T(8,128)(2,1)S(1)} %get-tuple-element.40), channel_id=1, source_target_pairs={{0,512},{64,576},{128,640},{192,704},{256,768},{320,832},{384,896}... | collective-permute-start | bytes 442376 | tf_op jit(solution)/shard_map/ppermute | solution.py:401
  98.8 13.5 %collective-permute-done.6.across_ref = bf16[24,3072]{1,0:T(8,128)(2,1)S(1)} collective-permute-done((bf16[24,3072]{1,0:T(8,128)(2,1)S(1)}, bf16[24,3072]{1,0:T(8,128)(2,1)S(1)}, u32[]{:S(2)}, u32[]{:S(2)}) %collective-permute-start.6) | collective-permute-done | bytes 147488 | tf_op jit(solution)/shard_map/ppermute | solution.py:401
  112.4 25.7 %all_gather.3.own_ref = bf16[96,3200]{1,0:T(8,128)(2,1)S(1)} all-gather(bf16[24,3200]{1,0:T(8,128)(2,1)S(1)} %shard_map.131), channel_id=1, replica_groups={{0,256,512,768},{64,320,576,832},{128,384,640,896},{192,448,704,960},{1..., dimensions={0}, use_global_device_ids=true | all-gather | bytes 768000 | tf_op jit(solution)/shard_map/all_gather | solution.py:460
  138.1 14.1 %collective-permute-start.8 = (bf16[96,3200]{1,0:T(8,128)(2,1)S(1)}, bf16[96,3200]{1,0:T(8,128)(2,1)S(1)}, u32[]{:S(2)}, u32[]{:S(2)}) collective-permute-start(bf16[96,3200]{1,0:T(8,128)(2,1)S(1)} %all_gather.3.own_ref), channel_id=1, source_target_pairs={{0,960},{64,0},{128,64},{192,128},{256,192},{320,256},{384,320},{4... | collective-permute-start | bytes 1843208 | tf_op jit(solution)/shard_map/ppermute | solution.py:401
  152.2 1.9 collective-permute-start.7
  154.1 10.1 %collective-permute-done.8.right_ref = bf16[96,3200]{1,0:T(8,128)(2,1)S(1)} collective-permute-done((bf16[96,3200]{1,0:T(8,128)(2,1)S(1)}, bf16[96,3200]{1,0:T(8,128)(2,1)S(1)}, u32[]{:S(2)}, u32[]{:S(2)}) %collective-permute-start.8) | collective-permute-done | bytes 614432 | tf_op jit(solution)/shard_map/ppermute | solution.py:401
  164.2 5.3 %collective-permute-start.10 = (bf16[48,3200]{1,0:T(8,128)(2,1)S(1)}, bf16[48,3200]{1,0:T(8,128)(2,1)S(1)}, u32[]{:S(2)}, u32[]{:S(2)}) collective-permute-start(bf16[48,3200]{1,0:T(8,128)(2,1)S(1)} %slice.9), channel_id=1, source_target_pairs={{0,960},{64,0},{128,64},{192,128},{256,192},{320,256},{384,320},{4... | collective-permute-start | bytes 921608 | tf_op jit(solution)/shard_map/ppermute | solution.py:401
  169.6 1.9 collective-permute-start.9
  171.5 2.5 %collective-permute-done.10.far_right_ref = bf16[48,3200]{1,0:T(8,128)(2,1)S(1)} collective-permute-done((bf16[48,3200]{1,0:T(8,128)(2,1)S(1)}, bf16[48,3200]{1,0:T(8,128)(2,1)S(1)}, u32[]{:S(2)}, u32[]{:S(2)}) %collective-permute-start.10) | collective-permute-done | bytes 307232 | tf_op jit(solution)/shard_map/ppermute | solution.py:401
  174.1 5.1 %collective-permute-done.9.far_left_ref = bf16[48,3200]{1,0:T(8,128)(2,1)S(1)} collective-permute-done((bf16[48,3200]{1,0:T(8,128)(2,1)S(1)}, bf16[48,3200]{1,0:T(8,128)(2,1)S(1)}, u32[]{:S(2)}, u32[]{:S(2)}) %collective-permute-start.9) | collective-permute-done | bytes 307232 | tf_op jit(solution)/shard_map/ppermute | solution.py:401
  179.2 3.3 %shard_map.132 = bf16[64,24,128]{2,1,0:T(8,128)(2,1)} custom-call(s32[1]{0:T(128)} %bitcast.place_ref, bf16[96,3200]{1,0:T(8,128)(2,1)S(1)} %all_gather.3.own_ref, bf16[96,3200]{1,0:T(8,128)(2,1)S(1)} %collective-permute-done.7.left_ref, bf16[96,3200]{1,0:T(8,128)(2,1)S(1)} %collective-permute-done.8.right_ref, ...), custom_call_target="tpu_custom_call" | custom-call | flops 700000000 | bytes 4500000 | tf_op jit(solution)/shard_map/pallas_call | solution.py:465
  182.5 9.2 %all-to-all-start.1 = ((bf16[64,24,128]{2,1,0:T(8,128)(2,1)}), bf16[64,24,128]{2,1,0:T(8,128)(2,1)S(1)}, u32[]{:S(2)}, u32[]{:S(2)}) async-start(bf16[64,24,128]{2,1,0:T(8,128)(2,1)} %shard_map.132), calls=%async_computation.1 | async-start | bytes 786432 | tf_op jit(solution)/shard_map/all_to_all | solution.py:473
  192.6 1.4 copy-done
  194.9 2.1 shard_map.135
  197.0 9.4 %all-to-all-done.1.back_ref = bf16[64,24,128]{2,1,0:T(8,128)(2,1)S(1)} async-done(((bf16[64,24,128]{2,1,0:T(8,128)(2,1)}), bf16[64,24,128]{2,1,0:T(8,128)(2,1)S(1)}, u32[]{:S(2)}, u32[]{:S(2)}) %all-to-all-start.1) | async-done | bytes 393248 | tf_op jit(solution)/shard_map/all_to_all | solution.py:473
  206.4 1.7 copy-done.1
  208.1 1.8 shard_map.134
  (40 shorter events, 8.6 us)
Async XLA Ops:
  0.6 0.7 copy-start.10
  1.3 0.7 copy-start.12
  2.0 0.8 copy-start.14
  2.8 0.8 copy-start.15
  3.6 0.7 copy-start.16
  6.7 33.0 %all-to-all-start = ((bf16[64,24,128]{2,1,0:T(8,128)(2,1)}), bf16[64,24,128]{2,1,0:T(8,128)(2,1)S(1)}, u32[]{:S(2)}, u32[]{:S(2)}) async-start(bf16[64,24,128]{2,1,0:T(8,128)(2,1)} %get-tuple-element.29), calls=%async_computation | async-start | bytes 786432 | tf_op jit(solution)/shard_map/all_to_all | solution.py:429
  39.7 1.0 copy-start.2
  40.7 1.0 copy-start.4
  41.7 1.0 copy-start.6
  45.1 0.7 copy-start.8
  45.8 24.6 %collective-permute-start = (bf16[96,3072]{1,0:T(8,128)(2,1)S(1)}, bf16[96,3072]{1,0:T(8,128)(2,1)S(1)}, u32[]{:S(2)}, u32[]{:S(2)}) collective-permute-start(bf16[96,3072]{1,0:T(8,128)(2,1)S(1)} %get-tuple-element.31), channel_id=1, source_target_pairs={{0,64},{64,128},{128,192},{192,256},{256,320},{320,384},{384,448},... | collective-permute-start | bytes 1769480 | tf_op jit(solution)/shard_map/ppermute | solution.py:401
  47.7 23.5 %collective-permute-start.1 = (bf16[96,3072]{1,0:T(8,128)(2,1)S(1)}, bf16[96,3072]{1,0:T(8,128)(2,1)S(1)}, u32[]{:S(2)}, u32[]{:S(2)}) collective-permute-start(bf16[96,3072]{1,0:T(8,128)(2,1)S(1)} %get-tuple-element.32), channel_id=1, source_target_pairs={{0,960},{64,0},{128,64},{192,128},{256,192},{320,256},{384,320},{4... | collective-permute-start | bytes 1769480 | tf_op jit(solution)/shard_map/ppermute | solution.py:401
  71.4 11.4 %collective-permute-start.2 = (bf16[48,3072]{1,0:T(8,128)(2,1)S(1)}, bf16[48,3072]{1,0:T(8,128)(2,1)S(1)}, u32[]{:S(2)}, u32[]{:S(2)}) collective-permute-start(bf16[48,3072]{1,0:T(8,128)(2,1)S(1)} %get-tuple-element.35), channel_id=1, source_target_pairs={{0,64},{64,128},{128,192},{192,256},{256,320},{320,384},{384,448},... | collective-permute-start | bytes 884744 | tf_op jit(solution)/shard_map/ppermute | solution.py:401
  73.3 10.4 %collective-permute-start.3 = (bf16[48,3072]{1,0:T(8,128)(2,1)S(1)}, bf16[48,3072]{1,0:T(8,128)(2,1)S(1)}, u32[]{:S(2)}, u32[]{:S(2)}) collective-permute-start(bf16[48,3072]{1,0:T(8,128)(2,1)S(1)} %get-tuple-element.36), channel_id=1, source_target_pairs={{0,960},{64,0},{128,64},{192,128},{256,192},{320,256},{384,320},{4... | collective-permute-start | bytes 884744 | tf_op jit(solution)/shard_map/ppermute | solution.py:401
  83.7 95.5 %copy-start.3 = (bf16[1,224,1024]{2,1,0:T(8,128)(2,1)S(1)}, bf16[1,224,1024]{2,1,0:T(8,128)(2,1)}, u32[]{:S(2)}) copy-start(bf16[1,224,1024]{2,1,0:T(8,128)(2,1)} %param.13) | copy-start | bytes 1376260
  83.7 95.5 %copy-start.5 = (bf16[1,224,1024]{2,1,0:T(8,128)(2,1)S(1)}, bf16[1,224,1024]{2,1,0:T(8,128)(2,1)}, u32[]{:S(2)}) copy-start(bf16[1,224,1024]{2,1,0:T(8,128)(2,1)} %param.14) | copy-start | bytes 1376260
  83.7 95.5 %copy-start.7 = (bf16[1,1024,224]{1,2,0:T(8,128)(2,1)S(1)}, bf16[1,1024,224]{1,2,0:T(8,128)(2,1)}, u32[]{:S(2)}) copy-start(bf16[1,1024,224]{1,2,0:T(8,128)(2,1)} %param.15) | copy-start | bytes 1376260
  84.1 14.7 %collective-permute-start.4 = (bf16[24,3072]{1,0:T(8,128)(2,1)S(1)}, bf16[24,3072]{1,0:T(8,128)(2,1)S(1)}, u32[]{:S(2)}, u32[]{:S(2)}) collective-permute-start(bf16[24,3072]{1,0:T(8,128)(2,1)S(1)} %get-tuple-element.38), channel_id=1, source_target_pairs={{0,256},{64,320},{128,384},{192,448},{256,512},{320,576},{384,640}... | collective-permute-start | bytes 442376 | tf_op jit(solution)/shard_map/ppermute | solution.py:401
  86.3 12.4 %collective-permute-start.5 = (bf16[24,3072]{1,0:T(8,128)(2,1)S(1)}, bf16[24,3072]{1,0:T(8,128)(2,1)S(1)}, u32[]{:S(2)}, u32[]{:S(2)}) collective-permute-start(bf16[24,3072]{1,0:T(8,128)(2,1)S(1)} %get-tuple-element.39), channel_id=1, source_target_pairs={{0,768},{64,832},{128,896},{192,960},{256,0},{320,64},{384,128},{4... | collective-permute-start | bytes 442376 | tf_op jit(solution)/shard_map/ppermute | solution.py:401
  93.3 19.0 %collective-permute-start.6 = (bf16[24,3072]{1,0:T(8,128)(2,1)S(1)}, bf16[24,3072]{1,0:T(8,128)(2,1)S(1)}, u32[]{:S(2)}, u32[]{:S(2)}) collective-permute-start(bf16[24,3072]{1,0:T(8,128)(2,1)S(1)} %get-tuple-element.40), channel_id=1, source_target_pairs={{0,512},{64,576},{128,640},{192,704},{256,768},{320,832},{384,896}... | collective-permute-start | bytes 442376 | tf_op jit(solution)/shard_map/ppermute | solution.py:401
  138.1 26.1 %collective-permute-start.8 = (bf16[96,3200]{1,0:T(8,128)(2,1)S(1)}, bf16[96,3200]{1,0:T(8,128)(2,1)S(1)}, u32[]{:S(2)}, u32[]{:S(2)}) collective-permute-start(bf16[96,3200]{1,0:T(8,128)(2,1)S(1)} %all_gather.3.own_ref), channel_id=1, source_target_pairs={{0,960},{64,0},{128,64},{192,128},{256,192},{320,256},{384,320},{4... | collective-permute-start | bytes 1843208 | tf_op jit(solution)/shard_map/ppermute | solution.py:401
  152.2 17.4 %collective-permute-start.7 = (bf16[96,3200]{1,0:T(8,128)(2,1)S(1)}, bf16[96,3200]{1,0:T(8,128)(2,1)S(1)}, u32[]{:S(2)}, u32[]{:S(2)}) collective-permute-start(bf16[96,3200]{1,0:T(8,128)(2,1)S(1)} %all_gather.3.own_ref), channel_id=1, source_target_pairs={{0,64},{64,128},{128,192},{192,256},{256,320},{320,384},{384,448},... | collective-permute-start | bytes 1843208 | tf_op jit(solution)/shard_map/ppermute | solution.py:401
  164.2 9.8 %collective-permute-start.10 = (bf16[48,3200]{1,0:T(8,128)(2,1)S(1)}, bf16[48,3200]{1,0:T(8,128)(2,1)S(1)}, u32[]{:S(2)}, u32[]{:S(2)}) collective-permute-start(bf16[48,3200]{1,0:T(8,128)(2,1)S(1)} %slice.9), channel_id=1, source_target_pairs={{0,960},{64,0},{128,64},{192,128},{256,192},{320,256},{384,320},{4... | collective-permute-start | bytes 921608 | tf_op jit(solution)/shard_map/ppermute | solution.py:401
  169.6 9.6 %collective-permute-start.9 = (bf16[48,3200]{1,0:T(8,128)(2,1)S(1)}, bf16[48,3200]{1,0:T(8,128)(2,1)S(1)}, u32[]{:S(2)}, u32[]{:S(2)}) collective-permute-start(bf16[48,3200]{1,0:T(8,128)(2,1)S(1)} %slice.8), channel_id=1, source_target_pairs={{0,64},{64,128},{128,192},{192,256},{256,320},{320,384},{384,448},... | collective-permute-start | bytes 921608 | tf_op jit(solution)/shard_map/ppermute | solution.py:401
  182.5 23.9 %copy-start.11 = (s32[128,8]{0,1:T(8,128)S(1)}, s32[128,8]{0,1:T(8,128)}, u32[]{:S(2)}) copy-start(s32[128,8]{0,1:T(8,128)} %param.10) | copy-start | bytes 12292
  182.5 23.9 %copy-start.13 = (f32[128,8]{0,1:T(8,128)S(1)}, f32[128,8]{0,1:T(8,128)}, u32[]{:S(2)}) copy-start(f32[128,8]{0,1:T(8,128)} %param.11) | copy-start | bytes 12292
  182.5 23.9 %all-to-all-start.1 = ((bf16[64,24,128]{2,1,0:T(8,128)(2,1)}), bf16[64,24,128]{2,1,0:T(8,128)(2,1)S(1)}, u32[]{:S(2)}, u32[]{:S(2)}) async-start(bf16[64,24,128]{2,1,0:T(8,128)(2,1)} %shard_map.132), calls=%async_computation.1 | async-start | bytes 786432 | tf_op jit(solution)/shard_map/all_to_all | solution.py:473
  192.6 1.4 copy-start
  194.0 0.9 copy-start.9
  206.4 1.7 copy-start.1

commit v6 on v5

--- a/solution.py
+++ b/solution.py
@@ -322,10 +322,14 @@
         )
 
 
-def choose_kernel(plan_ref, chosen_ref, scored_ref):
-    experts = plan_ref.shape[0] // 2
-    token_count = plan_ref.shape[1]
+def combine_kernel(
+    back_ref, plan_ref, routes_ref, weight_ref, mixed_ref, input_ref, score_ref, chosen_ref
+):
+    top_count, token_count = routes_ref.shape
+    experts = back_ref.shape[0]
+    width = mixed_ref.shape[0]
     rows = experts * GROUP
+    back = back_ref[...].reshape(rows, LANES)
     plan = plan_ref[...].T
     rank, scale = plan[:, :experts], plan[:, experts:]
     spread = one_zero(expert_of_row(iota((experts, rows), 1), iota((experts, rows), 0)))
@@ -340,17 +344,7 @@
     for index in range(2):
         place = (2 * WEIGHT_PARTS + index) * token_count
         chosen_ref[place : place + token_count] = jnp.where(tile == 2 + index, taken, 0.0).astype(BF16)
-    scored_ref[...] = jnp.where(tile == 1, taken, 0.0).astype(BF16)
-
-
-def combine_kernel(
-    back_ref, chosen_ref, scored_ref, routes_ref, weight_ref, mixed_ref, input_ref, score_ref
-):
-    top_count, token_count = routes_ref.shape
-    experts = back_ref.shape[0]
-    width = mixed_ref.shape[0]
-    rows = experts * GROUP
-    back = back_ref[...].reshape(rows, LANES)
+    scored = jnp.where(tile == 1, taken, 0.0).astype(BF16)
     values = dot(chosen_ref[...], back)
     blocks = [values[i * token_count : (i + 1) * token_count] for i in range(2 * WEIGHT_PARTS + 2)]
     low, high = sum(blocks[:WEIGHT_PARTS]), sum(blocks[WEIGHT_PARTS : 2 * WEIGHT_PARTS])
@@ -362,11 +356,9 @@
         ref[LANES:] = high.T[: width - LANES].astype(BF16)
     lane_of_part = iota((8, LANES), 1) - SCORE_LANE == iota((8, LANES), 0)
     row_score = dot(one_zero(lane_of_part & (iota((8, LANES), 0) < 3)), back, CONTRACT_LAST)
-    here = expert_of_row(iota((experts, rows), 1), iota((experts, rows), 0))
-    spread = jnp.concatenate(
-        [jnp.where(here, row_score[i : i + 1], 0.0).astype(BF16) for i in range(3)], axis=0
-    )
-    by_expert = dot(spread, scored_ref[...], CONTRACT_LAST)
+    spread = spread.astype(F32)
+    spread = jnp.concatenate([(spread * row_score[i : i + 1]).astype(BF16) for i in range(3)], axis=0)
+    by_expert = dot(spread, scored, CONTRACT_LAST)
     by_expert = sum(by_expert[i * experts : (i + 1) * experts] for i in range(3))
     expert = iota((experts, token_count), 0)
     for k in range(top_count):
@@ -482,22 +474,13 @@
     )(member, *pieces, token_rows, scaled_rows)
     down_grad = down_grad.T
     token_shape = shape((width, token_count), BF16)
-    slots = experts * GROUP
-    chosen, scored = kernel_call(
-        choose_kernel,
-        (
-            shape(((2 * WEIGHT_PARTS + 2) * token_count, slots), BF16),
-            shape((token_count, slots), BF16),
-        ),
-        200_000_000,
-        3_000_000,
-    )(plan)
     mixed, input_gradient, route_gradient = kernel_call(
         combine_kernel,
         (token_shape, token_shape, shape(arguments[0].shape, F32)),
         500_000_000,
         1_000_000,
-    )(returned, chosen, scored, arguments[0], arguments[1])
+        scratch=[pltpu.VMEM(((2 * WEIGHT_PARTS + 2) * token_count, experts * GROUP), BF16)],
+    )(returned, plan, arguments[0], arguments[1])
     return (
         mixed.T,
         input_gradient.T,

time: 211 us -> 207 us (0.981)
  local copies, waits for them, and re-layouts: 11.5 us -> 3.07 us
  waiting for transfers between devices: 72.7 us -> 75.9 us
    unnamed x34 -> x26, local copies, waits for them, and re-layouts: 11.4 us -> 3.03 us
    all_to_all x1, waiting for transfers between devices: 9.41 us -> 12.5 us  [per_device(): lax.all_to_all(back, 'dp', split_axis=0, concat_axis=0, tiled=True)]
where the time goes in v6:
time: 207 us; the launch traced here: 206 us
  starting transfers between devices  87.1 us (42%)
  waiting for transfers between devices  75.9 us (37%)
  blocking collectives  25.9 us (13%)
  Pallas kernels  13 us (6%)
  local copies, waits for them, and re-layouts  3.07 us (1%)
    ppermute x11, starting transfers between devices, shifted(): lax.ppermute(block, 'expert', [(i, (i + distance) % parts) for i in range...  57.8 us
    ppermute x11, waiting for transfers between devices, shifted(): lax.ppermute(block, 'expert', [(i, (i + distance) % parts) for i in range...  48.6 us
    all_gather x1, blocking collectives, per_device(): lax.all_gather(share, 'expert', axis=0, tiled=True, axis_index_groups=gro...  25.9 us
    all_to_all x1, starting transfers between devices, per_device(): lax.all_to_all(send, 'dp', split_axis=0, concat_axis=0, tiled=True)  18.4 us
    all_to_all x1, waiting for transfers between devices, per_device(): lax.all_to_all(send, 'dp', split_axis=0, concat_axis=0, tiled=True)  14.7 us
    all_to_all x1, waiting for transfers between devices, per_device(): lax.all_to_all(back, 'dp', split_axis=0, concat_axis=0, tiled=True)  12.5 us
    all_to_all x1, starting transfers between devices, per_device(): lax.all_to_all(back, 'dp', split_axis=0, concat_axis=0, tiled=True)  11 us
  transfers between devices with their start and end apart: 13, of which 10 were waited for; matrix products, arithmetic and copies ran while one was open for 0% of the time, Pallas kernels for 1%

profile of v6, /device:TPU:1, one launch (start us, length us, event | category | flops | bytes accessed | tf_op | source)
XLA Modules:
  0.0 205.9 jit_solution(17300987302590418253)
XLA Ops:
  1.3 0.8 copy-done.8
  2.2 0.8 copy-done.9
  3.0 2.4 %shard_map.127 = (bf16[64,24,128]{2,1,0:T(8,128)(2,1)}, f32[128,128]{1,0:T(8,128)S(1)}) custom-call(s32[8,128]{1,0:T(8,128)S(1)} %bitcast.27, f32[8,128]{1,0:T(8,128)S(1)} %bitcast.29, s32[1,64]{1,0:T(1,128)S(1)} %bitcast.31, bf16[224,128]{1,0:T(8,128)(2,1)S(1)} %bitcast.25, bf16[224,128]{1,0:T(8,128)(2,1)S(1)} %bitcast.26), custom_call_target="tpu_custom_call" | custom-call | flops 300000000 | bytes 1000000 | tf_op jit(solution)/shard_map/pallas_call | solution.py:413
  5.4 18.4 %all-to-all-start = ((bf16[64,24,128]{2,1,0:T(8,128)(2,1)}), bf16[64,24,128]{2,1,0:T(8,128)(2,1)S(1)}, u32[]{:S(2)}, u32[]{:S(2)}) async-start(bf16[64,24,128]{2,1,0:T(8,128)(2,1)} %get-tuple-element.27), calls=%async_computation | async-start | bytes 786432 | tf_op jit(solution)/shard_map/all_to_all | solution.py:421
  23.8 14.7 %all-to-all-done.recv_ref = bf16[64,24,128]{2,1,0:T(8,128)(2,1)S(1)} async-done(((bf16[64,24,128]{2,1,0:T(8,128)(2,1)}), bf16[64,24,128]{2,1,0:T(8,128)(2,1)S(1)}, u32[]{:S(2)}, u32[]{:S(2)}) %all-to-all-start) | async-done | bytes 393248 | tf_op jit(solution)/shard_map/all_to_all | solution.py:421
  38.5 2.4 %shard_map.128 = (bf16[96,3072]{1,0:T(8,128)(2,1)S(1)}, bf16[96,3072]{1,0:T(8,128)(2,1)S(1)}, bf16[96,3072]{1,0:T(8,128)(2,1)S(1)}, bf16[48,3072]{1,0:T(8,128)(2...) custom-call(s32[1]{0:T(128)} %bitcast.place_ref, ...), custom_call_target="tpu_custom_call" | custom-call | flops 700000000 | bytes 4500000 | tf_op jit(solution)/shard_map/pallas_call | solution.py:422
  40.9 0.7 copy-done.6
  41.6 1.9 collective-permute-start
  43.5 11.2 %collective-permute-start.1 = (bf16[96,3072]{1,0:T(8,128)(2,1)S(1)}, bf16[96,3072]{1,0:T(8,128)(2,1)S(1)}, u32[]{:S(2)}, u32[]{:S(2)}) collective-permute-start(bf16[96,3072]{1,0:T(8,128)(2,1)S(1)} %get-tuple-element.30), channel_id=1, source_target_pairs={{0,960},{64,0},{128,64},{192,128},{256,192},{320,256},{384,320},{4... | collective-permute-start | bytes 1769480 | tf_op jit(solution)/shard_map/ppermute | solution.py:393
  54.8 11.4 %collective-permute-done.from_left_ref = bf16[96,3072]{1,0:T(8,128)(2,1)S(1)} collective-permute-done((bf16[96,3072]{1,0:T(8,128)(2,1)S(1)}, bf16[96,3072]{1,0:T(8,128)(2,1)S(1)}, u32[]{:S(2)}, u32[]{:S(2)}) %collective-permute-start) | collective-permute-done | bytes 589856 | tf_op jit(solution)/shard_map/ppermute | solution.py:393
  66.2 0.9 collective-permute-done.1.from_right_ref
  67.2 1.9 collective-permute-start.2
  69.1 5.3 %collective-permute-start.3 = (bf16[48,3072]{1,0:T(8,128)(2,1)S(1)}, bf16[48,3072]{1,0:T(8,128)(2,1)S(1)}, u32[]{:S(2)}, u32[]{:S(2)}) collective-permute-start(bf16[48,3072]{1,0:T(8,128)(2,1)S(1)} %get-tuple-element.34), channel_id=1, source_target_pairs={{0,960},{64,0},{128,64},{192,128},{256,192},{320,256},{384,320},{4... | collective-permute-start | bytes 884744 | tf_op jit(solution)/shard_map/ppermute | solution.py:393
  74.5 4.2 %collective-permute-done.2.far_left_ref = bf16[48,3072]{1,0:T(8,128)(2,1)S(1)} collective-permute-done((bf16[48,3072]{1,0:T(8,128)(2,1)S(1)}, bf16[48,3072]{1,0:T(8,128)(2,1)S(1)}, u32[]{:S(2)}, u32[]{:S(2)}) %collective-permute-start.2) | collective-permute-done | bytes 294944 | tf_op jit(solution)/shard_map/ppermute | solution.py:393
  78.6 0.9 collective-permute-done.3.far_right_ref
  79.9 2.2 %collective-permute-start.4 = (bf16[24,3072]{1,0:T(8,128)(2,1)S(1)}, bf16[24,3072]{1,0:T(8,128)(2,1)S(1)}, u32[]{:S(2)}, u32[]{:S(2)}) collective-permute-start(bf16[24,3072]{1,0:T(8,128)(2,1)S(1)} %get-tuple-element.36), channel_id=1, source_target_pairs={{0,256},{64,320},{128,384},{192,448},{256,512},{320,576},{384,640}... | collective-permute-start | bytes 442376 | tf_op jit(solution)/shard_map/ppermute | solution.py:393
  82.2 6.9 %collective-permute-start.5 = (bf16[24,3072]{1,0:T(8,128)(2,1)S(1)}, bf16[24,3072]{1,0:T(8,128)(2,1)S(1)}, u32[]{:S(2)}, u32[]{:S(2)}) collective-permute-start(bf16[24,3072]{1,0:T(8,128)(2,1)S(1)} %get-tuple-element.37), channel_id=1, source_target_pairs={{0,768},{64,832},{128,896},{192,960},{256,0},{320,64},{384,128},{4... | collective-permute-start | bytes 442376 | tf_op jit(solution)/shard_map/ppermute | solution.py:393
  89.1 5.5 %collective-permute-start.6 = (bf16[24,3072]{1,0:T(8,128)(2,1)S(1)}, bf16[24,3072]{1,0:T(8,128)(2,1)S(1)}, u32[]{:S(2)}, u32[]{:S(2)}) collective-permute-start(bf16[24,3072]{1,0:T(8,128)(2,1)S(1)} %get-tuple-element.38), channel_id=1, source_target_pairs={{0,512},{64,576},{128,640},{192,704},{256,768},{320,832},{384,896}... | collective-permute-start | bytes 442376 | tf_op jit(solution)/shard_map/ppermute | solution.py:393
  94.6 13.5 %collective-permute-done.6.across_ref = bf16[24,3072]{1,0:T(8,128)(2,1)S(1)} collective-permute-done((bf16[24,3072]{1,0:T(8,128)(2,1)S(1)}, bf16[24,3072]{1,0:T(8,128)(2,1)S(1)}, u32[]{:S(2)}, u32[]{:S(2)}) %collective-permute-start.6) | collective-permute-done | bytes 147488 | tf_op jit(solution)/shard_map/ppermute | solution.py:393
  108.3 25.9 %all_gather.3.own_ref = bf16[96,3200]{1,0:T(8,128)(2,1)S(1)} all-gather(bf16[24,3200]{1,0:T(8,128)(2,1)S(1)} %shard_map.131), channel_id=1, replica_groups={{0,256,512,768},{64,320,576,832},{128,384,640,896},{192,448,704,960},{1..., dimensions={0}, use_global_device_ids=true | all-gather | bytes 768000 | tf_op jit(solution)/shard_map/all_gather | solution.py:452
  134.2 13.4 %collective-permute-start.8 = (bf16[96,3200]{1,0:T(8,128)(2,1)S(1)}, bf16[96,3200]{1,0:T(8,128)(2,1)S(1)}, u32[]{:S(2)}, u32[]{:S(2)}) collective-permute-start(bf16[96,3200]{1,0:T(8,128)(2,1)S(1)} %all_gather.3.own_ref), channel_id=1, source_target_pairs={{0,960},{64,0},{128,64},{192,128},{256,192},{320,256},{384,320},{4... | collective-permute-start | bytes 1843208 | tf_op jit(solution)/shard_map/ppermute | solution.py:393
  147.6 1.9 collective-permute-start.7
  149.6 10.1 %collective-permute-done.8.right_ref = bf16[96,3200]{1,0:T(8,128)(2,1)S(1)} collective-permute-done((bf16[96,3200]{1,0:T(8,128)(2,1)S(1)}, bf16[96,3200]{1,0:T(8,128)(2,1)S(1)}, u32[]{:S(2)}, u32[]{:S(2)}) %collective-permute-start.8) | collective-permute-done | bytes 614432 | tf_op jit(solution)/shard_map/ppermute | solution.py:393
  159.7 5.5 %collective-permute-start.10 = (bf16[48,3200]{1,0:T(8,128)(2,1)S(1)}, bf16[48,3200]{1,0:T(8,128)(2,1)S(1)}, u32[]{:S(2)}, u32[]{:S(2)}) collective-permute-start(bf16[48,3200]{1,0:T(8,128)(2,1)S(1)} %slice.9), channel_id=1, source_target_pairs={{0,960},{64,0},{128,64},{192,128},{256,192},{320,256},{384,320},{4... | collective-permute-start | bytes 921608 | tf_op jit(solution)/shard_map/ppermute | solution.py:393
  165.2 1.9 collective-permute-start.9
  167.2 2.6 %collective-permute-done.10.far_right_ref = bf16[48,3200]{1,0:T(8,128)(2,1)S(1)} collective-permute-done((bf16[48,3200]{1,0:T(8,128)(2,1)S(1)}, bf16[48,3200]{1,0:T(8,128)(2,1)S(1)}, u32[]{:S(2)}, u32[]{:S(2)}) %collective-permute-start.10) | collective-permute-done | bytes 307232 | tf_op jit(solution)/shard_map/ppermute | solution.py:393
  169.7 5.1 %collective-permute-done.9.far_left_ref = bf16[48,3200]{1,0:T(8,128)(2,1)S(1)} collective-permute-done((bf16[48,3200]{1,0:T(8,128)(2,1)S(1)}, bf16[48,3200]{1,0:T(8,128)(2,1)S(1)}, u32[]{:S(2)}, u32[]{:S(2)}) %collective-permute-start.9) | collective-permute-done | bytes 307232 | tf_op jit(solution)/shard_map/ppermute | solution.py:393
  174.8 3.3 %shard_map.132 = bf16[64,24,128]{2,1,0:T(8,128)(2,1)} custom-call(s32[1]{0:T(128)} %bitcast.place_ref, bf16[96,3200]{1,0:T(8,128)(2,1)S(1)} %all_gather.3.own_ref, bf16[96,3200]{1,0:T(8,128)(2,1)S(1)} %collective-permute-done.7.left_ref, bf16[96,3200]{1,0:T(8,128)(2,1)S(1)} %collective-permute-done.8.right_ref, ...), custom_call_target="tpu_custom_call" | custom-call | flops 700000000 | bytes 4500000 | tf_op jit(solution)/shard_map/pallas_call | solution.py:457
  178.2 11.0 %all-to-all-start.1 = ((bf16[64,24,128]{2,1,0:T(8,128)(2,1)}), bf16[64,24,128]{2,1,0:T(8,128)(2,1)S(1)}, u32[]{:S(2)}, u32[]{:S(2)}) async-start(bf16[64,24,128]{2,1,0:T(8,128)(2,1)} %shard_map.132), calls=%async_computation.1 | async-start | bytes 786432 | tf_op jit(solution)/shard_map/all_to_all | solution.py:465
  189.2 2.0 shard_map.134
  191.2 12.5 %all-to-all-done.1.back_ref = bf16[64,24,128]{2,1,0:T(8,128)(2,1)S(1)} async-done(((bf16[64,24,128]{2,1,0:T(8,128)(2,1)}), bf16[64,24,128]{2,1,0:T(8,128)(2,1)S(1)}, u32[]{:S(2)}, u32[]{:S(2)}) %all-to-all-start.1) | async-done | bytes 393248 | tf_op jit(solution)/shard_map/all_to_all | solution.py:465
  203.8 2.1 %shard_map.133 = (bf16[224,128]{1,0:T(8,128)(2,1)}, bf16[224,128]{1,0:T(8,128)(2,1)}, f32[8,128]{1,0:T(8,128)}) custom-call(bf16[64,24,128]{2,1,0:T(8,128)(2,1)S(1)} %all-to-all-done.1.back_ref, f32[128,128]{1,0:T(8,128)S(1)} %get-tuple-element.39.plan_ref, s32[8,128]{1,0:T(8,128)S(1)} %bitcast.28, f32[8,128]{1,0:T(8,128)S(1)} %bitcast.30), custom_call_target="tpu_custom_call" | custom-call | flops 500000000 | bytes 1000000 | tf_op jit(solution)/shard_map/pallas_call | solution.py:477
  (31 shorter events, 1.5 us)
Async XLA Ops:
  0.6 0.7 copy-start.11
  0.6 0.7 copy-start.10
  0.7 0.7 copy-start.12
  1.3 0.8 copy-start.8
  2.2 0.8 copy-start.9
  3.0 35.5 %copy-start.1 = (bf16[1,224,1024]{2,1,0:T(8,128)(2,1)S(1)}, bf16[1,224,1024]{2,1,0:T(8,128)(2,1)}, u32[]{:S(2)}) copy-start(bf16[1,224,1024]{2,1,0:T(8,128)(2,1)} %param.14) | copy-start | bytes 1376260
  3.0 35.5 %copy-start.2 = (bf16[1,1024,224]{1,2,0:T(8,128)(2,1)S(1)}, bf16[1,1024,224]{1,2,0:T(8,128)(2,1)}, u32[]{:S(2)}) copy-start(bf16[1,1024,224]{1,2,0:T(8,128)(2,1)} %param.15) | copy-start | bytes 1376260
  5.4 33.1 %copy-start = (bf16[1,224,1024]{2,1,0:T(8,128)(2,1)S(1)}, bf16[1,224,1024]{2,1,0:T(8,128)(2,1)}, u32[]{:S(2)}) copy-start(bf16[1,224,1024]{2,1,0:T(8,128)(2,1)} %param.13) | copy-start | bytes 1376260
  5.4 33.1 %all-to-all-start = ((bf16[64,24,128]{2,1,0:T(8,128)(2,1)}), bf16[64,24,128]{2,1,0:T(8,128)(2,1)S(1)}, u32[]{:S(2)}, u32[]{:S(2)}) async-start(bf16[64,24,128]{2,1,0:T(8,128)(2,1)} %get-tuple-element.27), calls=%async_computation | async-start | bytes 786432 | tf_op jit(solution)/shard_map/all_to_all | solution.py:421
  40.9 0.7 copy-start.6
  41.6 25.6 %copy-start.4 = (bf16[384,224]{1,0:T(8,128)(2,1)}, bf16[384,224]{1,0:T(8,128)(2,1)S(1)}, u32[]{:S(2)}) copy-start(bf16[384,224]{1,0:T(8,128)(2,1)S(1)} %get-tuple-element.43.tok_ref) | copy-start | bytes 516100
  41.6 24.6 %collective-permute-start = (bf16[96,3072]{1,0:T(8,128)(2,1)S(1)}, bf16[96,3072]{1,0:T(8,128)(2,1)S(1)}, u32[]{:S(2)}, u32[]{:S(2)}) collective-permute-start(bf16[96,3072]{1,0:T(8,128)(2,1)S(1)} %get-tuple-element.29), channel_id=1, source_target_pairs={{0,64},{64,128},{128,192},{192,256},{256,320},{320,384},{384,448},... | collective-permute-start | bytes 1769480 | tf_op jit(solution)/shard_map/ppermute | solution.py:393
  43.5 23.5 %collective-permute-start.1 = (bf16[96,3072]{1,0:T(8,128)(2,1)S(1)}, bf16[96,3072]{1,0:T(8,128)(2,1)S(1)}, u32[]{:S(2)}, u32[]{:S(2)}) collective-permute-start(bf16[96,3072]{1,0:T(8,128)(2,1)S(1)} %get-tuple-element.30), channel_id=1, source_target_pairs={{0,960},{64,0},{128,64},{192,128},{256,192},{320,256},{384,320},{4... | collective-permute-start | bytes 1769480 | tf_op jit(solution)/shard_map/ppermute | solution.py:393
  67.2 11.4 %collective-permute-start.2 = (bf16[48,3072]{1,0:T(8,128)(2,1)S(1)}, bf16[48,3072]{1,0:T(8,128)(2,1)S(1)}, u32[]{:S(2)}, u32[]{:S(2)}) collective-permute-start(bf16[48,3072]{1,0:T(8,128)(2,1)S(1)} %get-tuple-element.33), channel_id=1, source_target_pairs={{0,64},{64,128},{128,192},{192,256},{256,320},{320,384},{384,448},... | collective-permute-start | bytes 884744 | tf_op jit(solution)/shard_map/ppermute | solution.py:393
  69.1 10.4 %collective-permute-start.3 = (bf16[48,3072]{1,0:T(8,128)(2,1)S(1)}, bf16[48,3072]{1,0:T(8,128)(2,1)S(1)}, u32[]{:S(2)}, u32[]{:S(2)}) collective-permute-start(bf16[48,3072]{1,0:T(8,128)(2,1)S(1)} %get-tuple-element.34), channel_id=1, source_target_pairs={{0,960},{64,0},{128,64},{192,128},{256,192},{320,256},{384,320},{4... | collective-permute-start | bytes 884744 | tf_op jit(solution)/shard_map/ppermute | solution.py:393
  79.9 14.7 %collective-permute-start.4 = (bf16[24,3072]{1,0:T(8,128)(2,1)S(1)}, bf16[24,3072]{1,0:T(8,128)(2,1)S(1)}, u32[]{:S(2)}, u32[]{:S(2)}) collective-permute-start(bf16[24,3072]{1,0:T(8,128)(2,1)S(1)} %get-tuple-element.36), channel_id=1, source_target_pairs={{0,256},{64,320},{128,384},{192,448},{256,512},{320,576},{384,640}... | collective-permute-start | bytes 442376 | tf_op jit(solution)/shard_map/ppermute | solution.py:393
  82.2 12.4 %collective-permute-start.5 = (bf16[24,3072]{1,0:T(8,128)(2,1)S(1)}, bf16[24,3072]{1,0:T(8,128)(2,1)S(1)}, u32[]{:S(2)}, u32[]{:S(2)}) collective-permute-start(bf16[24,3072]{1,0:T(8,128)(2,1)S(1)} %get-tuple-element.37), channel_id=1, source_target_pairs={{0,768},{64,832},{128,896},{192,960},{256,0},{320,64},{384,128},{4... | collective-permute-start | bytes 442376 | tf_op jit(solution)/shard_map/ppermute | solution.py:393
  89.1 19.0 %collective-permute-start.6 = (bf16[24,3072]{1,0:T(8,128)(2,1)S(1)}, bf16[24,3072]{1,0:T(8,128)(2,1)S(1)}, u32[]{:S(2)}, u32[]{:S(2)}) collective-permute-start(bf16[24,3072]{1,0:T(8,128)(2,1)S(1)} %get-tuple-element.38), channel_id=1, source_target_pairs={{0,512},{64,576},{128,640},{192,704},{256,768},{320,832},{384,896}... | collective-permute-start | bytes 442376 | tf_op jit(solution)/shard_map/ppermute | solution.py:393
  134.2 25.5 %collective-permute-start.8 = (bf16[96,3200]{1,0:T(8,128)(2,1)S(1)}, bf16[96,3200]{1,0:T(8,128)(2,1)S(1)}, u32[]{:S(2)}, u32[]{:S(2)}) collective-permute-start(bf16[96,3200]{1,0:T(8,128)(2,1)S(1)} %all_gather.3.own_ref), channel_id=1, source_target_pairs={{0,960},{64,0},{128,64},{192,128},{256,192},{320,256},{384,320},{4... | collective-permute-start | bytes 1843208 | tf_op jit(solution)/shard_map/ppermute | solution.py:393
  147.6 17.6 %collective-permute-start.7 = (bf16[96,3200]{1,0:T(8,128)(2,1)S(1)}, bf16[96,3200]{1,0:T(8,128)(2,1)S(1)}, u32[]{:S(2)}, u32[]{:S(2)}) collective-permute-start(bf16[96,3200]{1,0:T(8,128)(2,1)S(1)} %all_gather.3.own_ref), channel_id=1, source_target_pairs={{0,64},{64,128},{128,192},{192,256},{256,320},{320,384},{384,448},... | collective-permute-start | bytes 1843208 | tf_op jit(solution)/shard_map/ppermute | solution.py:393
  159.7 15.1 %copy-start.3 = (bf16[1,1024,224]{1,2,0:T(8,128)(2,1)S(1)}, bf16[1,1024,224]{1,2,0:T(8,128)(2,1)}, u32[]{:S(2)}) copy-start(bf16[1,1024,224]{1,2,0:T(8,128)(2,1)} %param.15) | copy-start | bytes 1376260
  159.7 10.0 %collective-permute-start.10 = (bf16[48,3200]{1,0:T(8,128)(2,1)S(1)}, bf16[48,3200]{1,0:T(8,128)(2,1)S(1)}, u32[]{:S(2)}, u32[]{:S(2)}) collective-permute-start(bf16[48,3200]{1,0:T(8,128)(2,1)S(1)} %slice.9), channel_id=1, source_target_pairs={{0,960},{64,0},{128,64},{192,128},{256,192},{320,256},{384,320},{4... | collective-permute-start | bytes 921608 | tf_op jit(solution)/shard_map/ppermute | solution.py:393
  165.2 9.6 %collective-permute-start.9 = (bf16[48,3200]{1,0:T(8,128)(2,1)S(1)}, bf16[48,3200]{1,0:T(8,128)(2,1)S(1)}, u32[]{:S(2)}, u32[]{:S(2)}) collective-permute-start(bf16[48,3200]{1,0:T(8,128)(2,1)S(1)} %slice.8), channel_id=1, source_target_pairs={{0,64},{64,128},{128,192},{192,256},{256,320},{320,384},{384,448},... | collective-permute-start | bytes 921608 | tf_op jit(solution)/shard_map/ppermute | solution.py:393
  178.1 11.0 %copy-start.5 = (bf16[384,224]{1,0:T(8,128)(2,1)S(1)}, bf16[384,224]{1,0:T(8,128)(2,1)}, u32[]{:S(2)}) copy-start(bf16[384,224]{1,0:T(8,128)(2,1)} %copy-done.4) | copy-start | bytes 516100
  178.2 11.0 %copy-start.7 = (bf16[384,224]{1,0:T(8,128)(2,1)S(1)}, bf16[384,224]{1,0:T(8,128)(2,1)}, u32[]{:S(2)}) copy-start(bf16[384,224]{1,0:T(8,128)(2,1)} %copy-done.6) | copy-start | bytes 516100
  178.2 25.6 %all-to-all-start.1 = ((bf16[64,24,128]{2,1,0:T(8,128)(2,1)}), bf16[64,24,128]{2,1,0:T(8,128)(2,1)S(1)}, u32[]{:S(2)}, u32[]{:S(2)}) async-start(bf16[64,24,128]{2,1,0:T(8,128)(2,1)} %shard_map.132), calls=%async_computation.1 | async-start | bytes 786432 | tf_op jit(solution)/shard_map/all_to_all | solution.py:465

commit v7 on v4

--- a/solution.py
+++ b/solution.py
@@ -13,8 +13,9 @@
 SOURCES = 16
 RING = 4
 SCORE_LANE = 96
+WEIGHT_PARTS = 2
+PLACE_BITS = 4
 VMEM_LIMIT = 24 * 1024 * 1024
-WHOLE_VMEM = 63 * 1024 * 1024
 
 F32 = jnp.float32
 BF16 = jnp.bfloat16
@@ -66,6 +67,11 @@
     within = sorted_row - per_tile * tile
     source = lax.shift_right_logical(within * 43, 8)
     return one_zero(sent_row == within + (GROUP - CAP) * source + CAP * tile)
+
+
+def member_at(base, place_ref, step):
+    sign = 1 - 2 * lax.shift_right_logical(place_ref[0], PLACE_BITS)
+    return (base + sign * step) & (RING - 1)
 
 
 def fetch(sources, targets, sems):
@@ -176,7 +182,7 @@
             (RING - 1, ((to_left_ref, 0), (previous_ref, 0))),
             (0, ((own_ref, 0), (own_ref, half))),
         ):
-            member = (place_ref[0] + step) & (RING - 1)
+            member = member_at(place_ref[0], place_ref, step)
             begin = pl.multiple_of(member * held, held)
             value = dot(rows_ref[pl.ds(begin, held)], ref[...]).astype(BF16)
             for part, (out_ref, start) in enumerate(pieces):
@@ -214,7 +220,7 @@
     split = columns // 2
 
     def chunk(step, part):
-        member = (lax.shift_right_logical(place_ref[0], 2) + step) & (RING - 1)
+        member = member_at(lax.shift_right_logical(place_ref[0], 2), place_ref, step)
         begin = pl.multiple_of(member * share, share)
         return window_ref[pl.ds(begin, share), part].astype(BF16)
 
@@ -278,7 +284,7 @@
         (far_left_ref, RING // 2, 0),
         (far_right_ref, RING // 2, half),
     ):
-        member = (place_ref[0] + step) & (RING - 1)
+        member = member_at(place_ref[0], place_ref, step)
         begin = pl.multiple_of(member * held + start, half)
         full_ref[pl.ds(begin, ref.shape[0])] = ref[...]
 
@@ -351,38 +357,44 @@
         )
 
 
-def combine_kernel(back_ref, plan_ref, routes_ref, weight_ref, mixed_ref, input_ref, score_ref):
+def combine_kernel(
+    back_ref, plan_ref, routes_ref, weight_ref, mixed_ref, input_ref, score_ref, chosen_ref
+):
     top_count, token_count = routes_ref.shape
-    experts = plan_ref.shape[0] // 2
+    experts = back_ref.shape[0]
     width = mixed_ref.shape[0]
     rows = experts * GROUP
     back = back_ref[...].reshape(rows, LANES)
     plan = plan_ref[...].T
     rank, scale = plan[:, :experts], plan[:, experts:]
     spread = one_zero(expert_of_row(iota((experts, rows), 1), iota((experts, rows), 0)))
-    tile, slot = tile_and_slot(iota((token_count, rows), 1))
+    tile, slot = tile_and_slot(iota((1, rows), 1))
     taken = dot(rank.astype(BF16), spread) == slot.astype(F32)
-    mixed = [jnp.zeros((token_count, LANES), F32) for _ in range(2)]
-    for part in three_parts(scale):
-        row_scale = dot(part, spread)
+    for order, part in enumerate(three_parts(scale)[:WEIGHT_PARTS]):
+        row_scale = jnp.where(taken, dot(part, spread), 0.0)
         for index in range(2):
-            chosen = jnp.where(taken & (tile == index), row_scale, 0.0).astype(BF16)
-            mixed[index] = mixed[index] + dot(chosen, back)
+            place = (index * WEIGHT_PARTS + order) * token_count
+            chosen_ref[place : place + token_count] = jnp.where(tile == index, row_scale, 0.0).astype(BF16)
+    taken = jnp.where(taken, 1.0, 0.0)
+    for index in range(2):
+        place = (2 * WEIGHT_PARTS + index) * token_count
+        chosen_ref[place : place + token_count] = jnp.where(tile == 2 + index, taken, 0.0).astype(BF16)
+    scored = jnp.where(tile == 1, taken, 0.0).astype(BF16)
+    values = dot(chosen_ref[...], back)
+    blocks = [values[i * token_count : (i + 1) * token_count] for i in range(2 * WEIGHT_PARTS + 2)]
+    low, high = sum(blocks[:WEIGHT_PARTS]), sum(blocks[WEIGHT_PARTS : 2 * WEIGHT_PARTS])
     for ref, low, high in (
-        (mixed_ref, mixed[0], mixed[1]),
-        (
-            input_ref,
-            dot(one_zero(taken & (tile == 2)), back),
-            dot(one_zero(taken & (tile == 3)), back),
-        ),
+        (mixed_ref, low, high),
+        (input_ref, blocks[2 * WEIGHT_PARTS], blocks[2 * WEIGHT_PARTS + 1]),
     ):
         ref[:LANES] = low.T.astype(BF16)
         ref[LANES:] = high.T[: width - LANES].astype(BF16)
-    lane = iota((8, LANES), 1)
-    score_lanes = one_zero((lane >= SCORE_LANE) & (lane < SCORE_LANE + 3))
-    row_score = dot(score_lanes, back, CONTRACT_LAST)[:1]
-    routed = jnp.where(taken & (tile == 1), row_score, 0.0)
-    by_expert = sum(dot(spread, part, CONTRACT_LAST) for part in three_parts(routed))
+    lane_of_part = iota((8, LANES), 1) - SCORE_LANE == iota((8, LANES), 0)
+    row_score = dot(one_zero(lane_of_part & (iota((8, LANES), 0) < 3)), back, CONTRACT_LAST)
+    spread = spread.astype(F32)
+    spread = jnp.concatenate([(spread * row_score[i : i + 1]).astype(BF16) for i in range(3)], axis=0)
+    by_expert = dot(spread, scored, CONTRACT_LAST)
+    by_expert = sum(by_expert[i * experts : (i + 1) * experts] for i in range(3))
     expert = iota((experts, token_count), 0)
     for k in range(top_count):
         hit = routes_ref[k : k + 1] == expert
@@ -390,16 +402,16 @@
         score_ref[k : k + 1] = value / weight_ref[k : k + 1]
 
 
-def kernel_call(body, out_shape, flops, moved, spaces=None, scratch=(), limit=VMEM_LIMIT):
+def kernel_call(body, out_shape, flops, moved, spaces=None, scratch=()):
     places = {}
     if spaces is not None:
-        kinds = {"s": pltpu.SMEM, "v": pltpu.VMEM, "h": pltpu.HBM}
+        kinds = {"s": pltpu.SMEM, "v": pltpu.VMEM, "a": pl.ANY}
         places["in_specs"] = [pl.BlockSpec(memory_space=kinds[kind]) for kind in spaces]
     return pl.pallas_call(
         body,
         out_shape=out_shape,
         scratch_shapes=scratch,
-        compiler_params=pltpu.CompilerParams(vmem_limit_bytes=limit),
+        compiler_params=pltpu.CompilerParams(vmem_limit_bytes=VMEM_LIMIT),
         cost_estimate=pl.CostEstimate(flops=flops, bytes_accessed=moved, transcendentals=0),
         **places,
     )
@@ -412,8 +424,13 @@
 
 
 def shifted(block, distance):
-    parts = lax.axis_size("expert")
-    return lax.ppermute(block, "expert", [(i, (i + distance) % parts) for i in range(parts)])
+    parts, columns = lax.axis_size("expert"), lax.axis_size("dp")
+    route = [
+        (part * columns + column, (part + (1 - 2 * (column % 2)) * distance) % parts * columns + column)
+        for part in range(parts)
+        for column in range(columns)
+    ]
+    return lax.ppermute(block, ("expert", "dp"), route)
 
 
 def per_device(
@@ -430,7 +447,8 @@
     rows = shape((row_count, width), BF16)
     whole, halved = (shape((size, 3 * hidden), BF16) for size in (held, held // 2))
     groups = [list(range(i, parts, RING)) for i in range(RING)]
-    member = lax.axis_index("expert").astype(jnp.int32).reshape(1)
+    member = lax.axis_index("expert") + ((lax.axis_index("dp") & 1) << PLACE_BITS)
+    member = member.astype(jnp.int32).reshape(1)
     weights = (gate_weight[0], up_weight[0], down_weight[0].T)
     arguments = (routes.T, route_weights.T, owner_slots.reshape(1, experts), tokens.T, cotangent.T)
     send, plan = kernel_call(
@@ -438,8 +456,7 @@
         (exchanged, shape((2 * experts, token_count), F32)),
         300_000_000,
         1_000_000,
-        spaces="hhhhh",
-        limit=WHOLE_VMEM,
+        spaces="aaaaa",
         scratch=held_copies(*arguments),
     )(*arguments)
     arrived = lax.all_to_all(send, "dp", split_axis=0, concat_axis=0, tiled=True)
@@ -448,7 +465,7 @@
         (whole, whole, whole, halved, halved, rows, rows),
         700_000_000,
         4_500_000,
-        spaces="svhhh",
+        spaces="svaaa",
         scratch=held_copies(*weights),
     )(member, arrived, *weights)
     from_left, from_right = shifted(to_right, 1), shifted(to_left, -1)
@@ -489,7 +506,7 @@
         exchanged,
         700_000_000,
         4_500_000,
-        spaces="svvvvvhhh",
+        spaces="svvvvvaaa",
         scratch=[full, pltpu.VMEM((TILES, row_count, LANES), F32)] + held_copies(*weights),
     )(member, *pieces, *weights)
     returned = lax.all_to_all(back, "dp", split_axis=0, concat_axis=0, tiled=True)
@@ -509,6 +526,7 @@
         (token_shape, token_shape, shape(arguments[0].shape, F32)),
         500_000_000,
         1_000_000,
+        scratch=[pltpu.VMEM(((2 * WEIGHT_PARTS + 2) * token_count, experts * GROUP), BF16)],
     )(returned, plan, arguments[0], arguments[1])
     return (
         mixed.T,

time: 206 us -> 201 us (0.976)
  starting transfers between devices: 92.3 us -> 71.3 us
  waiting for transfers between devices: 67.8 us -> 85.7 us
    ppermute x12, waiting for transfers between devices: 40.6 us -> 58.4 us  [shifted(): return lax.ppermute(block, ('expert', 'dp'), route)]
    ppermute x12, starting transfers between devices: 62.8 us -> 46.6 us  [shifted(): return lax.ppermute(block, ('expert', 'dp'), route)]
    all_to_all x1, starting transfers between devices: 11.2 us -> 6.32 us  [per_device(): lax.all_to_all(back, 'dp', split_axis=0, concat_axis=0, tiled=True)]
  transfers between devices with their start and end apart: 14 -> 14, of which waited for: 14 -> 12; matrix products, arithmetic and copies ran while one was open for 0% -> 0% of each run, Pallas kernels for 1% -> 1%
where the time goes in v7:
time: 201 us; the launch traced here: 200 us
  waiting for transfers between devices  85.7 us (43%)
  starting transfers between devices  71.3 us (35%)
  blocking collectives  26.1 us (13%)
  Pallas kernels  13.1 us (7%)
  local copies, waits for them, and re-layouts  3.07 us (2%)
    ppermute x12, waiting for transfers between devices, shifted(): return lax.ppermute(block, ('expert', 'dp'), route)  58.4 us
    ppermute x12, starting transfers between devices, shifted(): return lax.ppermute(block, ('expert', 'dp'), route)  46.6 us
    all_gather x1, blocking collectives, per_device(): lax.all_gather(share, 'expert', axis=0, tiled=True, axis_index_groups=gro...  26.1 us
    all_to_all x1, starting transfers between devices, per_device(): lax.all_to_all(send, 'dp', split_axis=0, concat_axis=0, tiled=True)  18.4 us
    all_to_all x1, waiting for transfers between devices, per_device(): lax.all_to_all(send, 'dp', split_axis=0, concat_axis=0, tiled=True)  14.7 us
    all_to_all x1, waiting for transfers between devices, per_device(): lax.all_to_all(back, 'dp', split_axis=0, concat_axis=0, tiled=True)  12.5 us
    all_to_all x1, starting transfers between devices, per_device(): lax.all_to_all(back, 'dp', split_axis=0, concat_axis=0, tiled=True)  6.32 us
  transfers between devices with their start and end apart: 14, of which 12 were waited for; matrix products, arithmetic and copies ran while one was open for 0% of the time, Pallas kernels for 1%

profile of v7, /device:TPU:1, one launch (start us, length us, event | category | flops | bytes accessed | tf_op | source)
XLA Modules:
  0.0 200.2 jit_solution(1134946104897268908)
XLA Ops:
  3.0 2.4 %shard_map.127 = (bf16[64,24,128]{2,1,0:T(8,128)(2,1)}, f32[128,128]{1,0:T(8,128)S(1)}) custom-call(s32[8,128]{1,0:T(8,128)S(1)} %bitcast.27, f32[8,128]{1,0:T(8,128)S(1)} %bitcast.29, s32[1,64]{1,0:T(1,128)S(1)} %bitcast.31, bf16[224,128]{1,0:T(8,128)(2,1)S(1)} %bitcast.25, bf16[224,128]{1,0:T(8,128)(2,1)S(1)} %bitcast.26), custom_call_target="tpu_custom_call" | custom-call | flops 300000000 | bytes 1000000 | tf_op jit(solution)/shard_map/pallas_call | solution.py:454
  5.4 18.4 %all-to-all-start = ((bf16[64,24,128]{2,1,0:T(8,128)(2,1)}), bf16[64,24,128]{2,1,0:T(8,128)(2,1)S(1)}, u32[]{:S(2)}, u32[]{:S(2)}) async-start(bf16[64,24,128]{2,1,0:T(8,128)(2,1)} %get-tuple-element.30), calls=%async_computation | async-start | bytes 786432 | tf_op jit(solution)/shard_map/all_to_all | solution.py:462
  23.8 14.7 %all-to-all-done.recv_ref = bf16[64,24,128]{2,1,0:T(8,128)(2,1)S(1)} async-done(((bf16[64,24,128]{2,1,0:T(8,128)(2,1)}), bf16[64,24,128]{2,1,0:T(8,128)(2,1)S(1)}, u32[]{:S(2)}, u32[]{:S(2)}) %all-to-all-start) | async-done | bytes 393248 | tf_op jit(solution)/shard_map/all_to_all | solution.py:462
  38.5 2.4 %shard_map.128 = (bf16[96,3072]{1,0:T(8,128)(2,1)S(1)}, bf16[96,3072]{1,0:T(8,128)(2,1)S(1)}, bf16[96,3072]{1,0:T(8,128)(2,1)S(1)}, bf16[48,3072]{1,0:T(8,128)(2...) custom-call(s32[1]{0:T(128)} %bitcast.place_ref, ...), custom_call_target="tpu_custom_call" | custom-call | flops 700000000 | bytes 4500000 | tf_op jit(solution)/shard_map/pallas_call | solution.py:463
  41.6 11.2 %collective-permute-start = (bf16[96,3072]{1,0:T(8,128)(2,1)S(1)}, bf16[96,3072]{1,0:T(8,128)(2,1)S(1)}, u32[]{:S(2)}, u32[]{:S(2)}) collective-permute-start(bf16[96,3072]{1,0:T(8,128)(2,1)S(1)} %get-tuple-element.32), channel_id=1, source_target_pairs={{0,64},{1,961},{2,66},{3,963},{4,68},{5,965},{6,70},{7,967},{8,72}... | collective-permute-start | bytes 1769480 | tf_op jit(solution)/shard_map/ppermute | solution.py:433
  52.8 1.9 collective-permute-start.1
  54.8 8.3 %collective-permute-done.from_left_ref = bf16[96,3072]{1,0:T(8,128)(2,1)S(1)} collective-permute-done((bf16[96,3072]{1,0:T(8,128)(2,1)S(1)}, bf16[96,3072]{1,0:T(8,128)(2,1)S(1)}, u32[]{:S(2)}, u32[]{:S(2)}) %collective-permute-start) | collective-permute-done | bytes 589856 | tf_op jit(solution)/shard_map/ppermute | solution.py:433
  63.1 3.9 %collective-permute-done.1.from_right_ref = bf16[96,3072]{1,0:T(8,128)(2,1)S(1)} collective-permute-done((bf16[96,3072]{1,0:T(8,128)(2,1)S(1)}, bf16[96,3072]{1,0:T(8,128)(2,1)S(1)}, u32[]{:S(2)}, u32[]{:S(2)}) %collective-permute-start.1) | collective-permute-done | bytes 589856 | tf_op jit(solution)/shard_map/ppermute | solution.py:433
  67.1 3.9 %collective-permute-start.2 = (bf16[48,3072]{1,0:T(8,128)(2,1)S(1)}, bf16[48,3072]{1,0:T(8,128)(2,1)S(1)}, u32[]{:S(2)}, u32[]{:S(2)}) collective-permute-start(bf16[48,3072]{1,0:T(8,128)(2,1)S(1)} %get-tuple-element.36), channel_id=1, source_target_pairs={{0,64},{1,961},{2,66},{3,963},{4,68},{5,965},{6,70},{7,967},{8,72}... | collective-permute-start | bytes 884744 | tf_op jit(solution)/shard_map/ppermute | solution.py:433
  71.1 1.9 collective-permute-start.3
  73.0 3.2 %collective-permute-done.2.far_left_ref = bf16[48,3072]{1,0:T(8,128)(2,1)S(1)} collective-permute-done((bf16[48,3072]{1,0:T(8,128)(2,1)S(1)}, bf16[48,3072]{1,0:T(8,128)(2,1)S(1)}, u32[]{:S(2)}, u32[]{:S(2)}) %collective-permute-start.2) | collective-permute-done | bytes 294944 | tf_op jit(solution)/shard_map/ppermute | solution.py:433
  76.2 3.5 %collective-permute-done.3.far_right_ref = bf16[48,3072]{1,0:T(8,128)(2,1)S(1)} collective-permute-done((bf16[48,3072]{1,0:T(8,128)(2,1)S(1)}, bf16[48,3072]{1,0:T(8,128)(2,1)S(1)}, u32[]{:S(2)}, u32[]{:S(2)}) %collective-permute-start.3) | collective-permute-done | bytes 294944 | tf_op jit(solution)/shard_map/ppermute | solution.py:433
  80.2 3.4 %collective-permute-start.4 = (bf16[24,3072]{1,0:T(8,128)(2,1)S(1)}, bf16[24,3072]{1,0:T(8,128)(2,1)S(1)}, u32[]{:S(2)}, u32[]{:S(2)}) collective-permute-start(bf16[24,3072]{1,0:T(8,128)(2,1)S(1)} %get-tuple-element.39), channel_id=1, source_target_pairs={{0,256},{1,769},{2,258},{3,771},{4,260},{5,773},{6,262},{7,775},{8... | collective-permute-start | bytes 442376 | tf_op jit(solution)/shard_map/ppermute | solution.py:433
  83.5 5.8 %collective-permute-start.5 = (bf16[24,3072]{1,0:T(8,128)(2,1)S(1)}, bf16[24,3072]{1,0:T(8,128)(2,1)S(1)}, u32[]{:S(2)}, u32[]{:S(2)}) collective-permute-start(bf16[24,3072]{1,0:T(8,128)(2,1)S(1)} %get-tuple-element.40), channel_id=1, source_target_pairs={{0,768},{1,257},{2,770},{3,259},{4,772},{5,261},{6,774},{7,263},{8... | collective-permute-start | bytes 442376 | tf_op jit(solution)/shard_map/ppermute | solution.py:433
  89.4 6.5 %collective-permute-done.4.from_left_ref = bf16[24,3072]{1,0:T(8,128)(2,1)S(1)} collective-permute-done((bf16[24,3072]{1,0:T(8,128)(2,1)S(1)}, bf16[24,3072]{1,0:T(8,128)(2,1)S(1)}, u32[]{:S(2)}, u32[]{:S(2)}) %collective-permute-start.4) | collective-permute-done | bytes 147488 | tf_op jit(solution)/shard_map/ppermute | solution.py:433
  95.9 6.6 %collective-permute-done.5.from_right_ref = bf16[24,3072]{1,0:T(8,128)(2,1)S(1)} collective-permute-done((bf16[24,3072]{1,0:T(8,128)(2,1)S(1)}, bf16[24,3072]{1,0:T(8,128)(2,1)S(1)}, u32[]{:S(2)}, u32[]{:S(2)}) %collective-permute-start.5) | collective-permute-done | bytes 147488 | tf_op jit(solution)/shard_map/ppermute | solution.py:433
  102.5 3.4 %collective-permute-start.6 = (bf16[24,1536]{1,0:T(8,128)(2,1)S(1)}, bf16[24,1536]{1,0:T(8,128)(2,1)S(1)}, u32[]{:S(2)}, u32[]{:S(2)}) collective-permute-start(bf16[24,1536]{1,0:T(8,128)(2,1)S(1)} %get-tuple-element.43), channel_id=1, source_target_pairs={{0,256},{1,769},{2,258},{3,771},{4,260},{5,773},{6,262},{7,775},{8... | collective-permute-start | bytes 221192 | tf_op jit(solution)/shard_map/ppermute | solution.py:433
  105.9 5.8 %collective-permute-start.7 = (bf16[24,1536]{1,0:T(8,128)(2,1)S(1)}, bf16[24,1536]{1,0:T(8,128)(2,1)S(1)}, u32[]{:S(2)}, u32[]{:S(2)}) collective-permute-start(bf16[24,1536]{1,0:T(8,128)(2,1)S(1)} %get-tuple-element.44), channel_id=1, source_target_pairs={{0,768},{1,257},{2,770},{3,259},{4,772},{5,261},{6,774},{7,263},{8... | collective-permute-start | bytes 221192 | tf_op jit(solution)/shard_map/ppermute | solution.py:433
  111.7 4.0 %collective-permute-done.7.far_right_ref = bf16[24,1536]{1,0:T(8,128)(2,1)S(1)} collective-permute-done((bf16[24,1536]{1,0:T(8,128)(2,1)S(1)}, bf16[24,1536]{1,0:T(8,128)(2,1)S(1)}, u32[]{:S(2)}, u32[]{:S(2)}) %collective-permute-start.7) | collective-permute-done | bytes 73760 | tf_op jit(solution)/shard_map/ppermute | solution.py:433
  115.9 26.1 %all_gather.3.own_ref = bf16[96,3200]{1,0:T(8,128)(2,1)S(1)} all-gather(bf16[24,3200]{1,0:T(8,128)(2,1)S(1)} %shard_map.132), channel_id=1, replica_groups={{0,256,512,768},{64,320,576,832},{128,384,640,896},{192,448,704,960},{1..., dimensions={0}, use_global_device_ids=true | all-gather | bytes 768000 | tf_op jit(solution)/shard_map/all_gather | solution.py:499
  142.0 1.9 collective-permute-start.8
  143.9 3.4 %collective-permute-start.9 = (bf16[96,3200]{1,0:T(8,128)(2,1)S(1)}, bf16[96,3200]{1,0:T(8,128)(2,1)S(1)}, u32[]{:S(2)}, u32[]{:S(2)}) collective-permute-start(bf16[96,3200]{1,0:T(8,128)(2,1)S(1)} %all_gather.3.own_ref), channel_id=1, source_target_pairs={{0,960},{1,65},{2,962},{3,67},{4,964},{5,69},{6,966},{7,71},{8,968... | collective-permute-start | bytes 1843208 | tf_op jit(solution)/shard_map/ppermute | solution.py:433
  147.3 8.9 %collective-permute-done.8.left_ref = bf16[96,3200]{1,0:T(8,128)(2,1)S(1)} collective-permute-done((bf16[96,3200]{1,0:T(8,128)(2,1)S(1)}, bf16[96,3200]{1,0:T(8,128)(2,1)S(1)}, u32[]{:S(2)}, u32[]{:S(2)}) %collective-permute-start.8) | collective-permute-done | bytes 614432 | tf_op jit(solution)/shard_map/ppermute | solution.py:433
  156.2 2.1 %collective-permute-start.10 = (bf16[48,3200]{1,0:T(8,128)(2,1)S(1)}, bf16[48,3200]{1,0:T(8,128)(2,1)S(1)}, u32[]{:S(2)}, u32[]{:S(2)}) collective-permute-start(bf16[48,3200]{1,0:T(8,128)(2,1)S(1)} %slice.8), channel_id=1, source_target_pairs={{0,64},{1,961},{2,66},{3,963},{4,68},{5,965},{6,70},{7,967},{8,72}... | collective-permute-start | bytes 921608 | tf_op jit(solution)/shard_map/ppermute | solution.py:433
  158.3 3.7 %collective-permute-done.9.right_ref = bf16[96,3200]{1,0:T(8,128)(2,1)S(1)} collective-permute-done((bf16[96,3200]{1,0:T(8,128)(2,1)S(1)}, bf16[96,3200]{1,0:T(8,128)(2,1)S(1)}, u32[]{:S(2)}, u32[]{:S(2)}) %collective-permute-start.9) | collective-permute-done | bytes 614432 | tf_op jit(solution)/shard_map/ppermute | solution.py:433
  162.0 1.9 collective-permute-start.11
  164.0 9.8 %collective-permute-done.11.far_right_ref = bf16[48,3200]{1,0:T(8,128)(2,1)S(1)} collective-permute-done((bf16[48,3200]{1,0:T(8,128)(2,1)S(1)}, bf16[48,3200]{1,0:T(8,128)(2,1)S(1)}, u32[]{:S(2)}, u32[]{:S(2)}) %collective-permute-start.11) | collective-permute-done | bytes 307232 | tf_op jit(solution)/shard_map/ppermute | solution.py:433
  173.7 3.3 %shard_map.133 = bf16[64,24,128]{2,1,0:T(8,128)(2,1)} custom-call(s32[1]{0:T(128)} %bitcast.place_ref, bf16[96,3200]{1,0:T(8,128)(2,1)S(1)} %all_gather.3.own_ref, bf16[96,3200]{1,0:T(8,128)(2,1)S(1)} %collective-permute-done.8.left_ref, bf16[96,3200]{1,0:T(8,128)(2,1)S(1)} %collective-permute-done.9.right_ref, ...), custom_call_target="tpu_custom_call" | custom-call | flops 700000000 | bytes 4500000 | tf_op jit(solution)/shard_map/pallas_call | solution.py:504
  177.1 6.3 %all-to-all-start.1 = ((bf16[64,24,128]{2,1,0:T(8,128)(2,1)}), bf16[64,24,128]{2,1,0:T(8,128)(2,1)S(1)}, u32[]{:S(2)}, u32[]{:S(2)}) async-start(bf16[64,24,128]{2,1,0:T(8,128)(2,1)} %shard_map.133), calls=%async_computation.1 | async-start | bytes 786432 | tf_op jit(solution)/shard_map/all_to_all | solution.py:512
  183.4 2.1 %shard_map.135 = (bf16[224,1024]{1,0:T(8,128)(2,1)}, bf16[224,1024]{1,0:T(8,128)(2,1)}, bf16[224,1024]{1,0:T(8,128)(2,1)}) custom-call(s32[1]{0:T(128)} %bitcast.place_ref, bf16[96,3200]{1,0:T(8,128)(2,1)S(1)} %all_gather.3.own_ref, bf16[96,3200]{1,0:T(8,128)(2,1)S(1)} %collective-permute-done.8.left_ref, ...), custom_call_target="tpu_custom_call" | custom-call | flops 700000000 | bytes 4500000 | tf_op jit(solution)/shard_map/pallas_call | solution.py:514
  185.5 12.5 %all-to-all-done.1.back_ref = bf16[64,24,128]{2,1,0:T(8,128)(2,1)S(1)} async-done(((bf16[64,24,128]{2,1,0:T(8,128)(2,1)}), bf16[64,24,128]{2,1,0:T(8,128)(2,1)S(1)}, u32[]{:S(2)}, u32[]{:S(2)}) %all-to-all-start.1) | async-done | bytes 393248 | tf_op jit(solution)/shard_map/all_to_all | solution.py:512
  198.0 2.1 %shard_map.134 = (bf16[224,128]{1,0:T(8,128)(2,1)}, bf16[224,128]{1,0:T(8,128)(2,1)}, f32[8,128]{1,0:T(8,128)}) custom-call(bf16[64,24,128]{2,1,0:T(8,128)(2,1)S(1)} %all-to-all-done.1.back_ref, f32[128,128]{1,0:T(8,128)S(1)} %get-tuple-element.45.plan_ref, s32[8,128]{1,0:T(8,128)S(1)} %bitcast.28, f32[8,128]{1,0:T(8,128)S(1)} %bitcast.30), custom_call_target="tpu_custom_call" | custom-call | flops 500000000 | bytes 1000000 | tf_op jit(solution)/shard_map/pallas_call | solution.py:524
  (34 shorter events, 3.8 us)
Async XLA Ops:
  0.6 0.7 copy-start.11
  0.6 0.7 copy-start.10
  0.7 0.7 copy-start.12
  1.3 0.8 copy-start.8
  2.2 0.8 copy-start.9
  3.0 35.5 %copy-start.1 = (bf16[1,224,1024]{2,1,0:T(8,128)(2,1)S(1)}, bf16[1,224,1024]{2,1,0:T(8,128)(2,1)}, u32[]{:S(2)}) copy-start(bf16[1,224,1024]{2,1,0:T(8,128)(2,1)} %param.14) | copy-start | bytes 1376260
  3.0 35.5 %copy-start.2 = (bf16[1,1024,224]{1,2,0:T(8,128)(2,1)S(1)}, bf16[1,1024,224]{1,2,0:T(8,128)(2,1)}, u32[]{:S(2)}) copy-start(bf16[1,1024,224]{1,2,0:T(8,128)(2,1)} %param.15) | copy-start | bytes 1376260
  5.4 33.1 %copy-start = (bf16[1,224,1024]{2,1,0:T(8,128)(2,1)S(1)}, bf16[1,224,1024]{2,1,0:T(8,128)(2,1)}, u32[]{:S(2)}) copy-start(bf16[1,224,1024]{2,1,0:T(8,128)(2,1)} %param.13) | copy-start | bytes 1376260
  5.4 33.1 %all-to-all-start = ((bf16[64,24,128]{2,1,0:T(8,128)(2,1)}), bf16[64,24,128]{2,1,0:T(8,128)(2,1)S(1)}, u32[]{:S(2)}, u32[]{:S(2)}) async-start(bf16[64,24,128]{2,1,0:T(8,128)(2,1)} %get-tuple-element.30), calls=%async_computation | async-start | bytes 786432 | tf_op jit(solution)/shard_map/all_to_all | solution.py:462
  40.9 0.7 copy-start.6
  41.6 25.5 %copy-start.4 = (bf16[384,224]{1,0:T(8,128)(2,1)}, bf16[384,224]{1,0:T(8,128)(2,1)S(1)}, u32[]{:S(2)}) copy-start(bf16[384,224]{1,0:T(8,128)(2,1)S(1)} %get-tuple-element.49.tok_ref) | copy-start | bytes 516100
  41.6 21.5 %collective-permute-start = (bf16[96,3072]{1,0:T(8,128)(2,1)S(1)}, bf16[96,3072]{1,0:T(8,128)(2,1)S(1)}, u32[]{:S(2)}, u32[]{:S(2)}) collective-permute-start(bf16[96,3072]{1,0:T(8,128)(2,1)S(1)} %get-tuple-element.32), channel_id=1, source_target_pairs={{0,64},{1,961},{2,66},{3,963},{4,68},{5,965},{6,70},{7,967},{8,72}... | collective-permute-start | bytes 1769480 | tf_op jit(solution)/shard_map/ppermute | solution.py:433
  52.8 14.2 %collective-permute-start.1 = (bf16[96,3072]{1,0:T(8,128)(2,1)S(1)}, bf16[96,3072]{1,0:T(8,128)(2,1)S(1)}, u32[]{:S(2)}, u32[]{:S(2)}) collective-permute-start(bf16[96,3072]{1,0:T(8,128)(2,1)S(1)} %get-tuple-element.33), channel_id=1, source_target_pairs={{0,960},{1,65},{2,962},{3,67},{4,964},{5,69},{6,966},{7,71},{8,968... | collective-permute-start | bytes 1769480 | tf_op jit(solution)/shard_map/ppermute | solution.py:433
  67.1 9.1 %collective-permute-start.2 = (bf16[48,3072]{1,0:T(8,128)(2,1)S(1)}, bf16[48,3072]{1,0:T(8,128)(2,1)S(1)}, u32[]{:S(2)}, u32[]{:S(2)}) collective-permute-start(bf16[48,3072]{1,0:T(8,128)(2,1)S(1)} %get-tuple-element.36), channel_id=1, source_target_pairs={{0,64},{1,961},{2,66},{3,963},{4,68},{5,965},{6,70},{7,967},{8,72}... | collective-permute-start | bytes 884744 | tf_op jit(solution)/shard_map/ppermute | solution.py:433
  71.1 8.7 %collective-permute-start.3 = (bf16[48,3072]{1,0:T(8,128)(2,1)S(1)}, bf16[48,3072]{1,0:T(8,128)(2,1)S(1)}, u32[]{:S(2)}, u32[]{:S(2)}) collective-permute-start(bf16[48,3072]{1,0:T(8,128)(2,1)S(1)} %get-tuple-element.37), channel_id=1, source_target_pairs={{0,960},{1,65},{2,962},{3,67},{4,964},{5,69},{6,966},{7,71},{8,968... | collective-permute-start | bytes 884744 | tf_op jit(solution)/shard_map/ppermute | solution.py:433
  80.2 15.7 %collective-permute-start.4 = (bf16[24,3072]{1,0:T(8,128)(2,1)S(1)}, bf16[24,3072]{1,0:T(8,128)(2,1)S(1)}, u32[]{:S(2)}, u32[]{:S(2)}) collective-permute-start(bf16[24,3072]{1,0:T(8,128)(2,1)S(1)} %get-tuple-element.39), channel_id=1, source_target_pairs={{0,256},{1,769},{2,258},{3,771},{4,260},{5,773},{6,262},{7,775},{8... | collective-permute-start | bytes 442376 | tf_op jit(solution)/shard_map/ppermute | solution.py:433
  83.5 18.9 %collective-permute-start.5 = (bf16[24,3072]{1,0:T(8,128)(2,1)S(1)}, bf16[24,3072]{1,0:T(8,128)(2,1)S(1)}, u32[]{:S(2)}, u32[]{:S(2)}) collective-permute-start(bf16[24,3072]{1,0:T(8,128)(2,1)S(1)} %get-tuple-element.40), channel_id=1, source_target_pairs={{0,768},{1,257},{2,770},{3,259},{4,772},{5,261},{6,774},{7,263},{8... | collective-permute-start | bytes 442376 | tf_op jit(solution)/shard_map/ppermute | solution.py:433
  102.5 9.2 %collective-permute-start.6 = (bf16[24,1536]{1,0:T(8,128)(2,1)S(1)}, bf16[24,1536]{1,0:T(8,128)(2,1)S(1)}, u32[]{:S(2)}, u32[]{:S(2)}) collective-permute-start(bf16[24,1536]{1,0:T(8,128)(2,1)S(1)} %get-tuple-element.43), channel_id=1, source_target_pairs={{0,256},{1,769},{2,258},{3,771},{4,260},{5,773},{6,262},{7,775},{8... | collective-permute-start | bytes 221192 | tf_op jit(solution)/shard_map/ppermute | solution.py:433
  105.9 9.8 %collective-permute-start.7 = (bf16[24,1536]{1,0:T(8,128)(2,1)S(1)}, bf16[24,1536]{1,0:T(8,128)(2,1)S(1)}, u32[]{:S(2)}, u32[]{:S(2)}) collective-permute-start(bf16[24,1536]{1,0:T(8,128)(2,1)S(1)} %get-tuple-element.44), channel_id=1, source_target_pairs={{0,768},{1,257},{2,770},{3,259},{4,772},{5,261},{6,774},{7,263},{8... | collective-permute-start | bytes 221192 | tf_op jit(solution)/shard_map/ppermute | solution.py:433
  142.0 14.2 %collective-permute-start.8 = (bf16[96,3200]{1,0:T(8,128)(2,1)S(1)}, bf16[96,3200]{1,0:T(8,128)(2,1)S(1)}, u32[]{:S(2)}, u32[]{:S(2)}) collective-permute-start(bf16[96,3200]{1,0:T(8,128)(2,1)S(1)} %all_gather.3.own_ref), channel_id=1, source_target_pairs={{0,64},{1,961},{2,66},{3,963},{4,68},{5,965},{6,70},{7,967},{8,72}... | collective-permute-start | bytes 1843208 | tf_op jit(solution)/shard_map/ppermute | solution.py:433
  143.9 18.0 %collective-permute-start.9 = (bf16[96,3200]{1,0:T(8,128)(2,1)S(1)}, bf16[96,3200]{1,0:T(8,128)(2,1)S(1)}, u32[]{:S(2)}, u32[]{:S(2)}) collective-permute-start(bf16[96,3200]{1,0:T(8,128)(2,1)S(1)} %all_gather.3.own_ref), channel_id=1, source_target_pairs={{0,960},{1,65},{2,962},{3,67},{4,964},{5,69},{6,966},{7,71},{8,968... | collective-permute-start | bytes 1843208 | tf_op jit(solution)/shard_map/ppermute | solution.py:433
  156.2 17.5 %copy-start.3 = (bf16[1,1024,224]{1,2,0:T(8,128)(2,1)S(1)}, bf16[1,1024,224]{1,2,0:T(8,128)(2,1)}, u32[]{:S(2)}) copy-start(bf16[1,1024,224]{1,2,0:T(8,128)(2,1)} %param.15) | copy-start | bytes 1376260
  156.2 7.7 %collective-permute-start.10 = (bf16[48,3200]{1,0:T(8,128)(2,1)S(1)}, bf16[48,3200]{1,0:T(8,128)(2,1)S(1)}, u32[]{:S(2)}, u32[]{:S(2)}) collective-permute-start(bf16[48,3200]{1,0:T(8,128)(2,1)S(1)} %slice.8), channel_id=1, source_target_pairs={{0,64},{1,961},{2,66},{3,963},{4,68},{5,965},{6,70},{7,967},{8,72}... | collective-permute-start | bytes 921608 | tf_op jit(solution)/shard_map/ppermute | solution.py:433
  162.0 11.7 %collective-permute-start.11 = (bf16[48,3200]{1,0:T(8,128)(2,1)S(1)}, bf16[48,3200]{1,0:T(8,128)(2,1)S(1)}, u32[]{:S(2)}, u32[]{:S(2)}) collective-permute-start(bf16[48,3200]{1,0:T(8,128)(2,1)S(1)} %slice.9), channel_id=1, source_target_pairs={{0,960},{1,65},{2,962},{3,67},{4,964},{5,69},{6,966},{7,71},{8,968... | collective-permute-start | bytes 921608 | tf_op jit(solution)/shard_map/ppermute | solution.py:433
  177.1 6.4 %copy-start.5 = (bf16[384,224]{1,0:T(8,128)(2,1)S(1)}, bf16[384,224]{1,0:T(8,128)(2,1)}, u32[]{:S(2)}) copy-start(bf16[384,224]{1,0:T(8,128)(2,1)} %copy-done.4) | copy-start | bytes 516100
  177.1 6.4 %copy-start.7 = (bf16[384,224]{1,0:T(8,128)(2,1)S(1)}, bf16[384,224]{1,0:T(8,128)(2,1)}, u32[]{:S(2)}) copy-start(bf16[384,224]{1,0:T(8,128)(2,1)} %copy-done.6) | copy-start | bytes 516100
  177.1 20.9 %all-to-all-start.1 = ((bf16[64,24,128]{2,1,0:T(8,128)(2,1)}), bf16[64,24,128]{2,1,0:T(8,128)(2,1)S(1)}, u32[]{:S(2)}, u32[]{:S(2)}) async-start(bf16[64,24,128]{2,1,0:T(8,128)(2,1)} %shard_map.133), calls=%async_computation.1 | async-start | bytes 786432 | tf_op jit(solution)/shard_map/all_to_all | solution.py:512

commit v8 on v7

--- a/solution.py
+++ b/solution.py
@@ -137,44 +137,11 @@
     send_ref[...] = (picked * row_scale).astype(BF16).reshape(send_ref.shape)
 
 
-def partial_kernel(
-    place_ref,
-    recv_ref,
-    gate_hbm,
-    up_hbm,
-    down_hbm,
-    own_ref,
-    to_right_ref,
-    to_left_ref,
-    next_ref,
-    previous_ref,
-    tok_ref,
-    scaled_ref,
-    gate_ref,
-    up_ref,
-    down_ref,
-    sems,
-):
-    copies = fetch((gate_hbm, up_hbm, down_hbm), (gate_ref, up_ref, down_ref), sems)
-    experts = recv_ref.shape[0]
-    width, hidden = gate_ref.shape
-    block = SOURCES * GROUP
-    per_tile = SOURCES * CAP
-    reorder = reorder_matrix(iota((block, block), 0), iota((block, block), 1))
-    for b in range(experts // SOURCES):
-        sent = recv_ref[b * SOURCES : (b + 1) * SOURCES].reshape(block, LANES)
-        rows = dot(reorder, sent).astype(BF16)
-        place = slice(b * per_tile, (b + 1) * per_tile)
-        for ref, index in ((tok_ref, 0), (scaled_ref, 2)):
-            ref[place, :LANES] = rows[index * per_tile : (index + 1) * per_tile]
-            ref[place, LANES:] = rows[(index + 1) * per_tile : (index + 2) * per_tile, : width - LANES]
-    held = tok_ref.shape[0] // RING
+def window_partials(place_ref, products, own_ref, to_right_ref, to_left_ref, next_ref, previous_ref):
+    held = own_ref.shape[0]
     half = held // 2
-    for copy in copies:
-        copy.wait()
-    for index, (rows_ref, ref) in enumerate(
-        ((tok_ref, gate_ref), (tok_ref, up_ref), (scaled_ref, down_ref))
-    ):
+    for index, (rows_ref, ref) in enumerate(products):
+        hidden = ref.shape[1]
         columns = slice(index * hidden, (index + 1) * hidden)
         for step, pieces in (
             (RING // 2, ((to_right_ref, 0), (to_left_ref, half))),
@@ -187,6 +154,52 @@
             value = dot(rows_ref[pl.ds(begin, held)], ref[...]).astype(BF16)
             for part, (out_ref, start) in enumerate(pieces):
                 out_ref[start : start + half, columns] = value[part * half : (part + 1) * half]
+
+
+def partial_kernel(
+    place_ref,
+    recv_ref,
+    gate_hbm,
+    up_hbm,
+    own_ref,
+    to_right_ref,
+    to_left_ref,
+    next_ref,
+    previous_ref,
+    tok_ref,
+    scaled_ref,
+    gate_ref,
+    up_ref,
+    sems,
+):
+    copies = fetch((gate_hbm, up_hbm), (gate_ref, up_ref), sems)
+    experts = recv_ref.shape[0]
+    width = gate_ref.shape[0]
+    block = SOURCES * GROUP
+    per_tile = SOURCES * CAP
+    reorder = reorder_matrix(iota((block, block), 0), iota((block, block), 1))
+    for b in range(experts // SOURCES):
+        sent = recv_ref[b * SOURCES : (b + 1) * SOURCES].reshape(block, LANES)
+        rows = dot(reorder, sent).astype(BF16)
+        place = slice(b * per_tile, (b + 1) * per_tile)
+        for ref, index in ((tok_ref, 0), (scaled_ref, 2)):
+            ref[place, :LANES] = rows[index * per_tile : (index + 1) * per_tile]
+            ref[place, LANES:] = rows[(index + 1) * per_tile : (index + 2) * per_tile, : width - LANES]
+    for copy in copies:
+        copy.wait()
+    products = ((tok_ref, gate_ref), (tok_ref, up_ref))
+    window_partials(
+        place_ref, products, own_ref, to_right_ref, to_left_ref, next_ref, previous_ref
+    )
+
+
+def backward_partial_kernel(
+    place_ref, scaled_ref, down_ref, own_ref, to_right_ref, to_left_ref, next_ref, previous_ref
+):
+    products = ((scaled_ref, down_ref),)
+    window_partials(
+        place_ref, products, own_ref, to_right_ref, to_left_ref, next_ref, previous_ref
+    )
 
 
 def relay_kernel(next_ref, previous_ref, from_left_ref, from_right_ref, to_right_ref, to_left_ref):
@@ -244,10 +257,7 @@
     ).astype(BF16)
 
 
-def middle_kernel(
-    kept_ref, from_left_ref, from_right_ref, far_left_ref, far_right_ref, out_ref, sum_ref
-):
-    hidden = kept_ref.shape[1] // 3
+def chunk_sum(sum_ref, kept_ref, from_left_ref, from_right_ref, far_left_ref, far_right_ref):
     split = far_left_ref.shape[1]
     sum_ref[:, :split] = (
         kept_ref[:, :split].astype(F32)
@@ -259,7 +269,14 @@
         + from_left_ref[:, split:].astype(F32)
         + far_right_ref[...].astype(F32)
     )
-    gate, up, grad = (sum_ref[:, i * hidden : (i + 1) * hidden] for i in range(3))
+
+
+def middle_kernel(*refs):
+    forward, backward, (out_ref, sum_ref, grad_ref) = refs[:5], refs[5:10], refs[10:]
+    chunk_sum(sum_ref, *forward)
+    chunk_sum(grad_ref, *backward)
+    hidden = grad_ref.shape[1]
+    gate, up, grad = sum_ref[:, :hidden], sum_ref[:, hidden:], grad_ref[...]
     sigmoid = jax.nn.sigmoid(gate)
     gated = gate * sigmoid
     hidden_value = (gated * up).astype(BF16)
@@ -433,6 +450,38 @@
     return lax.ppermute(block, ("expert", "dp"), route)
 
 
+def partial_shapes(held, columns):
+    whole, halved = (jax.ShapeDtypeStruct((size, columns), BF16) for size in (held, held // 2))
+    return (whole, whole, whole, halved, halved)
+
+
+def reduced(member, partials, parts):
+    own, to_right, to_left, following, previous = partials
+    held, columns = own.shape
+    shape = jax.ShapeDtypeStruct
+    halved = shape((held // 2, columns), BF16)
+    from_left, from_right = shifted(to_right, 1), shifted(to_left, -1)
+    relay_right, relay_left = kernel_call(relay_kernel, (halved, halved), 300_000, 1_500_000)(
+        following, previous, from_left, from_right
+    )
+    far_left, far_right = shifted(relay_right, 1), shifted(relay_left, -1)
+    chunk, chunk_half = (shape((held // (parts // RING), size), BF16) for size in (columns, columns // 2))
+    kept, to_right, to_left, following, previous = kernel_call(
+        window_kernel,
+        (chunk, chunk, chunk, chunk_half, chunk_half),
+        600_000,
+        2_000_000,
+        spaces="svvvvv",
+        scratch=[pltpu.VMEM((held, columns), F32)],
+    )(member, own, from_left, from_right, far_left, far_right)
+    from_left, from_right = shifted(to_right, RING), shifted(to_left, -RING)
+    relay_right, relay_left = kernel_call(
+        second_relay_kernel, (chunk_half, chunk_half), 100_000, 400_000
+    )(following, previous, from_left, from_right)
+    far_left, far_right = shifted(relay_right, RING), shifted(relay_left, -RING)
+    return [kept, from_left, from_right, far_left, far_right]
+
+
 def per_device(
     tokens, cotangent, routes, route_weights, owner_slots, gate_weight, up_weight, down_weight
 ):
@@ -445,7 +494,6 @@
     shape = jax.ShapeDtypeStruct
     exchanged = shape((experts, GROUP, LANES), BF16)
     rows = shape((row_count, width), BF16)
-    whole, halved = (shape((size, 3 * hidden), BF16) for size in (held, held // 2))
     groups = [list(range(i, parts, RING)) for i in range(RING)]
     member = lax.axis_index("expert") + ((lax.axis_index("dp") & 1) << PLACE_BITS)
     member = member.astype(jnp.int32).reshape(1)
@@ -460,42 +508,31 @@
         scratch=held_copies(*arguments),
     )(*arguments)
     arrived = lax.all_to_all(send, "dp", split_axis=0, concat_axis=0, tiled=True)
-    own, to_right, to_left, following, previous, token_rows, scaled_rows = kernel_call(
+    columns = 2 * hidden
+    *forward, token_rows, scaled_rows = kernel_call(
         partial_kernel,
-        (whole, whole, whole, halved, halved, rows, rows),
-        700_000_000,
-        4_500_000,
-        spaces="svaaa",
-        scratch=held_copies(*weights),
-    )(member, arrived, *weights)
-    from_left, from_right = shifted(to_right, 1), shifted(to_left, -1)
-    relay_right, relay_left = kernel_call(relay_kernel, (halved, halved), 300_000, 1_500_000)(
-        following, previous, from_left, from_right
-    )
-    far_left, far_right = shifted(relay_right, 1), shifted(relay_left, -1)
-    chunk, chunk_half = (
-        shape((row_count // parts, columns), BF16) for columns in (3 * hidden, 3 * hidden // 2)
-    )
-    kept, to_right, to_left, following, previous = kernel_call(
-        window_kernel,
-        (chunk, chunk, chunk, chunk_half, chunk_half),
-        600_000,
-        2_000_000,
-        spaces="svvvvv",
-        scratch=[pltpu.VMEM(whole.shape, F32)],
-    )(member, own, from_left, from_right, far_left, far_right)
-    from_left, from_right = shifted(to_right, RING), shifted(to_left, -RING)
-    relay_right, relay_left = kernel_call(
-        second_relay_kernel, (chunk_half, chunk_half), 100_000, 400_000
-    )(following, previous, from_left, from_right)
-    far_left, far_right = shifted(relay_right, RING), shifted(relay_left, -RING)
+        (*partial_shapes(held, columns), rows, rows),
+        450_000_000,
+        3_000_000,
+        spaces="svaa",
+        scratch=held_copies(*weights[:2]),
+    )(member, arrived, *weights[:2])
+    backward = kernel_call(
+        backward_partial_kernel,
+        partial_shapes(held, hidden),
+        180_000_000,
+        1_500_000,
+        spaces="svv",
+    )(member, scaled_rows, weights[2])
+    summands = reduced(member, forward, parts) + reduced(member, backward, parts)
+    share_rows = row_count // parts
     share = kernel_call(
         middle_kernel,
-        shape((row_count // parts, 3 * hidden + LANES), BF16),
+        shape((share_rows, 3 * hidden + LANES), BF16),
         1_000_000,
         700_000,
-        scratch=[pltpu.VMEM(chunk.shape, F32)],
-    )(kept, from_left, from_right, far_left, far_right)
+        scratch=[pltpu.VMEM((share_rows, columns), F32), pltpu.VMEM((share_rows, hidden), F32)],
+    )(*summands)
     own = lax.all_gather(share, "expert", axis=0, tiled=True, axis_index_groups=groups)
     half = held // 2
     left, right = shifted(own, 1), shifted(own, -1)

time: 201 us -> 205 us (1.020)
  starting transfers between devices: 71.3 us -> 111 us
  waiting for transfers between devices: 85.7 us -> 49.4 us
    ppermute x12 -> x20, waiting for transfers between devices: 58.4 us -> 22.1 us  [shifted(): return lax.ppermute(block, ('expert', 'dp'), route)]
    ppermute x12 -> x20, starting transfers between devices: 46.6 us -> 81.1 us  [shifted(): return lax.ppermute(block, ('expert', 'dp'), route)]
    all_to_all x1, starting transfers between devices: 6.32 us -> 11.3 us  [per_device(): lax.all_to_all(back, 'dp', split_axis=0, concat_axis=0, tiled=True)]
  transfers between devices with their start and end apart: 14 -> 22, of which waited for: 12 -> 7; matrix products, arithmetic and copies ran while one was open for 0% -> 0% of each run, Pallas kernels for 1% -> 2%
where the time goes in v8:
time: 205 us; the launch traced here: 204 us
  starting transfers between devices  111 us (54%)
  waiting for transfers between devices  49.4 us (24%)
  blocking collectives  27.2 us (13%)
  Pallas kernels  12.9 us (6%)
  local copies, waits for them, and re-layouts  2.4 us (1%)
    ppermute x20, starting transfers between devices, shifted(): return lax.ppermute(block, ('expert', 'dp'), route)  81.1 us
    all_gather x1, blocking collectives, per_device(): lax.all_gather(share, 'expert', axis=0, tiled=True, axis_index_groups=gro...  27.2 us
    ppermute x20, waiting for transfers between devices, shifted(): return lax.ppermute(block, ('expert', 'dp'), route)  22.1 us
    all_to_all x1, starting transfers between devices, per_device(): lax.all_to_all(send, 'dp', split_axis=0, concat_axis=0, tiled=True)  18.4 us
    all_to_all x1, waiting for transfers between devices, per_device(): lax.all_to_all(send, 'dp', split_axis=0, concat_axis=0, tiled=True)  14.7 us
    all_to_all x1, waiting for transfers between devices, per_device(): lax.all_to_all(back, 'dp', split_axis=0, concat_axis=0, tiled=True)  12.5 us
    all_to_all x1, starting transfers between devices, per_device(): lax.all_to_all(back, 'dp', split_axis=0, concat_axis=0, tiled=True)  11.3 us
  transfers between devices with their start and end apart: 22, of which 7 were waited for; matrix products, arithmetic and copies ran while one was open for 0% of the time, Pallas kernels for 2%

profile of v8, /device:TPU:1, one launch (start us, length us, event | category | flops | bytes accessed | tf_op | source)
XLA Modules:
  0.0 203.7 jit_solution(2952185915592989804)
XLA Ops:
  3.0 2.4 %shard_map.127 = (bf16[64,24,128]{2,1,0:T(8,128)(2,1)}, f32[128,128]{1,0:T(8,128)S(1)}) custom-call(s32[8,128]{1,0:T(8,128)S(1)} %bitcast.27, f32[8,128]{1,0:T(8,128)S(1)} %bitcast.29, s32[1,64]{1,0:T(1,128)S(1)} %bitcast.31, bf16[224,128]{1,0:T(8,128)(2,1)S(1)} %bitcast.25, bf16[224,128]{1,0:T(8,128)(2,1)S(1)} %bitcast.26), custom_call_target="tpu_custom_call" | custom-call | flops 300000000 | bytes 1000000 | tf_op jit(solution)/shard_map/pallas_call | solution.py:502
  5.4 18.4 %all-to-all-start = ((bf16[64,24,128]{2,1,0:T(8,128)(2,1)}), bf16[64,24,128]{2,1,0:T(8,128)(2,1)S(1)}, u32[]{:S(2)}, u32[]{:S(2)}) async-start(bf16[64,24,128]{2,1,0:T(8,128)(2,1)} %get-tuple-element.44), calls=%async_computation | async-start | bytes 786432 | tf_op jit(solution)/shard_map/all_to_all | solution.py:510
  23.8 14.7 %all-to-all-done.recv_ref = bf16[64,24,128]{2,1,0:T(8,128)(2,1)S(1)} async-done(((bf16[64,24,128]{2,1,0:T(8,128)(2,1)}), bf16[64,24,128]{2,1,0:T(8,128)(2,1)S(1)}, u32[]{:S(2)}, u32[]{:S(2)}) %all-to-all-start) | async-done | bytes 393248 | tf_op jit(solution)/shard_map/all_to_all | solution.py:510
  40.4 11.2 %collective-permute-start = (bf16[96,2048]{1,0:T(8,128)(2,1)S(1)}, bf16[96,2048]{1,0:T(8,128)(2,1)S(1)}, u32[]{:S(2)}, u32[]{:S(2)}) collective-permute-start(bf16[96,2048]{1,0:T(8,128)(2,1)S(1)} %get-tuple-element.46), channel_id=1, source_target_pairs={{0,64},{1,961},{2,66},{3,963},{4,68},{5,965},{6,70},{7,967},{8,72}... | collective-permute-start | bytes 1179656 | tf_op jit(solution)/shard_map/ppermute | solution.py:450
  51.6 1.9 collective-permute-start.1
  54.0 4.6 %collective-permute-start.8 = (bf16[96,1024]{1,0:T(8,128)(2,1)S(1)}, bf16[96,1024]{1,0:T(8,128)(2,1)S(1)}, u32[]{:S(2)}, u32[]{:S(2)}) collective-permute-start(bf16[96,1024]{1,0:T(8,128)(2,1)S(1)} %get-tuple-element.61), channel_id=1, source_target_pairs={{0,64},{1,961},{2,66},{3,963},{4,68},{5,965},{6,70},{7,967},{8,72}... | collective-permute-start | bytes 589832 | tf_op jit(solution)/shard_map/ppermute | solution.py:450
  58.6 1.9 collective-permute-start.9
  60.5 2.1 %collective-permute-done.1.from_right_ref = bf16[96,2048]{1,0:T(8,128)(2,1)S(1)} collective-permute-done((bf16[96,2048]{1,0:T(8,128)(2,1)S(1)}, bf16[96,2048]{1,0:T(8,128)(2,1)S(1)}, u32[]{:S(2)}, u32[]{:S(2)}) %collective-permute-start.1) | collective-permute-done | bytes 393248 | tf_op jit(solution)/shard_map/ppermute | solution.py:450
  62.7 4.2 %collective-permute-start.2 = (bf16[48,2048]{1,0:T(8,128)(2,1)S(1)}, bf16[48,2048]{1,0:T(8,128)(2,1)S(1)}, u32[]{:S(2)}, u32[]{:S(2)}) collective-permute-start(bf16[48,2048]{1,0:T(8,128)(2,1)S(1)} %get-tuple-element.50), channel_id=1, source_target_pairs={{0,64},{1,961},{2,66},{3,963},{4,68},{5,965},{6,70},{7,967},{8,72}... | collective-permute-start | bytes 589832 | tf_op jit(solution)/shard_map/ppermute | solution.py:450
  67.0 1.9 collective-permute-start.3
  69.0 4.6 %collective-permute-start.10 = (bf16[48,1024]{1,0:T(8,128)(2,1)S(1)}, bf16[48,1024]{1,0:T(8,128)(2,1)S(1)}, u32[]{:S(2)}, u32[]{:S(2)}) collective-permute-start(bf16[48,1024]{1,0:T(8,128)(2,1)S(1)} %get-tuple-element.65), channel_id=1, source_target_pairs={{0,64},{1,961},{2,66},{3,963},{4,68},{5,965},{6,70},{7,967},{8,72}... | collective-permute-start | bytes 294920 | tf_op jit(solution)/shard_map/ppermute | solution.py:450
  75.7 3.4 %collective-permute-start.4 = (bf16[24,2048]{1,0:T(8,128)(2,1)S(1)}, bf16[24,2048]{1,0:T(8,128)(2,1)S(1)}, u32[]{:S(2)}, u32[]{:S(2)}) collective-permute-start(bf16[24,2048]{1,0:T(8,128)(2,1)S(1)} %get-tuple-element.53), channel_id=1, source_target_pairs={{0,256},{1,769},{2,258},{3,771},{4,260},{5,773},{6,262},{7,775},{8... | collective-permute-start | bytes 294920 | tf_op jit(solution)/shard_map/ppermute | solution.py:450
  79.1 5.8 %collective-permute-start.5 = (bf16[24,2048]{1,0:T(8,128)(2,1)S(1)}, bf16[24,2048]{1,0:T(8,128)(2,1)S(1)}, u32[]{:S(2)}, u32[]{:S(2)}) collective-permute-start(bf16[24,2048]{1,0:T(8,128)(2,1)S(1)} %get-tuple-element.54), channel_id=1, source_target_pairs={{0,768},{1,257},{2,770},{3,259},{4,772},{5,261},{6,774},{7,263},{8... | collective-permute-start | bytes 294920 | tf_op jit(solution)/shard_map/ppermute | solution.py:450
  85.1 3.4 %collective-permute-start.12 = (bf16[24,1024]{1,0:T(8,128)(2,1)S(1)}, bf16[24,1024]{1,0:T(8,128)(2,1)S(1)}, u32[]{:S(2)}, u32[]{:S(2)}) collective-permute-start(bf16[24,1024]{1,0:T(8,128)(2,1)S(1)} %get-tuple-element.68), channel_id=1, source_target_pairs={{0,256},{1,769},{2,258},{3,771},{4,260},{5,773},{6,262},{7,775},{8... | collective-permute-start | bytes 147464 | tf_op jit(solution)/shard_map/ppermute | solution.py:450
  88.4 5.8 %collective-permute-start.13 = (bf16[24,1024]{1,0:T(8,128)(2,1)S(1)}, bf16[24,1024]{1,0:T(8,128)(2,1)S(1)}, u32[]{:S(2)}, u32[]{:S(2)}) collective-permute-start(bf16[24,1024]{1,0:T(8,128)(2,1)S(1)} %get-tuple-element.69), channel_id=1, source_target_pairs={{0,768},{1,257},{2,770},{3,259},{4,772},{5,261},{6,774},{7,263},{8... | collective-permute-start | bytes 147464 | tf_op jit(solution)/shard_map/ppermute | solution.py:450
  94.3 3.5 %collective-permute-start.6 = (bf16[24,1024]{1,0:T(8,128)(2,1)S(1)}, bf16[24,1024]{1,0:T(8,128)(2,1)S(1)}, u32[]{:S(2)}, u32[]{:S(2)}) collective-permute-start(bf16[24,1024]{1,0:T(8,128)(2,1)S(1)} %get-tuple-element.57), channel_id=1, source_target_pairs={{0,256},{1,769},{2,258},{3,771},{4,260},{5,773},{6,262},{7,775},{8... | collective-permute-start | bytes 147464 | tf_op jit(solution)/shard_map/ppermute | solution.py:450
  97.9 5.7 %collective-permute-start.7 = (bf16[24,1024]{1,0:T(8,128)(2,1)S(1)}, bf16[24,1024]{1,0:T(8,128)(2,1)S(1)}, u32[]{:S(2)}, u32[]{:S(2)}) collective-permute-start(bf16[24,1024]{1,0:T(8,128)(2,1)S(1)} %get-tuple-element.58), channel_id=1, source_target_pairs={{0,768},{1,257},{2,770},{3,259},{4,772},{5,261},{6,774},{7,263},{8... | collective-permute-start | bytes 147464 | tf_op jit(solution)/shard_map/ppermute | solution.py:450
  103.6 3.5 %collective-permute-start.14 = (bf16[24,512]{1,0:T(8,128)(2,1)S(1)}, bf16[24,512]{1,0:T(8,128)(2,1)S(1)}, u32[]{:S(2)}, u32[]{:S(2)}) collective-permute-start(bf16[24,512]{1,0:T(8,128)(2,1)S(1)} %get-tuple-element.72), channel_id=1, source_target_pairs={{0,256},{1,769},{2,258},{3,771},{4,260},{5,773},{6,262},{7,775},{8... | collective-permute-start | bytes 73736 | tf_op jit(solution)/shard_map/ppermute | solution.py:450
  107.1 5.7 %collective-permute-start.15 = (bf16[24,512]{1,0:T(8,128)(2,1)S(1)}, bf16[24,512]{1,0:T(8,128)(2,1)S(1)}, u32[]{:S(2)}, u32[]{:S(2)}) collective-permute-start(bf16[24,512]{1,0:T(8,128)(2,1)S(1)} %get-tuple-element.73), channel_id=1, source_target_pairs={{0,768},{1,257},{2,770},{3,259},{4,772},{5,261},{6,774},{7,263},{8... | collective-permute-start | bytes 73736 | tf_op jit(solution)/shard_map/ppermute | solution.py:450
  112.8 4.4 %collective-permute-done.15.refs_9_ = bf16[24,512]{1,0:T(8,128)(2,1)S(1)} collective-permute-done((bf16[24,512]{1,0:T(8,128)(2,1)S(1)}, bf16[24,512]{1,0:T(8,128)(2,1)S(1)}, u32[]{:S(2)}, u32[]{:S(2)}) %collective-permute-start.15) | collective-permute-done | bytes 24608 | tf_op jit(solution)/shard_map/ppermute | solution.py:450
  117.4 27.2 %all_gather.3.own_ref = bf16[96,3200]{1,0:T(8,128)(2,1)S(1)} all-gather(bf16[24,3200]{1,0:T(8,128)(2,1)S(1)} %shard_map.136), channel_id=1, replica_groups={{0,256,512,768},{64,320,576,832},{128,384,640,896},{192,448,704,960},{1..., dimensions={0}, use_global_device_ids=true | all-gather | bytes 768000 | tf_op jit(solution)/shard_map/all_gather | solution.py:536
  146.6 3.4 %collective-permute-start.17 = (bf16[96,3200]{1,0:T(8,128)(2,1)S(1)}, bf16[96,3200]{1,0:T(8,128)(2,1)S(1)}, u32[]{:S(2)}, u32[]{:S(2)}) collective-permute-start(bf16[96,3200]{1,0:T(8,128)(2,1)S(1)} %all_gather.3.own_ref), channel_id=1, source_target_pairs={{0,960},{1,65},{2,962},{3,67},{4,964},{5,69},{6,966},{7,71},{8,968... | collective-permute-start | bytes 1843208 | tf_op jit(solution)/shard_map/ppermute | solution.py:450
  149.9 5.9 %collective-permute-done.16.left_ref = bf16[96,3200]{1,0:T(8,128)(2,1)S(1)} collective-permute-done((bf16[96,3200]{1,0:T(8,128)(2,1)S(1)}, bf16[96,3200]{1,0:T(8,128)(2,1)S(1)}, u32[]{:S(2)}, u32[]{:S(2)}) %collective-permute-start.16) | collective-permute-done | bytes 614432 | tf_op jit(solution)/shard_map/ppermute | solution.py:450
  155.8 2.8 %collective-permute-start.18 = (bf16[48,3200]{1,0:T(8,128)(2,1)S(1)}, bf16[48,3200]{1,0:T(8,128)(2,1)S(1)}, u32[]{:S(2)}, u32[]{:S(2)}) collective-permute-start(bf16[48,3200]{1,0:T(8,128)(2,1)S(1)} %slice.8), channel_id=1, source_target_pairs={{0,64},{1,961},{2,66},{3,963},{4,68},{5,965},{6,70},{7,967},{8,72}... | collective-permute-start | bytes 921608 | tf_op jit(solution)/shard_map/ppermute | solution.py:450
  158.7 4.3 %collective-permute-done.17.right_ref = bf16[96,3200]{1,0:T(8,128)(2,1)S(1)} collective-permute-done((bf16[96,3200]{1,0:T(8,128)(2,1)S(1)}, bf16[96,3200]{1,0:T(8,128)(2,1)S(1)}, u32[]{:S(2)}, u32[]{:S(2)}) %collective-permute-start.17) | collective-permute-done | bytes 614432 | tf_op jit(solution)/shard_map/ppermute | solution.py:450
  163.0 4.0 %collective-permute-start.19 = (bf16[48,3200]{1,0:T(8,128)(2,1)S(1)}, bf16[48,3200]{1,0:T(8,128)(2,1)S(1)}, u32[]{:S(2)}, u32[]{:S(2)}) collective-permute-start(bf16[48,3200]{1,0:T(8,128)(2,1)S(1)} %slice.9), channel_id=1, source_target_pairs={{0,960},{1,65},{2,962},{3,67},{4,964},{5,69},{6,966},{7,71},{8,968... | collective-permute-start | bytes 921608 | tf_op jit(solution)/shard_map/ppermute | solution.py:450
  167.0 5.4 %collective-permute-done.19.far_right_ref = bf16[48,3200]{1,0:T(8,128)(2,1)S(1)} collective-permute-done((bf16[48,3200]{1,0:T(8,128)(2,1)S(1)}, bf16[48,3200]{1,0:T(8,128)(2,1)S(1)}, u32[]{:S(2)}, u32[]{:S(2)}) %collective-permute-start.19) | collective-permute-done | bytes 307232 | tf_op jit(solution)/shard_map/ppermute | solution.py:450
  172.3 3.3 %shard_map.137 = bf16[64,24,128]{2,1,0:T(8,128)(2,1)} custom-call(s32[1]{0:T(128)} %bitcast.place_ref, bf16[96,3200]{1,0:T(8,128)(2,1)S(1)} %all_gather.3.own_ref, bf16[96,3200]{1,0:T(8,128)(2,1)S(1)} %collective-permute-done.16.left_ref, bf16[96,3200]{1,0:T(8,128)(2,1)S(1)} %collective-permute-done.17.right_ref, ...), custom_call_target="tpu_custom_call" | custom-call | flops 700000000 | bytes 4500000 | tf_op jit(solution)/shard_map/pallas_call | solution.py:541
  175.7 11.3 %all-to-all-start.1 = ((bf16[64,24,128]{2,1,0:T(8,128)(2,1)}), bf16[64,24,128]{2,1,0:T(8,128)(2,1)S(1)}, u32[]{:S(2)}, u32[]{:S(2)}) async-start(bf16[64,24,128]{2,1,0:T(8,128)(2,1)} %shard_map.137), calls=%async_computation.1 | async-start | bytes 786432 | tf_op jit(solution)/shard_map/all_to_all | solution.py:549
  187.0 2.1 %shard_map.139 = (bf16[224,1024]{1,0:T(8,128)(2,1)}, bf16[224,1024]{1,0:T(8,128)(2,1)}, bf16[224,1024]{1,0:T(8,128)(2,1)}) custom-call(s32[1]{0:T(128)} %bitcast.place_ref, bf16[96,3200]{1,0:T(8,128)(2,1)S(1)} %all_gather.3.own_ref, bf16[96,3200]{1,0:T(8,128)(2,1)S(1)} %collective-permute-done.16.left_ref, ...), custom_call_target="tpu_custom_call" | custom-call | flops 700000000 | bytes 4500000 | tf_op jit(solution)/shard_map/pallas_call | solution.py:551
  189.1 12.5 %all-to-all-done.1.back_ref = bf16[64,24,128]{2,1,0:T(8,128)(2,1)S(1)} async-done(((bf16[64,24,128]{2,1,0:T(8,128)(2,1)}), bf16[64,24,128]{2,1,0:T(8,128)(2,1)S(1)}, u32[]{:S(2)}, u32[]{:S(2)}) %all-to-all-start.1) | async-done | bytes 393248 | tf_op jit(solution)/shard_map/all_to_all | solution.py:549
  201.6 2.1 %shard_map.138 = (bf16[224,128]{1,0:T(8,128)(2,1)}, bf16[224,128]{1,0:T(8,128)(2,1)}, f32[8,128]{1,0:T(8,128)}) custom-call(bf16[64,24,128]{2,1,0:T(8,128)(2,1)S(1)} %all-to-all-done.1.back_ref, f32[128,128]{1,0:T(8,128)S(1)} %get-tuple-element.74.plan_ref, s32[8,128]{1,0:T(8,128)S(1)} %bitcast.28, f32[8,128]{1,0:T(8,128)S(1)} %bitcast.30), custom_call_target="tpu_custom_call" | custom-call | flops 500000000 | bytes 1000000 | tf_op jit(solution)/shard_map/pallas_call | solution.py:561
  (52 shorter events, 9.3 us)
Async XLA Ops:
  0.6 0.7 copy-start.9
  1.3 0.8 copy-start.7
  2.2 0.8 copy-start.8
  3.0 35.5 %copy-start.1 = (bf16[1,224,1024]{2,1,0:T(8,128)(2,1)S(1)}, bf16[1,224,1024]{2,1,0:T(8,128)(2,1)}, u32[]{:S(2)}) copy-start(bf16[1,224,1024]{2,1,0:T(8,128)(2,1)} %param.14) | copy-start | bytes 1376260
  5.4 33.1 %copy-start = (bf16[1,224,1024]{2,1,0:T(8,128)(2,1)S(1)}, bf16[1,224,1024]{2,1,0:T(8,128)(2,1)}, u32[]{:S(2)}) copy-start(bf16[1,224,1024]{2,1,0:T(8,128)(2,1)} %param.13) | copy-start | bytes 1376260
  5.4 33.1 %all-to-all-start = ((bf16[64,24,128]{2,1,0:T(8,128)(2,1)}), bf16[64,24,128]{2,1,0:T(8,128)(2,1)S(1)}, u32[]{:S(2)}, u32[]{:S(2)}) async-start(bf16[64,24,128]{2,1,0:T(8,128)(2,1)} %get-tuple-element.44), calls=%async_computation | async-start | bytes 786432 | tf_op jit(solution)/shard_map/all_to_all | solution.py:510
  38.5 15.0 %copy-start.2 = (bf16[1,1024,224]{1,2,0:T(8,128)(2,1)S(1)}, bf16[1,1024,224]{1,2,0:T(8,128)(2,1)}, u32[]{:S(2)}) copy-start(bf16[1,1024,224]{1,2,0:T(8,128)(2,1)} %param.15) | copy-start | bytes 1376260
  40.3 13.7 %copy-start.3 = (bf16[384,224]{1,0:T(8,128)(2,1)}, bf16[384,224]{1,0:T(8,128)(2,1)S(1)}, u32[]{:S(2)}) copy-start(bf16[384,224]{1,0:T(8,128)(2,1)S(1)} %get-tuple-element.78.tok_ref) | copy-start | bytes 516100
  40.3 13.6 %copy-start.5 = (bf16[384,224]{1,0:T(8,128)(2,1)}, bf16[384,224]{1,0:T(8,128)(2,1)S(1)}, u32[]{:S(2)}) copy-start(bf16[384,224]{1,0:T(8,128)(2,1)S(1)} %get-tuple-element.59.scaled_ref) | copy-start | bytes 516100
  40.4 20.2 %collective-permute-start = (bf16[96,2048]{1,0:T(8,128)(2,1)S(1)}, bf16[96,2048]{1,0:T(8,128)(2,1)S(1)}, u32[]{:S(2)}, u32[]{:S(2)}) collective-permute-start(bf16[96,2048]{1,0:T(8,128)(2,1)S(1)} %get-tuple-element.46), channel_id=1, source_target_pairs={{0,64},{1,961},{2,66},{3,963},{4,68},{5,965},{6,70},{7,967},{8,72}... | collective-permute-start | bytes 1179656 | tf_op jit(solution)/shard_map/ppermute | solution.py:450
  51.6 11.1 %collective-permute-start.1 = (bf16[96,2048]{1,0:T(8,128)(2,1)S(1)}, bf16[96,2048]{1,0:T(8,128)(2,1)S(1)}, u32[]{:S(2)}, u32[]{:S(2)}) collective-permute-start(bf16[96,2048]{1,0:T(8,128)(2,1)S(1)} %get-tuple-element.47), channel_id=1, source_target_pairs={{0,960},{1,65},{2,962},{3,67},{4,964},{5,69},{6,966},{7,71},{8,968... | collective-permute-start | bytes 1179656 | tf_op jit(solution)/shard_map/ppermute | solution.py:450
  54.0 14.9 %collective-permute-start.8 = (bf16[96,1024]{1,0:T(8,128)(2,1)S(1)}, bf16[96,1024]{1,0:T(8,128)(2,1)S(1)}, u32[]{:S(2)}, u32[]{:S(2)}) collective-permute-start(bf16[96,1024]{1,0:T(8,128)(2,1)S(1)} %get-tuple-element.61), channel_id=1, source_target_pairs={{0,64},{1,961},{2,66},{3,963},{4,68},{5,965},{6,70},{7,967},{8,72}... | collective-permute-start | bytes 589832 | tf_op jit(solution)/shard_map/ppermute | solution.py:450
  58.6 10.3 %collective-permute-start.9 = (bf16[96,1024]{1,0:T(8,128)(2,1)S(1)}, bf16[96,1024]{1,0:T(8,128)(2,1)S(1)}, u32[]{:S(2)}, u32[]{:S(2)}) collective-permute-start(bf16[96,1024]{1,0:T(8,128)(2,1)S(1)} %get-tuple-element.62), channel_id=1, source_target_pairs={{0,960},{1,65},{2,962},{3,67},{4,964},{5,69},{6,966},{7,71},{8,968... | collective-permute-start | bytes 589832 | tf_op jit(solution)/shard_map/ppermute | solution.py:450
  62.7 12.7 %collective-permute-start.2 = (bf16[48,2048]{1,0:T(8,128)(2,1)S(1)}, bf16[48,2048]{1,0:T(8,128)(2,1)S(1)}, u32[]{:S(2)}, u32[]{:S(2)}) collective-permute-start(bf16[48,2048]{1,0:T(8,128)(2,1)S(1)} %get-tuple-element.50), channel_id=1, source_target_pairs={{0,64},{1,961},{2,66},{3,963},{4,68},{5,965},{6,70},{7,967},{8,72}... | collective-permute-start | bytes 589832 | tf_op jit(solution)/shard_map/ppermute | solution.py:450
  67.0 8.5 %collective-permute-start.3 = (bf16[48,2048]{1,0:T(8,128)(2,1)S(1)}, bf16[48,2048]{1,0:T(8,128)(2,1)S(1)}, u32[]{:S(2)}, u32[]{:S(2)}) collective-permute-start(bf16[48,2048]{1,0:T(8,128)(2,1)S(1)} %get-tuple-element.51), channel_id=1, source_target_pairs={{0,960},{1,65},{2,962},{3,67},{4,964},{5,69},{6,966},{7,71},{8,968... | collective-permute-start | bytes 589832 | tf_op jit(solution)/shard_map/ppermute | solution.py:450
  69.0 16.0 %collective-permute-start.10 = (bf16[48,1024]{1,0:T(8,128)(2,1)S(1)}, bf16[48,1024]{1,0:T(8,128)(2,1)S(1)}, u32[]{:S(2)}, u32[]{:S(2)}) collective-permute-start(bf16[48,1024]{1,0:T(8,128)(2,1)S(1)} %get-tuple-element.65), channel_id=1, source_target_pairs={{0,64},{1,961},{2,66},{3,963},{4,68},{5,965},{6,70},{7,967},{8,72}... | collective-permute-start | bytes 294920 | tf_op jit(solution)/shard_map/ppermute | solution.py:450
  73.5 11.4 %collective-permute-start.11 = (bf16[48,1024]{1,0:T(8,128)(2,1)S(1)}, bf16[48,1024]{1,0:T(8,128)(2,1)S(1)}, u32[]{:S(2)}, u32[]{:S(2)}) collective-permute-start(bf16[48,1024]{1,0:T(8,128)(2,1)S(1)} %get-tuple-element.66), channel_id=1, source_target_pairs={{0,960},{1,65},{2,962},{3,67},{4,964},{5,69},{6,966},{7,71},{8,968... | collective-permute-start | bytes 294920 | tf_op jit(solution)/shard_map/ppermute | solution.py:450
  75.7 18.5 %collective-permute-start.4 = (bf16[24,2048]{1,0:T(8,128)(2,1)S(1)}, bf16[24,2048]{1,0:T(8,128)(2,1)S(1)}, u32[]{:S(2)}, u32[]{:S(2)}) collective-permute-start(bf16[24,2048]{1,0:T(8,128)(2,1)S(1)} %get-tuple-element.53), channel_id=1, source_target_pairs={{0,256},{1,769},{2,258},{3,771},{4,260},{5,773},{6,262},{7,775},{8... | collective-permute-start | bytes 294920 | tf_op jit(solution)/shard_map/ppermute | solution.py:450
  79.1 15.2 %collective-permute-start.5 = (bf16[24,2048]{1,0:T(8,128)(2,1)S(1)}, bf16[24,2048]{1,0:T(8,128)(2,1)S(1)}, u32[]{:S(2)}, u32[]{:S(2)}) collective-permute-start(bf16[24,2048]{1,0:T(8,128)(2,1)S(1)} %get-tuple-element.54), channel_id=1, source_target_pairs={{0,768},{1,257},{2,770},{3,259},{4,772},{5,261},{6,774},{7,263},{8... | collective-permute-start | bytes 294920 | tf_op jit(solution)/shard_map/ppermute | solution.py:450
  85.1 18.5 %collective-permute-start.12 = (bf16[24,1024]{1,0:T(8,128)(2,1)S(1)}, bf16[24,1024]{1,0:T(8,128)(2,1)S(1)}, u32[]{:S(2)}, u32[]{:S(2)}) collective-permute-start(bf16[24,1024]{1,0:T(8,128)(2,1)S(1)} %get-tuple-element.68), channel_id=1, source_target_pairs={{0,256},{1,769},{2,258},{3,771},{4,260},{5,773},{6,262},{7,775},{8... | collective-permute-start | bytes 147464 | tf_op jit(solution)/shard_map/ppermute | solution.py:450
  88.4 15.1 %collective-permute-start.13 = (bf16[24,1024]{1,0:T(8,128)(2,1)S(1)}, bf16[24,1024]{1,0:T(8,128)(2,1)S(1)}, u32[]{:S(2)}, u32[]{:S(2)}) collective-permute-start(bf16[24,1024]{1,0:T(8,128)(2,1)S(1)} %get-tuple-element.69), channel_id=1, source_target_pairs={{0,768},{1,257},{2,770},{3,259},{4,772},{5,261},{6,774},{7,263},{8... | collective-permute-start | bytes 147464 | tf_op jit(solution)/shard_map/ppermute | solution.py:450
  94.3 22.9 %collective-permute-start.6 = (bf16[24,1024]{1,0:T(8,128)(2,1)S(1)}, bf16[24,1024]{1,0:T(8,128)(2,1)S(1)}, u32[]{:S(2)}, u32[]{:S(2)}) collective-permute-start(bf16[24,1024]{1,0:T(8,128)(2,1)S(1)} %get-tuple-element.57), channel_id=1, source_target_pairs={{0,256},{1,769},{2,258},{3,771},{4,260},{5,773},{6,262},{7,775},{8... | collective-permute-start | bytes 147464 | tf_op jit(solution)/shard_map/ppermute | solution.py:450
  97.9 19.4 %collective-permute-start.7 = (bf16[24,1024]{1,0:T(8,128)(2,1)S(1)}, bf16[24,1024]{1,0:T(8,128)(2,1)S(1)}, u32[]{:S(2)}, u32[]{:S(2)}) collective-permute-start(bf16[24,1024]{1,0:T(8,128)(2,1)S(1)} %get-tuple-element.58), channel_id=1, source_target_pairs={{0,768},{1,257},{2,770},{3,259},{4,772},{5,261},{6,774},{7,263},{8... | collective-permute-start | bytes 147464 | tf_op jit(solution)/shard_map/ppermute | solution.py:450
  103.6 9.2 %collective-permute-start.14 = (bf16[24,512]{1,0:T(8,128)(2,1)S(1)}, bf16[24,512]{1,0:T(8,128)(2,1)S(1)}, u32[]{:S(2)}, u32[]{:S(2)}) collective-permute-start(bf16[24,512]{1,0:T(8,128)(2,1)S(1)} %get-tuple-element.72), channel_id=1, source_target_pairs={{0,256},{1,769},{2,258},{3,771},{4,260},{5,773},{6,262},{7,775},{8... | collective-permute-start | bytes 73736 | tf_op jit(solution)/shard_map/ppermute | solution.py:450
  107.1 10.1 %collective-permute-start.15 = (bf16[24,512]{1,0:T(8,128)(2,1)S(1)}, bf16[24,512]{1,0:T(8,128)(2,1)S(1)}, u32[]{:S(2)}, u32[]{:S(2)}) collective-permute-start(bf16[24,512]{1,0:T(8,128)(2,1)S(1)} %get-tuple-element.73), channel_id=1, source_target_pairs={{0,768},{1,257},{2,770},{3,259},{4,772},{5,261},{6,774},{7,263},{8... | collective-permute-start | bytes 73736 | tf_op jit(solution)/shard_map/ppermute | solution.py:450
  144.6 11.2 %collective-permute-start.16 = (bf16[96,3200]{1,0:T(8,128)(2,1)S(1)}, bf16[96,3200]{1,0:T(8,128)(2,1)S(1)}, u32[]{:S(2)}, u32[]{:S(2)}) collective-permute-start(bf16[96,3200]{1,0:T(8,128)(2,1)S(1)} %all_gather.3.own_ref), channel_id=1, source_target_pairs={{0,64},{1,961},{2,66},{3,963},{4,68},{5,965},{6,70},{7,967},{8,72}... | collective-permute-start | bytes 1843208 | tf_op jit(solution)/shard_map/ppermute | solution.py:450
  146.6 16.4 %collective-permute-start.17 = (bf16[96,3200]{1,0:T(8,128)(2,1)S(1)}, bf16[96,3200]{1,0:T(8,128)(2,1)S(1)}, u32[]{:S(2)}, u32[]{:S(2)}) collective-permute-start(bf16[96,3200]{1,0:T(8,128)(2,1)S(1)} %all_gather.3.own_ref), channel_id=1, source_target_pairs={{0,960},{1,65},{2,962},{3,67},{4,964},{5,69},{6,966},{7,71},{8,968... | collective-permute-start | bytes 1843208 | tf_op jit(solution)/shard_map/ppermute | solution.py:450
  155.8 11.1 %collective-permute-start.18 = (bf16[48,3200]{1,0:T(8,128)(2,1)S(1)}, bf16[48,3200]{1,0:T(8,128)(2,1)S(1)}, u32[]{:S(2)}, u32[]{:S(2)}) collective-permute-start(bf16[48,3200]{1,0:T(8,128)(2,1)S(1)} %slice.8), channel_id=1, source_target_pairs={{0,64},{1,961},{2,66},{3,963},{4,68},{5,965},{6,70},{7,967},{8,72}... | collective-permute-start | bytes 921608 | tf_op jit(solution)/shard_map/ppermute | solution.py:450
  163.0 9.4 %collective-permute-start.19 = (bf16[48,3200]{1,0:T(8,128)(2,1)S(1)}, bf16[48,3200]{1,0:T(8,128)(2,1)S(1)}, u32[]{:S(2)}, u32[]{:S(2)}) collective-permute-start(bf16[48,3200]{1,0:T(8,128)(2,1)S(1)} %slice.9), channel_id=1, source_target_pairs={{0,960},{1,65},{2,962},{3,67},{4,964},{5,69},{6,966},{7,71},{8,968... | collective-permute-start | bytes 921608 | tf_op jit(solution)/shard_map/ppermute | solution.py:450
  175.7 11.3 %copy-start.4 = (bf16[384,224]{1,0:T(8,128)(2,1)S(1)}, bf16[384,224]{1,0:T(8,128)(2,1)}, u32[]{:S(2)}) copy-start(bf16[384,224]{1,0:T(8,128)(2,1)} %copy-done.3) | copy-start | bytes 516100
  175.7 11.3 %copy-start.6 = (bf16[384,224]{1,0:T(8,128)(2,1)S(1)}, bf16[384,224]{1,0:T(8,128)(2,1)}, u32[]{:S(2)}) copy-start(bf16[384,224]{1,0:T(8,128)(2,1)} %copy-done.5) | copy-start | bytes 516100
  175.7 25.9 %all-to-all-start.1 = ((bf16[64,24,128]{2,1,0:T(8,128)(2,1)}), bf16[64,24,128]{2,1,0:T(8,128)(2,1)S(1)}, u32[]{:S(2)}, u32[]{:S(2)}) async-start(bf16[64,24,128]{2,1,0:T(8,128)(2,1)} %shard_map.137), calls=%async_computation.1 | async-start | bytes 786432 | tf_op jit(solution)/shard_map/all_to_all | solution.py:549
  (2 other events, 1.4 us)

commit v9 on v3

--- a/solution.py
+++ b/solution.py
@@ -13,6 +13,8 @@
 SOURCES = 16
 RING = 4
 SCORE_LANE = 96
+WEIGHT_PARTS = 2
+PLACE_BITS = 4
 VMEM_LIMIT = 24 * 1024 * 1024
 
 F32 = jnp.float32
@@ -65,6 +67,11 @@
     within = sorted_row - per_tile * tile
     source = lax.shift_right_logical(within * 43, 8)
     return one_zero(sent_row == within + (GROUP - CAP) * source + CAP * tile)
+
+
+def member_at(base, place_ref, step):
+    sign = 1 - 2 * lax.shift_right_logical(place_ref[0], PLACE_BITS)
+    return (base + sign * step) & (RING - 1)
 
 
 def fetch(sources, targets, sems):
@@ -175,7 +182,7 @@
             (RING - 1, ((to_left_ref, 0), (previous_ref, 0))),
             (0, ((own_ref, 0), (own_ref, half))),
         ):
-            member = (place_ref[0] + step) & (RING - 1)
+            member = member_at(place_ref[0], place_ref, step)
             begin = pl.multiple_of(member * held, held)
             value = dot(rows_ref[pl.ds(begin, held)], ref[...]).astype(BF16)
             for part, (out_ref, start) in enumerate(pieces):
@@ -231,7 +238,7 @@
         (far_left_ref, RING // 2, 0),
         (far_right_ref, RING // 2, half),
     ):
-        member = (place_ref[0] + step) & (RING - 1)
+        member = member_at(place_ref[0], place_ref, step)
         begin = pl.multiple_of(member * held + start, half)
         full_ref[pl.ds(begin, ref.shape[0])] = ref[...]
 
@@ -304,38 +311,44 @@
         )
 
 
-def combine_kernel(back_ref, plan_ref, routes_ref, weight_ref, mixed_ref, input_ref, score_ref):
+def combine_kernel(
+    back_ref, plan_ref, routes_ref, weight_ref, mixed_ref, input_ref, score_ref, chosen_ref
+):
     top_count, token_count = routes_ref.shape
-    experts = plan_ref.shape[0] // 2
+    experts = back_ref.shape[0]
     width = mixed_ref.shape[0]
     rows = experts * GROUP
     back = back_ref[...].reshape(rows, LANES)
     plan = plan_ref[...].T
     rank, scale = plan[:, :experts], plan[:, experts:]
     spread = one_zero(expert_of_row(iota((experts, rows), 1), iota((experts, rows), 0)))
-    tile, slot = tile_and_slot(iota((token_count, rows), 1))
+    tile, slot = tile_and_slot(iota((1, rows), 1))
     taken = dot(rank.astype(BF16), spread) == slot.astype(F32)
-    mixed = [jnp.zeros((token_count, LANES), F32) for _ in range(2)]
-    for part in three_parts(scale):
-        row_scale = dot(part, spread)
+    for order, part in enumerate(three_parts(scale)[:WEIGHT_PARTS]):
+        row_scale = jnp.where(taken, dot(part, spread), 0.0)
         for index in range(2):
-            chosen = jnp.where(taken & (tile == index), row_scale, 0.0).astype(BF16)
-            mixed[index] = mixed[index] + dot(chosen, back)
+            place = (index * WEIGHT_PARTS + order) * token_count
+            chosen_ref[place : place + token_count] = jnp.where(tile == index, row_scale, 0.0).astype(BF16)
+    taken = jnp.where(taken, 1.0, 0.0)
+    for index in range(2):
+        place = (2 * WEIGHT_PARTS + index) * token_count
+        chosen_ref[place : place + token_count] = jnp.where(tile == 2 + index, taken, 0.0).astype(BF16)
+    scored = jnp.where(tile == 1, taken, 0.0).astype(BF16)
+    values = dot(chosen_ref[...], back)
+    blocks = [values[i * token_count : (i + 1) * token_count] for i in range(2 * WEIGHT_PARTS + 2)]
+    low, high = sum(blocks[:WEIGHT_PARTS]), sum(blocks[WEIGHT_PARTS : 2 * WEIGHT_PARTS])
     for ref, low, high in (
-        (mixed_ref, mixed[0], mixed[1]),
-        (
-            input_ref,
-            dot(one_zero(taken & (tile == 2)), back),
-            dot(one_zero(taken & (tile == 3)), back),
-        ),
+        (mixed_ref, low, high),
+        (input_ref, blocks[2 * WEIGHT_PARTS], blocks[2 * WEIGHT_PARTS + 1]),
     ):
         ref[:LANES] = low.T.astype(BF16)
         ref[LANES:] = high.T[: width - LANES].astype(BF16)
-    lane = iota((8, LANES), 1)
-    score_lanes = one_zero((lane >= SCORE_LANE) & (lane < SCORE_LANE + 3))
-    row_score = dot(score_lanes, back, CONTRACT_LAST)[:1]
-    routed = jnp.where(taken & (tile == 1), row_score, 0.0)
-    by_expert = sum(dot(spread, part, CONTRACT_LAST) for part in three_parts(routed))
+    lane_of_part = iota((8, LANES), 1) - SCORE_LANE == iota((8, LANES), 0)
+    row_score = dot(one_zero(lane_of_part & (iota((8, LANES), 0) < 3)), back, CONTRACT_LAST)
+    spread = spread.astype(F32)
+    spread = jnp.concatenate([(spread * row_score[i : i + 1]).astype(BF16) for i in range(3)], axis=0)
+    by_expert = dot(spread, scored, CONTRACT_LAST)
+    by_expert = sum(by_expert[i * experts : (i + 1) * experts] for i in range(3))
     expert = iota((experts, token_count), 0)
     for k in range(top_count):
         hit = routes_ref[k : k + 1] == expert
@@ -365,8 +378,13 @@
 
 
 def shifted(block, distance):
-    parts = lax.axis_size("expert")
-    return lax.ppermute(block, "expert", [(i, (i + distance) % parts) for i in range(parts)])
+    parts, columns = lax.axis_size("expert"), lax.axis_size("dp")
+    route = [
+        (part * columns + column, (part + (1 - 2 * (column % 2)) * distance) % parts * columns + column)
+        for part in range(parts)
+        for column in range(columns)
+    ]
+    return lax.ppermute(block, ("expert", "dp"), route)
 
 
 def per_device(
@@ -383,7 +401,8 @@
     rows = shape((row_count, width), BF16)
     whole, halved = (shape((size, 3 * hidden), BF16) for size in (held, held // 2))
     groups = [list(range(i, parts, RING)) for i in range(RING)]
-    member = (lax.axis_index("expert") % RING).astype(jnp.int32).reshape(1)
+    member = lax.axis_index("expert") + ((lax.axis_index("dp") & 1) << PLACE_BITS)
+    member = member.astype(jnp.int32).reshape(1)
     weights = (gate_weight[0], up_weight[0], down_weight[0].T)
     arguments = (routes.T, route_weights.T, owner_slots.reshape(1, experts), tokens.T, cotangent.T)
     send, plan = kernel_call(
@@ -447,6 +466,7 @@
         (token_shape, token_shape, shape(arguments[0].shape, F32)),
         500_000_000,
         1_000_000,
+        scratch=[pltpu.VMEM(((2 * WEIGHT_PARTS + 2) * token_count, experts * GROUP), BF16)],
     )(returned, plan, arguments[0], arguments[1])
     return (
         mixed.T,

time: 201 us -> 205 us (1.020)
  starting transfers between devices: 76.5 us -> 61 us
  blocking collectives: 50.2 us -> 60.3 us
  waiting for transfers between devices: 56.8 us -> 66.6 us
    all_to_all x1, blocking collectives: 21.3 us -> 34.8 us  [per_device(): lax.all_to_all(window, 'expert', split_axis=0, concat_axis=0, tiled=True,...]
    ppermute x8, starting transfers between devices: 45.4 us -> 34.1 us  [shifted(): return lax.ppermute(block, ('expert', 'dp'), route)]
    ppermute x8, waiting for transfers between devices: 29.6 us -> 39.4 us  [shifted(): return lax.ppermute(block, ('expert', 'dp'), route)]
    all_to_all x1, starting transfers between devices: 12.7 us -> 8.59 us  [per_device(): lax.all_to_all(back, 'dp', split_axis=0, concat_axis=0, tiled=True)]
    all_gather x1, blocking collectives: 29 us -> 25.5 us  [per_device(): lax.all_gather(share, 'expert', axis=0, tiled=True, axis_index_groups=gro...]
where the time goes in v9:
time: 205 us; the launch traced here: 204 us
  waiting for transfers between devices  66.6 us (32%)
  starting transfers between devices  61 us (30%)
  blocking collectives  60.3 us (29%)
  Pallas kernels  12.9 us (6%)
  local copies, waits for them, and re-layouts  2.41 us (1%)
    ppermute x8, waiting for transfers between devices, shifted(): return lax.ppermute(block, ('expert', 'dp'), route)  39.4 us
    all_to_all x1, blocking collectives, per_device(): lax.all_to_all(window, 'expert', split_axis=0, concat_axis=0, tiled=True,...  34.8 us
    ppermute x8, starting transfers between devices, shifted(): return lax.ppermute(block, ('expert', 'dp'), route)  34.1 us
    all_gather x1, blocking collectives, per_device(): lax.all_gather(share, 'expert', axis=0, tiled=True, axis_index_groups=gro...  25.5 us
    all_to_all x1, starting transfers between devices, per_device(): lax.all_to_all(send, 'dp', split_axis=0, concat_axis=0, tiled=True)  18.4 us
    all_to_all x1, waiting for transfers between devices, per_device(): lax.all_to_all(send, 'dp', split_axis=0, concat_axis=0, tiled=True)  14.7 us
    all_to_all x1, waiting for transfers between devices, per_device(): lax.all_to_all(back, 'dp', split_axis=0, concat_axis=0, tiled=True)  12.5 us
    all_to_all x1, starting transfers between devices, per_device(): lax.all_to_all(back, 'dp', split_axis=0, concat_axis=0, tiled=True)  8.59 us
  transfers between devices with their start and end apart: 10, of which 9 were waited for; matrix products, arithmetic and copies ran while one was open for 0% of the time, Pallas kernels for 1%

profile of v9, /device:TPU:1, one launch (start us, length us, event | category | flops | bytes accessed | tf_op | source)
XLA Modules:
  0.0 204.1 jit_solution(10933528262578355683)
XLA Ops:
  0.7 0.7 copy-done.11
  1.3 0.8 copy-done.8
  2.2 0.8 copy-done.9
  3.0 2.4 %shard_map.127 = (bf16[64,24,128]{2,1,0:T(8,128)(2,1)}, f32[128,128]{1,0:T(8,128)S(1)}) custom-call(s32[8,128]{1,0:T(8,128)S(1)} %bitcast.31, f32[8,128]{1,0:T(8,128)S(1)} %bitcast.33, s32[1,64]{1,0:T(1,128)S(1)} %bitcast.35, bf16[224,128]{1,0:T(8,128)(2,1)S(1)} %bitcast.29, bf16[224,128]{1,0:T(8,128)(2,1)S(1)} %bitcast.30), custom_call_target="tpu_custom_call" | custom-call | flops 300000000 | bytes 1000000 | tf_op jit(solution)/shard_map/pallas_call | solution.py:408
  5.4 18.4 %all-to-all-start = ((bf16[64,24,128]{2,1,0:T(8,128)(2,1)}), bf16[64,24,128]{2,1,0:T(8,128)(2,1)S(1)}, u32[]{:S(2)}, u32[]{:S(2)}) async-start(bf16[64,24,128]{2,1,0:T(8,128)(2,1)} %get-tuple-element.23), calls=%async_computation | async-start | bytes 786432 | tf_op jit(solution)/shard_map/all_to_all | solution.py:416
  23.8 14.7 %all-to-all-done.recv_ref = bf16[64,24,128]{2,1,0:T(8,128)(2,1)S(1)} async-done(((bf16[64,24,128]{2,1,0:T(8,128)(2,1)}), bf16[64,24,128]{2,1,0:T(8,128)(2,1)S(1)}, u32[]{:S(2)}, u32[]{:S(2)}) %all-to-all-start) | async-done | bytes 393248 | tf_op jit(solution)/shard_map/all_to_all | solution.py:416
  38.5 2.4 %shard_map.128 = (bf16[96,3072]{1,0:T(8,128)(2,1)S(1)}, bf16[96,3072]{1,0:T(8,128)(2,1)S(1)}, bf16[96,3072]{1,0:T(8,128)(2,1)S(1)}, bf16[48,3072]{1,0:T(8,128)(2...) custom-call(s32[1]{0:T(128)} %bitcast.place_ref, ...), custom_call_target="tpu_custom_call" | custom-call | flops 700000000 | bytes 4500000 | tf_op jit(solution)/shard_map/pallas_call | solution.py:417
  40.9 11.2 %collective-permute-start = (bf16[96,3072]{1,0:T(8,128)(2,1)S(1)}, bf16[96,3072]{1,0:T(8,128)(2,1)S(1)}, u32[]{:S(2)}, u32[]{:S(2)}) collective-permute-start(bf16[96,3072]{1,0:T(8,128)(2,1)S(1)} %get-tuple-element.25), channel_id=1, source_target_pairs={{0,64},{1,961},{2,66},{3,963},{4,68},{5,965},{6,70},{7,967},{8,72}... | collective-permute-start | bytes 1769480 | tf_op jit(solution)/shard_map/ppermute | solution.py:387
  52.2 1.9 collective-permute-start.1
  54.1 8.3 %collective-permute-done.from_left_ref = bf16[96,3072]{1,0:T(8,128)(2,1)S(1)} collective-permute-done((bf16[96,3072]{1,0:T(8,128)(2,1)S(1)}, bf16[96,3072]{1,0:T(8,128)(2,1)S(1)}, u32[]{:S(2)}, u32[]{:S(2)}) %collective-permute-start) | collective-permute-done | bytes 589856 | tf_op jit(solution)/shard_map/ppermute | solution.py:387
  62.5 3.9 %collective-permute-done.1.from_right_ref = bf16[96,3072]{1,0:T(8,128)(2,1)S(1)} collective-permute-done((bf16[96,3072]{1,0:T(8,128)(2,1)S(1)}, bf16[96,3072]{1,0:T(8,128)(2,1)S(1)}, u32[]{:S(2)}, u32[]{:S(2)}) %collective-permute-start.1) | collective-permute-done | bytes 589856 | tf_op jit(solution)/shard_map/ppermute | solution.py:387
  66.3 0.1 shard_map.129
  66.5 3.9 %collective-permute-start.2 = (bf16[48,3072]{1,0:T(8,128)(2,1)S(1)}, bf16[48,3072]{1,0:T(8,128)(2,1)S(1)}, u32[]{:S(2)}, u32[]{:S(2)}) collective-permute-start(bf16[48,3072]{1,0:T(8,128)(2,1)S(1)} %get-tuple-element.29), channel_id=1, source_target_pairs={{0,64},{1,961},{2,66},{3,963},{4,68},{5,965},{6,70},{7,967},{8,72}... | collective-permute-start | bytes 884744 | tf_op jit(solution)/shard_map/ppermute | solution.py:387
  70.4 1.9 collective-permute-start.3
  72.4 3.2 %collective-permute-done.2.far_left_ref = bf16[48,3072]{1,0:T(8,128)(2,1)S(1)} collective-permute-done((bf16[48,3072]{1,0:T(8,128)(2,1)S(1)}, bf16[48,3072]{1,0:T(8,128)(2,1)S(1)}, u32[]{:S(2)}, u32[]{:S(2)}) %collective-permute-start.2) | collective-permute-done | bytes 294944 | tf_op jit(solution)/shard_map/ppermute | solution.py:387
  75.6 3.5 %collective-permute-done.3.far_right_ref = bf16[48,3072]{1,0:T(8,128)(2,1)S(1)} collective-permute-done((bf16[48,3072]{1,0:T(8,128)(2,1)S(1)}, bf16[48,3072]{1,0:T(8,128)(2,1)S(1)}, u32[]{:S(2)}, u32[]{:S(2)}) %collective-permute-start.3) | collective-permute-done | bytes 294944 | tf_op jit(solution)/shard_map/ppermute | solution.py:387
  79.1 0.2 shard_map.130
  79.3 34.8 %all_to_all.21 = bf16[4,24,3072]{2,1,0:T(8,128)(2,1)S(1)} all-to-all(bf16[4,24,3072]{2,1,0:T(8,128)(2,1)S(1)} %bitcast.22), channel_id=1, replica_groups={{0,256,512,768},{64,320,576,832},{128,384,640,896},{192,448,704,960},{1..., dimensions={0} | all-to-all | bytes 1179648 | tf_op jit(solution)/shard_map/all_to_all | solution.py:433
  114.2 0.2 shard_map.131
  114.3 25.5 %all_gather.3.own_ref = bf16[96,3200]{1,0:T(8,128)(2,1)S(1)} all-gather(bf16[24,3200]{1,0:T(8,128)(2,1)S(1)} %shard_map.131), channel_id=1, replica_groups={{0,256,512,768},{64,320,576,832},{128,384,640,896},{192,448,704,960},{1..., dimensions={0}, use_global_device_ids=true | all-gather | bytes 768000 | tf_op jit(solution)/shard_map/all_gather | solution.py:439
  139.8 5.8 %collective-permute-start.4 = (bf16[96,3200]{1,0:T(8,128)(2,1)S(1)}, bf16[96,3200]{1,0:T(8,128)(2,1)S(1)}, u32[]{:S(2)}, u32[]{:S(2)}) collective-permute-start(bf16[96,3200]{1,0:T(8,128)(2,1)S(1)} %all_gather.3.own_ref), channel_id=1, source_target_pairs={{0,64},{1,961},{2,66},{3,963},{4,68},{5,965},{6,70},{7,967},{8,72}... | collective-permute-start | bytes 1843208 | tf_op jit(solution)/shard_map/ppermute | solution.py:387
  145.6 1.9 collective-permute-start.5
  147.6 5.4 %collective-permute-done.4.left_ref = bf16[96,3200]{1,0:T(8,128)(2,1)S(1)} collective-permute-done((bf16[96,3200]{1,0:T(8,128)(2,1)S(1)}, bf16[96,3200]{1,0:T(8,128)(2,1)S(1)}, u32[]{:S(2)}, u32[]{:S(2)}) %collective-permute-start.4) | collective-permute-done | bytes 614432 | tf_op jit(solution)/shard_map/ppermute | solution.py:387
  153.0 5.5 %collective-permute-start.6 = (bf16[48,3200]{1,0:T(8,128)(2,1)S(1)}, bf16[48,3200]{1,0:T(8,128)(2,1)S(1)}, u32[]{:S(2)}, u32[]{:S(2)}) collective-permute-start(bf16[48,3200]{1,0:T(8,128)(2,1)S(1)} %slice.8), channel_id=1, source_target_pairs={{0,64},{1,961},{2,66},{3,963},{4,68},{5,965},{6,70},{7,967},{8,72}... | collective-permute-start | bytes 921608 | tf_op jit(solution)/shard_map/ppermute | solution.py:387
  158.5 5.3 %collective-permute-done.5.right_ref = bf16[96,3200]{1,0:T(8,128)(2,1)S(1)} collective-permute-done((bf16[96,3200]{1,0:T(8,128)(2,1)S(1)}, bf16[96,3200]{1,0:T(8,128)(2,1)S(1)}, u32[]{:S(2)}, u32[]{:S(2)}) %collective-permute-start.5) | collective-permute-done | bytes 614432 | tf_op jit(solution)/shard_map/ppermute | solution.py:387
  163.8 1.9 collective-permute-start.7
  165.7 9.7 %collective-permute-done.7.far_right_ref = bf16[48,3200]{1,0:T(8,128)(2,1)S(1)} collective-permute-done((bf16[48,3200]{1,0:T(8,128)(2,1)S(1)}, bf16[48,3200]{1,0:T(8,128)(2,1)S(1)}, u32[]{:S(2)}, u32[]{:S(2)}) %collective-permute-start.7) | collective-permute-done | bytes 307232 | tf_op jit(solution)/shard_map/ppermute | solution.py:387
  175.4 3.3 %shard_map.132 = bf16[64,24,128]{2,1,0:T(8,128)(2,1)} custom-call(s32[1]{0:T(128)} %bitcast.place_ref, bf16[96,3200]{1,0:T(8,128)(2,1)S(1)} %all_gather.3.own_ref, bf16[96,3200]{1,0:T(8,128)(2,1)S(1)} %collective-permute-done.4.left_ref, bf16[96,3200]{1,0:T(8,128)(2,1)S(1)} %collective-permute-done.5.right_ref, ...), custom_call_target="tpu_custom_call" | custom-call | flops 700000000 | bytes 4500000 | tf_op jit(solution)/shard_map/pallas_call | solution.py:444
  178.8 8.6 %all-to-all-start.2 = ((bf16[64,24,128]{2,1,0:T(8,128)(2,1)}), bf16[64,24,128]{2,1,0:T(8,128)(2,1)S(1)}, u32[]{:S(2)}, u32[]{:S(2)}) async-start(bf16[64,24,128]{2,1,0:T(8,128)(2,1)} %shard_map.132), calls=%async_computation.2 | async-start | bytes 786432 | tf_op jit(solution)/shard_map/all_to_all | solution.py:452
  187.4 2.1 %shard_map.134 = (bf16[224,1024]{1,0:T(8,128)(2,1)}, bf16[224,1024]{1,0:T(8,128)(2,1)}, bf16[224,1024]{1,0:T(8,128)(2,1)}) custom-call(s32[1]{0:T(128)} %bitcast.place_ref, bf16[96,3200]{1,0:T(8,128)(2,1)S(1)} %all_gather.3.own_ref, bf16[96,3200]{1,0:T(8,128)(2,1)S(1)} %collective-permute-done.4.left_ref, ...), custom_call_target="tpu_custom_call" | custom-call | flops 700000000 | bytes 4500000 | tf_op jit(solution)/shard_map/pallas_call | solution.py:454
  189.5 12.5 %all-to-all-done.2.back_ref = bf16[64,24,128]{2,1,0:T(8,128)(2,1)S(1)} async-done(((bf16[64,24,128]{2,1,0:T(8,128)(2,1)}), bf16[64,24,128]{2,1,0:T(8,128)(2,1)S(1)}, u32[]{:S(2)}, u32[]{:S(2)}) %all-to-all-start.2) | async-done | bytes 393248 | tf_op jit(solution)/shard_map/all_to_all | solution.py:452
  202.0 2.1 %shard_map.133 = (bf16[224,128]{1,0:T(8,128)(2,1)}, bf16[224,128]{1,0:T(8,128)(2,1)}, f32[8,128]{1,0:T(8,128)}) custom-call(bf16[64,24,128]{2,1,0:T(8,128)(2,1)S(1)} %all-to-all-done.2.back_ref, f32[128,128]{1,0:T(8,128)S(1)} %get-tuple-element.31.plan_ref, s32[8,128]{1,0:T(8,128)S(1)} %bitcast.32, f32[8,128]{1,0:T(8,128)S(1)} %bitcast.34), custom_call_target="tpu_custom_call" | custom-call | flops 500000000 | bytes 1000000 | tf_op jit(solution)/shard_map/pallas_call | solution.py:464
  (26 shorter events, 0.1 us)
Async XLA Ops:
  0.6 0.7 copy-start.11
  0.6 0.7 copy-start.10
  0.7 0.7 copy-start.12
  1.3 0.8 copy-start.8
  2.2 0.8 copy-start.9
  3.0 35.5 %copy-start.1 = (bf16[1,224,1024]{2,1,0:T(8,128)(2,1)S(1)}, bf16[1,224,1024]{2,1,0:T(8,128)(2,1)}, u32[]{:S(2)}) copy-start(bf16[1,224,1024]{2,1,0:T(8,128)(2,1)} %param.14) | copy-start | bytes 1376260
  3.0 35.5 %copy-start.2 = (bf16[1,1024,224]{1,2,0:T(8,128)(2,1)S(1)}, bf16[1,1024,224]{1,2,0:T(8,128)(2,1)}, u32[]{:S(2)}) copy-start(bf16[1,1024,224]{1,2,0:T(8,128)(2,1)} %param.15) | copy-start | bytes 1376260
  5.4 33.1 %copy-start = (bf16[1,224,1024]{2,1,0:T(8,128)(2,1)S(1)}, bf16[1,224,1024]{2,1,0:T(8,128)(2,1)}, u32[]{:S(2)}) copy-start(bf16[1,224,1024]{2,1,0:T(8,128)(2,1)} %param.13) | copy-start | bytes 1376260
  5.4 33.1 %all-to-all-start = ((bf16[64,24,128]{2,1,0:T(8,128)(2,1)}), bf16[64,24,128]{2,1,0:T(8,128)(2,1)S(1)}, u32[]{:S(2)}, u32[]{:S(2)}) async-start(bf16[64,24,128]{2,1,0:T(8,128)(2,1)} %get-tuple-element.23), calls=%async_computation | async-start | bytes 786432 | tf_op jit(solution)/shard_map/all_to_all | solution.py:416
  40.9 25.6 %copy-start.4 = (bf16[384,224]{1,0:T(8,128)(2,1)}, bf16[384,224]{1,0:T(8,128)(2,1)S(1)}, u32[]{:S(2)}) copy-start(bf16[384,224]{1,0:T(8,128)(2,1)S(1)} %get-tuple-element.35.tok_ref) | copy-start | bytes 516100
  40.9 25.6 %copy-start.6 = (bf16[384,224]{1,0:T(8,128)(2,1)}, bf16[384,224]{1,0:T(8,128)(2,1)S(1)}, u32[]{:S(2)}) copy-start(bf16[384,224]{1,0:T(8,128)(2,1)S(1)} %get-tuple-element.36.scaled_ref) | copy-start | bytes 516100
  40.9 21.5 %collective-permute-start = (bf16[96,3072]{1,0:T(8,128)(2,1)S(1)}, bf16[96,3072]{1,0:T(8,128)(2,1)S(1)}, u32[]{:S(2)}, u32[]{:S(2)}) collective-permute-start(bf16[96,3072]{1,0:T(8,128)(2,1)S(1)} %get-tuple-element.25), channel_id=1, source_target_pairs={{0,64},{1,961},{2,66},{3,963},{4,68},{5,965},{6,70},{7,967},{8,72}... | collective-permute-start | bytes 1769480 | tf_op jit(solution)/shard_map/ppermute | solution.py:387
  52.2 14.2 %collective-permute-start.1 = (bf16[96,3072]{1,0:T(8,128)(2,1)S(1)}, bf16[96,3072]{1,0:T(8,128)(2,1)S(1)}, u32[]{:S(2)}, u32[]{:S(2)}) collective-permute-start(bf16[96,3072]{1,0:T(8,128)(2,1)S(1)} %get-tuple-element.26), channel_id=1, source_target_pairs={{0,960},{1,65},{2,962},{3,67},{4,964},{5,69},{6,966},{7,71},{8,968... | collective-permute-start | bytes 1769480 | tf_op jit(solution)/shard_map/ppermute | solution.py:387
  66.5 9.1 %collective-permute-start.2 = (bf16[48,3072]{1,0:T(8,128)(2,1)S(1)}, bf16[48,3072]{1,0:T(8,128)(2,1)S(1)}, u32[]{:S(2)}, u32[]{:S(2)}) collective-permute-start(bf16[48,3072]{1,0:T(8,128)(2,1)S(1)} %get-tuple-element.29), channel_id=1, source_target_pairs={{0,64},{1,961},{2,66},{3,963},{4,68},{5,965},{6,70},{7,967},{8,72}... | collective-permute-start | bytes 884744 | tf_op jit(solution)/shard_map/ppermute | solution.py:387
  70.4 8.7 %collective-permute-start.3 = (bf16[48,3072]{1,0:T(8,128)(2,1)S(1)}, bf16[48,3072]{1,0:T(8,128)(2,1)S(1)}, u32[]{:S(2)}, u32[]{:S(2)}) collective-permute-start(bf16[48,3072]{1,0:T(8,128)(2,1)S(1)} %get-tuple-element.30), channel_id=1, source_target_pairs={{0,960},{1,65},{2,962},{3,67},{4,964},{5,69},{6,966},{7,71},{8,968... | collective-permute-start | bytes 884744 | tf_op jit(solution)/shard_map/ppermute | solution.py:387
  139.8 13.1 %collective-permute-start.4 = (bf16[96,3200]{1,0:T(8,128)(2,1)S(1)}, bf16[96,3200]{1,0:T(8,128)(2,1)S(1)}, u32[]{:S(2)}, u32[]{:S(2)}) collective-permute-start(bf16[96,3200]{1,0:T(8,128)(2,1)S(1)} %all_gather.3.own_ref), channel_id=1, source_target_pairs={{0,64},{1,961},{2,66},{3,963},{4,68},{5,965},{6,70},{7,967},{8,72}... | collective-permute-start | bytes 1843208 | tf_op jit(solution)/shard_map/ppermute | solution.py:387
  145.6 18.1 %collective-permute-start.5 = (bf16[96,3200]{1,0:T(8,128)(2,1)S(1)}, bf16[96,3200]{1,0:T(8,128)(2,1)S(1)}, u32[]{:S(2)}, u32[]{:S(2)}) collective-permute-start(bf16[96,3200]{1,0:T(8,128)(2,1)S(1)} %all_gather.3.own_ref), channel_id=1, source_target_pairs={{0,960},{1,65},{2,962},{3,67},{4,964},{5,69},{6,966},{7,71},{8,968... | collective-permute-start | bytes 1843208 | tf_op jit(solution)/shard_map/ppermute | solution.py:387
  153.0 22.4 %copy-start.3 = (bf16[1,1024,224]{1,2,0:T(8,128)(2,1)S(1)}, bf16[1,1024,224]{1,2,0:T(8,128)(2,1)}, u32[]{:S(2)}) copy-start(bf16[1,1024,224]{1,2,0:T(8,128)(2,1)} %param.15) | copy-start | bytes 1376260
  153.0 12.7 %collective-permute-start.6 = (bf16[48,3200]{1,0:T(8,128)(2,1)S(1)}, bf16[48,3200]{1,0:T(8,128)(2,1)S(1)}, u32[]{:S(2)}, u32[]{:S(2)}) collective-permute-start(bf16[48,3200]{1,0:T(8,128)(2,1)S(1)} %slice.8), channel_id=1, source_target_pairs={{0,64},{1,961},{2,66},{3,963},{4,68},{5,965},{6,70},{7,967},{8,72}... | collective-permute-start | bytes 921608 | tf_op jit(solution)/shard_map/ppermute | solution.py:387
  163.8 11.6 %collective-permute-start.7 = (bf16[48,3200]{1,0:T(8,128)(2,1)S(1)}, bf16[48,3200]{1,0:T(8,128)(2,1)S(1)}, u32[]{:S(2)}, u32[]{:S(2)}) collective-permute-start(bf16[48,3200]{1,0:T(8,128)(2,1)S(1)} %slice.9), channel_id=1, source_target_pairs={{0,960},{1,65},{2,962},{3,67},{4,964},{5,69},{6,966},{7,71},{8,968... | collective-permute-start | bytes 921608 | tf_op jit(solution)/shard_map/ppermute | solution.py:387
  178.7 8.6 %copy-start.5 = (bf16[384,224]{1,0:T(8,128)(2,1)S(1)}, bf16[384,224]{1,0:T(8,128)(2,1)}, u32[]{:S(2)}) copy-start(bf16[384,224]{1,0:T(8,128)(2,1)} %copy-done.4) | copy-start | bytes 516100
  178.8 8.6 %copy-start.7 = (bf16[384,224]{1,0:T(8,128)(2,1)S(1)}, bf16[384,224]{1,0:T(8,128)(2,1)}, u32[]{:S(2)}) copy-start(bf16[384,224]{1,0:T(8,128)(2,1)} %copy-done.6) | copy-start | bytes 516100
  178.8 23.2 %all-to-all-start.2 = ((bf16[64,24,128]{2,1,0:T(8,128)(2,1)}), bf16[64,24,128]{2,1,0:T(8,128)(2,1)S(1)}, u32[]{:S(2)}, u32[]{:S(2)}) async-start(bf16[64,24,128]{2,1,0:T(8,128)(2,1)} %shard_map.132), calls=%async_computation.2 | async-start | bytes 786432 | tf_op jit(solution)/shard_map/all_to_all | solution.py:452

commit v10 on v9

--- a/solution.py
+++ b/solution.py
@@ -14,7 +14,6 @@
 RING = 4
 SCORE_LANE = 96
 WEIGHT_PARTS = 2
-PLACE_BITS = 4
 VMEM_LIMIT = 24 * 1024 * 1024
 
 F32 = jnp.float32
@@ -67,11 +66,6 @@
     within = sorted_row - per_tile * tile
     source = lax.shift_right_logical(within * 43, 8)
     return one_zero(sent_row == within + (GROUP - CAP) * source + CAP * tile)
-
-
-def member_at(base, place_ref, step):
-    sign = 1 - 2 * lax.shift_right_logical(place_ref[0], PLACE_BITS)
-    return (base + sign * step) & (RING - 1)
 
 
 def fetch(sources, targets, sems):
@@ -182,7 +176,7 @@
             (RING - 1, ((to_left_ref, 0), (previous_ref, 0))),
             (0, ((own_ref, 0), (own_ref, half))),
         ):
-            member = member_at(place_ref[0], place_ref, step)
+            member = (place_ref[0] + step) & (RING - 1)
             begin = pl.multiple_of(member * held, held)
             value = dot(rows_ref[pl.ds(begin, held)], ref[...]).astype(BF16)
             for part, (out_ref, start) in enumerate(pieces):
@@ -238,7 +232,7 @@
         (far_left_ref, RING // 2, 0),
         (far_right_ref, RING // 2, half),
     ):
-        member = member_at(place_ref[0], place_ref, step)
+        member = (place_ref[0] + step) & (RING - 1)
         begin = pl.multiple_of(member * held + start, half)
         full_ref[pl.ds(begin, ref.shape[0])] = ref[...]
 
@@ -378,13 +372,8 @@
 
 
 def shifted(block, distance):
-    parts, columns = lax.axis_size("expert"), lax.axis_size("dp")
-    route = [
-        (part * columns + column, (part + (1 - 2 * (column % 2)) * distance) % parts * columns + column)
-        for part in range(parts)
-        for column in range(columns)
-    ]
-    return lax.ppermute(block, ("expert", "dp"), route)
+    parts = lax.axis_size("expert")
+    return lax.ppermute(block, "expert", [(i, (i + distance) % parts) for i in range(parts)])
 
 
 def per_device(
@@ -401,8 +390,7 @@
     rows = shape((row_count, width), BF16)
     whole, halved = (shape((size, 3 * hidden), BF16) for size in (held, held // 2))
     groups = [list(range(i, parts, RING)) for i in range(RING)]
-    member = lax.axis_index("expert") + ((lax.axis_index("dp") & 1) << PLACE_BITS)
-    member = member.astype(jnp.int32).reshape(1)
+    member = lax.axis_index("expert").astype(jnp.int32).reshape(1)
     weights = (gate_weight[0], up_weight[0], down_weight[0].T)
     arguments = (routes.T, route_weights.T, owner_slots.reshape(1, experts), tokens.T, cotangent.T)
     send, plan = kernel_call(

time: 205 us -> 200 us (0.976)
  starting transfers between devices: 61 us -> 76.5 us
  blocking collectives: 60.3 us -> 50.2 us
  waiting for transfers between devices: 66.6 us -> 56.9 us
    all_to_all x1, blocking collectives: 34.8 us -> 21.3 us  [per_device(): lax.all_to_all(window, 'expert', split_axis=0, concat_axis=0, tiled=True,...]
    ppermute x8, starting transfers between devices: 34.1 us -> 45.4 us  [shifted(): lax.ppermute(block, 'expert', [(i, (i + distance) % parts) for i in range...]
    ppermute x8, waiting for transfers between devices: 39.4 us -> 29.6 us  [shifted(): lax.ppermute(block, 'expert', [(i, (i + distance) % parts) for i in range...]
    all_to_all x1, starting transfers between devices: 8.59 us -> 12.7 us  [per_device(): lax.all_to_all(back, 'dp', split_axis=0, concat_axis=0, tiled=True)]
    all_gather x1, blocking collectives: 25.5 us -> 29 us  [per_device(): lax.all_gather(share, 'expert', axis=0, tiled=True, axis_index_groups=gro...]
where the time goes in v10:
time: 200 us
  starting transfers between devices  76.5 us (38%)
  waiting for transfers between devices  56.9 us (28%)
  blocking collectives  50.2 us (25%)
  Pallas kernels  12.9 us (6%)
  local copies, waits for them, and re-layouts  2.41 us (1%)
    ppermute x8, starting transfers between devices, shifted(): lax.ppermute(block, 'expert', [(i, (i + distance) % parts) for i in range...  45.4 us
    ppermute x8, waiting for transfers between devices, shifted(): lax.ppermute(block, 'expert', [(i, (i + distance) % parts) for i in range...  29.6 us
    all_gather x1, blocking collectives, per_device(): lax.all_gather(share, 'expert', axis=0, tiled=True, axis_index_groups=gro...  29 us
    all_to_all x1, blocking collectives, per_device(): lax.all_to_all(window, 'expert', split_axis=0, concat_axis=0, tiled=True,...  21.3 us
    all_to_all x1, starting transfers between devices, per_device(): lax.all_to_all(send, 'dp', split_axis=0, concat_axis=0, tiled=True)  18.4 us
    all_to_all x1, waiting for transfers between devices, per_device(): lax.all_to_all(send, 'dp', split_axis=0, concat_axis=0, tiled=True)  14.7 us
    all_to_all x1, starting transfers between devices, per_device(): lax.all_to_all(back, 'dp', split_axis=0, concat_axis=0, tiled=True)  12.7 us
    all_to_all x1, waiting for transfers between devices, per_device(): lax.all_to_all(back, 'dp', split_axis=0, concat_axis=0, tiled=True)  12.5 us
  transfers between devices with their start and end apart: 10, of which 9 were waited for; matrix products, arithmetic and copies ran while one was open for 0% of the time, Pallas kernels for 1%

profile of v10, /device:TPU:1, one launch (start us, length us, event | category | flops | bytes accessed | tf_op | source)
XLA Modules:
  0.0 199.7 jit_solution(14480349745926671801)
XLA Ops:
  0.7 0.7 copy-done.11
  1.3 0.8 copy-done.8
  2.2 0.8 copy-done.9
  3.0 2.4 %shard_map.127 = (bf16[64,24,128]{2,1,0:T(8,128)(2,1)}, f32[128,128]{1,0:T(8,128)S(1)}) custom-call(s32[8,128]{1,0:T(8,128)S(1)} %bitcast.31, f32[8,128]{1,0:T(8,128)S(1)} %bitcast.33, s32[1,64]{1,0:T(1,128)S(1)} %bitcast.35, bf16[224,128]{1,0:T(8,128)(2,1)S(1)} %bitcast.29, bf16[224,128]{1,0:T(8,128)(2,1)S(1)} %bitcast.30), custom_call_target="tpu_custom_call" | custom-call | flops 300000000 | bytes 1000000 | tf_op jit(solution)/shard_map/pallas_call | solution.py:396
  5.4 18.4 %all-to-all-start = ((bf16[64,24,128]{2,1,0:T(8,128)(2,1)}), bf16[64,24,128]{2,1,0:T(8,128)(2,1)S(1)}, u32[]{:S(2)}, u32[]{:S(2)}) async-start(bf16[64,24,128]{2,1,0:T(8,128)(2,1)} %get-tuple-element.23), calls=%async_computation | async-start | bytes 786432 | tf_op jit(solution)/shard_map/all_to_all | solution.py:404
  23.8 14.7 %all-to-all-done.recv_ref = bf16[64,24,128]{2,1,0:T(8,128)(2,1)S(1)} async-done(((bf16[64,24,128]{2,1,0:T(8,128)(2,1)}), bf16[64,24,128]{2,1,0:T(8,128)(2,1)S(1)}, u32[]{:S(2)}, u32[]{:S(2)}) %all-to-all-start) | async-done | bytes 393248 | tf_op jit(solution)/shard_map/all_to_all | solution.py:404
  38.5 2.4 %shard_map.128 = (bf16[96,3072]{1,0:T(8,128)(2,1)S(1)}, bf16[96,3072]{1,0:T(8,128)(2,1)S(1)}, bf16[96,3072]{1,0:T(8,128)(2,1)S(1)}, bf16[48,3072]{1,0:T(8,128)(2...) custom-call(s32[1]{0:T(128)} %bitcast.place_ref, ...), custom_call_target="tpu_custom_call" | custom-call | flops 700000000 | bytes 4500000 | tf_op jit(solution)/shard_map/pallas_call | solution.py:405
  40.9 1.9 collective-permute-start
  42.9 11.2 %collective-permute-start.1 = (bf16[96,3072]{1,0:T(8,128)(2,1)S(1)}, bf16[96,3072]{1,0:T(8,128)(2,1)S(1)}, u32[]{:S(2)}, u32[]{:S(2)}) collective-permute-start(bf16[96,3072]{1,0:T(8,128)(2,1)S(1)} %get-tuple-element.26), channel_id=1, source_target_pairs={{0,960},{64,0},{128,64},{192,128},{256,192},{320,256},{384,320},{4... | collective-permute-start | bytes 1769480 | tf_op jit(solution)/shard_map/ppermute | solution.py:376
  54.1 11.4 %collective-permute-done.from_left_ref = bf16[96,3072]{1,0:T(8,128)(2,1)S(1)} collective-permute-done((bf16[96,3072]{1,0:T(8,128)(2,1)S(1)}, bf16[96,3072]{1,0:T(8,128)(2,1)S(1)}, u32[]{:S(2)}, u32[]{:S(2)}) %collective-permute-start) | collective-permute-done | bytes 589856 | tf_op jit(solution)/shard_map/ppermute | solution.py:376
  65.5 0.9 collective-permute-done.1.from_right_ref
  66.4 0.1 shard_map.129
  66.6 1.9 collective-permute-start.2
  68.5 5.3 %collective-permute-start.3 = (bf16[48,3072]{1,0:T(8,128)(2,1)S(1)}, bf16[48,3072]{1,0:T(8,128)(2,1)S(1)}, u32[]{:S(2)}, u32[]{:S(2)}) collective-permute-start(bf16[48,3072]{1,0:T(8,128)(2,1)S(1)} %get-tuple-element.30), channel_id=1, source_target_pairs={{0,960},{64,0},{128,64},{192,128},{256,192},{320,256},{384,320},{4... | collective-permute-start | bytes 884744 | tf_op jit(solution)/shard_map/ppermute | solution.py:376
  73.8 4.2 %collective-permute-done.2.far_left_ref = bf16[48,3072]{1,0:T(8,128)(2,1)S(1)} collective-permute-done((bf16[48,3072]{1,0:T(8,128)(2,1)S(1)}, bf16[48,3072]{1,0:T(8,128)(2,1)S(1)}, u32[]{:S(2)}, u32[]{:S(2)}) %collective-permute-start.2) | collective-permute-done | bytes 294944 | tf_op jit(solution)/shard_map/ppermute | solution.py:376
  78.0 0.9 collective-permute-done.3.far_right_ref
  78.9 0.2 shard_map.130
  79.1 21.3 %all_to_all.21 = bf16[4,24,3072]{2,1,0:T(8,128)(2,1)S(1)} all-to-all(bf16[4,24,3072]{2,1,0:T(8,128)(2,1)S(1)} %bitcast.22), channel_id=1, replica_groups={{0,256,512,768},{64,320,576,832},{128,384,640,896},{192,448,704,960},{1..., dimensions={0} | all-to-all | bytes 1179648 | tf_op jit(solution)/shard_map/all_to_all | solution.py:421
  100.3 0.2 shard_map.131
  100.5 29.0 %all_gather.3.own_ref = bf16[96,3200]{1,0:T(8,128)(2,1)S(1)} all-gather(bf16[24,3200]{1,0:T(8,128)(2,1)S(1)} %shard_map.131), channel_id=1, replica_groups={{0,256,512,768},{64,320,576,832},{128,384,640,896},{192,448,704,960},{1..., dimensions={0}, use_global_device_ids=true | all-gather | bytes 768000 | tf_op jit(solution)/shard_map/all_gather | solution.py:427
  129.5 16.2 %collective-permute-start.4 = (bf16[96,3200]{1,0:T(8,128)(2,1)S(1)}, bf16[96,3200]{1,0:T(8,128)(2,1)S(1)}, u32[]{:S(2)}, u32[]{:S(2)}) collective-permute-start(bf16[96,3200]{1,0:T(8,128)(2,1)S(1)} %all_gather.3.own_ref), channel_id=1, source_target_pairs={{0,64},{64,128},{128,192},{192,256},{256,320},{320,384},{384,448},... | collective-permute-start | bytes 1843208 | tf_op jit(solution)/shard_map/ppermute | solution.py:376
  145.7 2.2 %collective-permute-start.5 = (bf16[96,3200]{1,0:T(8,128)(2,1)S(1)}, bf16[96,3200]{1,0:T(8,128)(2,1)S(1)}, u32[]{:S(2)}, u32[]{:S(2)}) collective-permute-start(bf16[96,3200]{1,0:T(8,128)(2,1)S(1)} %all_gather.3.own_ref), channel_id=1, source_target_pairs={{0,960},{64,0},{128,64},{192,128},{256,192},{320,256},{384,320},{4... | collective-permute-start | bytes 1843208 | tf_op jit(solution)/shard_map/ppermute | solution.py:376
  147.9 7.4 %collective-permute-done.4.left_ref = bf16[96,3200]{1,0:T(8,128)(2,1)S(1)} collective-permute-done((bf16[96,3200]{1,0:T(8,128)(2,1)S(1)}, bf16[96,3200]{1,0:T(8,128)(2,1)S(1)}, u32[]{:S(2)}, u32[]{:S(2)}) %collective-permute-start.4) | collective-permute-done | bytes 614432 | tf_op jit(solution)/shard_map/ppermute | solution.py:376
  155.3 3.9 %collective-permute-start.6 = (bf16[48,3200]{1,0:T(8,128)(2,1)S(1)}, bf16[48,3200]{1,0:T(8,128)(2,1)S(1)}, u32[]{:S(2)}, u32[]{:S(2)}) collective-permute-start(bf16[48,3200]{1,0:T(8,128)(2,1)S(1)} %slice.8), channel_id=1, source_target_pairs={{0,64},{64,128},{128,192},{192,256},{256,320},{320,384},{384,448},... | collective-permute-start | bytes 921608 | tf_op jit(solution)/shard_map/ppermute | solution.py:376
  159.3 2.7 %collective-permute-start.7 = (bf16[48,3200]{1,0:T(8,128)(2,1)S(1)}, bf16[48,3200]{1,0:T(8,128)(2,1)S(1)}, u32[]{:S(2)}, u32[]{:S(2)}) collective-permute-start(bf16[48,3200]{1,0:T(8,128)(2,1)S(1)} %slice.9), channel_id=1, source_target_pairs={{0,960},{64,0},{128,64},{192,128},{256,192},{320,256},{384,320},{4... | collective-permute-start | bytes 921608 | tf_op jit(solution)/shard_map/ppermute | solution.py:376
  162.0 2.3 %collective-permute-done.6.far_left_ref = bf16[48,3200]{1,0:T(8,128)(2,1)S(1)} collective-permute-done((bf16[48,3200]{1,0:T(8,128)(2,1)S(1)}, bf16[48,3200]{1,0:T(8,128)(2,1)S(1)}, u32[]{:S(2)}, u32[]{:S(2)}) %collective-permute-start.6) | collective-permute-done | bytes 307232 | tf_op jit(solution)/shard_map/ppermute | solution.py:376
  164.3 2.6 %collective-permute-done.7.far_right_ref = bf16[48,3200]{1,0:T(8,128)(2,1)S(1)} collective-permute-done((bf16[48,3200]{1,0:T(8,128)(2,1)S(1)}, bf16[48,3200]{1,0:T(8,128)(2,1)S(1)}, u32[]{:S(2)}, u32[]{:S(2)}) %collective-permute-start.7) | collective-permute-done | bytes 307232 | tf_op jit(solution)/shard_map/ppermute | solution.py:376
  166.9 3.3 %shard_map.132 = bf16[64,24,128]{2,1,0:T(8,128)(2,1)} custom-call(s32[1]{0:T(128)} %bitcast.place_ref, bf16[96,3200]{1,0:T(8,128)(2,1)S(1)} %all_gather.3.own_ref, bf16[96,3200]{1,0:T(8,128)(2,1)S(1)} %collective-permute-done.4.left_ref, bf16[96,3200]{1,0:T(8,128)(2,1)S(1)} %collective-permute-done.5.right_ref, ...), custom_call_target="tpu_custom_call" | custom-call | flops 700000000 | bytes 4500000 | tf_op jit(solution)/shard_map/pallas_call | solution.py:432
  170.3 12.7 %all-to-all-start.2 = ((bf16[64,24,128]{2,1,0:T(8,128)(2,1)}), bf16[64,24,128]{2,1,0:T(8,128)(2,1)S(1)}, u32[]{:S(2)}, u32[]{:S(2)}) async-start(bf16[64,24,128]{2,1,0:T(8,128)(2,1)} %shard_map.132), calls=%async_computation.2 | async-start | bytes 786432 | tf_op jit(solution)/shard_map/all_to_all | solution.py:440
  183.0 2.1 %shard_map.134 = (bf16[224,1024]{1,0:T(8,128)(2,1)}, bf16[224,1024]{1,0:T(8,128)(2,1)}, bf16[224,1024]{1,0:T(8,128)(2,1)}) custom-call(s32[1]{0:T(128)} %bitcast.place_ref, bf16[96,3200]{1,0:T(8,128)(2,1)S(1)} %all_gather.3.own_ref, bf16[96,3200]{1,0:T(8,128)(2,1)S(1)} %collective-permute-done.4.left_ref, ...), custom_call_target="tpu_custom_call" | custom-call | flops 700000000 | bytes 4500000 | tf_op jit(solution)/shard_map/pallas_call | solution.py:442
  185.0 12.5 %all-to-all-done.2.back_ref = bf16[64,24,128]{2,1,0:T(8,128)(2,1)S(1)} async-done(((bf16[64,24,128]{2,1,0:T(8,128)(2,1)}), bf16[64,24,128]{2,1,0:T(8,128)(2,1)S(1)}, u32[]{:S(2)}, u32[]{:S(2)}) %all-to-all-start.2) | async-done | bytes 393248 | tf_op jit(solution)/shard_map/all_to_all | solution.py:440
  197.6 2.1 %shard_map.133 = (bf16[224,128]{1,0:T(8,128)(2,1)}, bf16[224,128]{1,0:T(8,128)(2,1)}, f32[8,128]{1,0:T(8,128)}) custom-call(bf16[64,24,128]{2,1,0:T(8,128)(2,1)S(1)} %all-to-all-done.2.back_ref, f32[128,128]{1,0:T(8,128)S(1)} %get-tuple-element.31.plan_ref, s32[8,128]{1,0:T(8,128)S(1)} %bitcast.32, f32[8,128]{1,0:T(8,128)S(1)} %bitcast.34), custom_call_target="tpu_custom_call" | custom-call | flops 500000000 | bytes 1000000 | tf_op jit(solution)/shard_map/pallas_call | solution.py:452
  (26 shorter events, 0.1 us)
Async XLA Ops:
  0.6 0.7 copy-start.11
  0.6 0.7 copy-start.10
  0.7 0.7 copy-start.12
  1.3 0.8 copy-start.8
  2.2 0.8 copy-start.9
  3.0 35.5 %copy-start.1 = (bf16[1,224,1024]{2,1,0:T(8,128)(2,1)S(1)}, bf16[1,224,1024]{2,1,0:T(8,128)(2,1)}, u32[]{:S(2)}) copy-start(bf16[1,224,1024]{2,1,0:T(8,128)(2,1)} %param.14) | copy-start | bytes 1376260
  3.0 35.5 %copy-start.2 = (bf16[1,1024,224]{1,2,0:T(8,128)(2,1)S(1)}, bf16[1,1024,224]{1,2,0:T(8,128)(2,1)}, u32[]{:S(2)}) copy-start(bf16[1,1024,224]{1,2,0:T(8,128)(2,1)} %param.15) | copy-start | bytes 1376260
  5.4 33.1 %copy-start = (bf16[1,224,1024]{2,1,0:T(8,128)(2,1)S(1)}, bf16[1,224,1024]{2,1,0:T(8,128)(2,1)}, u32[]{:S(2)}) copy-start(bf16[1,224,1024]{2,1,0:T(8,128)(2,1)} %param.13) | copy-start | bytes 1376260
  5.4 33.1 %all-to-all-start = ((bf16[64,24,128]{2,1,0:T(8,128)(2,1)}), bf16[64,24,128]{2,1,0:T(8,128)(2,1)S(1)}, u32[]{:S(2)}, u32[]{:S(2)}) async-start(bf16[64,24,128]{2,1,0:T(8,128)(2,1)} %get-tuple-element.23), calls=%async_computation | async-start | bytes 786432 | tf_op jit(solution)/shard_map/all_to_all | solution.py:404
  40.9 25.6 %copy-start.4 = (bf16[384,224]{1,0:T(8,128)(2,1)}, bf16[384,224]{1,0:T(8,128)(2,1)S(1)}, u32[]{:S(2)}) copy-start(bf16[384,224]{1,0:T(8,128)(2,1)S(1)} %get-tuple-element.35.tok_ref) | copy-start | bytes 516100
  40.9 25.6 %copy-start.6 = (bf16[384,224]{1,0:T(8,128)(2,1)}, bf16[384,224]{1,0:T(8,128)(2,1)S(1)}, u32[]{:S(2)}) copy-start(bf16[384,224]{1,0:T(8,128)(2,1)S(1)} %get-tuple-element.36.scaled_ref) | copy-start | bytes 516100
  40.9 24.6 %collective-permute-start = (bf16[96,3072]{1,0:T(8,128)(2,1)S(1)}, bf16[96,3072]{1,0:T(8,128)(2,1)S(1)}, u32[]{:S(2)}, u32[]{:S(2)}) collective-permute-start(bf16[96,3072]{1,0:T(8,128)(2,1)S(1)} %get-tuple-element.25), channel_id=1, source_target_pairs={{0,64},{64,128},{128,192},{192,256},{256,320},{320,384},{384,448},... | collective-permute-start | bytes 1769480 | tf_op jit(solution)/shard_map/ppermute | solution.py:376
  42.9 23.5 %collective-permute-start.1 = (bf16[96,3072]{1,0:T(8,128)(2,1)S(1)}, bf16[96,3072]{1,0:T(8,128)(2,1)S(1)}, u32[]{:S(2)}, u32[]{:S(2)}) collective-permute-start(bf16[96,3072]{1,0:T(8,128)(2,1)S(1)} %get-tuple-element.26), channel_id=1, source_target_pairs={{0,960},{64,0},{128,64},{192,128},{256,192},{320,256},{384,320},{4... | collective-permute-start | bytes 1769480 | tf_op jit(solution)/shard_map/ppermute | solution.py:376
  66.6 11.4 %collective-permute-start.2 = (bf16[48,3072]{1,0:T(8,128)(2,1)S(1)}, bf16[48,3072]{1,0:T(8,128)(2,1)S(1)}, u32[]{:S(2)}, u32[]{:S(2)}) collective-permute-start(bf16[48,3072]{1,0:T(8,128)(2,1)S(1)} %get-tuple-element.29), channel_id=1, source_target_pairs={{0,64},{64,128},{128,192},{192,256},{256,320},{320,384},{384,448},... | collective-permute-start | bytes 884744 | tf_op jit(solution)/shard_map/ppermute | solution.py:376
  68.5 10.4 %collective-permute-start.3 = (bf16[48,3072]{1,0:T(8,128)(2,1)S(1)}, bf16[48,3072]{1,0:T(8,128)(2,1)S(1)}, u32[]{:S(2)}, u32[]{:S(2)}) collective-permute-start(bf16[48,3072]{1,0:T(8,128)(2,1)S(1)} %get-tuple-element.30), channel_id=1, source_target_pairs={{0,960},{64,0},{128,64},{192,128},{256,192},{320,256},{384,320},{4... | collective-permute-start | bytes 884744 | tf_op jit(solution)/shard_map/ppermute | solution.py:376
  129.5 25.8 %collective-permute-start.4 = (bf16[96,3200]{1,0:T(8,128)(2,1)S(1)}, bf16[96,3200]{1,0:T(8,128)(2,1)S(1)}, u32[]{:S(2)}, u32[]{:S(2)}) collective-permute-start(bf16[96,3200]{1,0:T(8,128)(2,1)S(1)} %all_gather.3.own_ref), channel_id=1, source_target_pairs={{0,64},{64,128},{128,192},{192,256},{256,320},{320,384},{384,448},... | collective-permute-start | bytes 1843208 | tf_op jit(solution)/shard_map/ppermute | solution.py:376
  145.7 13.6 %collective-permute-start.5 = (bf16[96,3200]{1,0:T(8,128)(2,1)S(1)}, bf16[96,3200]{1,0:T(8,128)(2,1)S(1)}, u32[]{:S(2)}, u32[]{:S(2)}) collective-permute-start(bf16[96,3200]{1,0:T(8,128)(2,1)S(1)} %all_gather.3.own_ref), channel_id=1, source_target_pairs={{0,960},{64,0},{128,64},{192,128},{256,192},{320,256},{384,320},{4... | collective-permute-start | bytes 1843208 | tf_op jit(solution)/shard_map/ppermute | solution.py:376
  155.3 11.6 %copy-start.3 = (bf16[1,1024,224]{1,2,0:T(8,128)(2,1)S(1)}, bf16[1,1024,224]{1,2,0:T(8,128)(2,1)}, u32[]{:S(2)}) copy-start(bf16[1,1024,224]{1,2,0:T(8,128)(2,1)} %param.15) | copy-start | bytes 1376260
  155.3 8.9 %collective-permute-start.6 = (bf16[48,3200]{1,0:T(8,128)(2,1)S(1)}, bf16[48,3200]{1,0:T(8,128)(2,1)S(1)}, u32[]{:S(2)}, u32[]{:S(2)}) collective-permute-start(bf16[48,3200]{1,0:T(8,128)(2,1)S(1)} %slice.8), channel_id=1, source_target_pairs={{0,64},{64,128},{128,192},{192,256},{256,320},{320,384},{384,448},... | collective-permute-start | bytes 921608 | tf_op jit(solution)/shard_map/ppermute | solution.py:376
  159.3 7.6 %collective-permute-start.7 = (bf16[48,3200]{1,0:T(8,128)(2,1)S(1)}, bf16[48,3200]{1,0:T(8,128)(2,1)S(1)}, u32[]{:S(2)}, u32[]{:S(2)}) collective-permute-start(bf16[48,3200]{1,0:T(8,128)(2,1)S(1)} %slice.9), channel_id=1, source_target_pairs={{0,960},{64,0},{128,64},{192,128},{256,192},{320,256},{384,320},{4... | collective-permute-start | bytes 921608 | tf_op jit(solution)/shard_map/ppermute | solution.py:376
  170.3 12.7 %copy-start.5 = (bf16[384,224]{1,0:T(8,128)(2,1)S(1)}, bf16[384,224]{1,0:T(8,128)(2,1)}, u32[]{:S(2)}) copy-start(bf16[384,224]{1,0:T(8,128)(2,1)} %copy-done.4) | copy-start | bytes 516100
  170.3 12.7 %copy-start.7 = (bf16[384,224]{1,0:T(8,128)(2,1)S(1)}, bf16[384,224]{1,0:T(8,128)(2,1)}, u32[]{:S(2)}) copy-start(bf16[384,224]{1,0:T(8,128)(2,1)} %copy-done.6) | copy-start | bytes 516100
  170.3 27.3 %all-to-all-start.2 = ((bf16[64,24,128]{2,1,0:T(8,128)(2,1)}), bf16[64,24,128]{2,1,0:T(8,128)(2,1)S(1)}, u32[]{:S(2)}, u32[]{:S(2)}) async-start(bf16[64,24,128]{2,1,0:T(8,128)(2,1)} %shard_map.132), calls=%async_computation.2 | async-start | bytes 786432 | tf_op jit(solution)/shard_map/all_to_all | solution.py:440
